TPU v7x, 128 devices: a whole 4x4x4 slice. The times are simulated.
128 devices in a mesh: row: 16 (over x, z), col: 8 (over y, core).
Axes of the slice: x: 4, y: 4, z: 4, core: 2. Of those that a mesh axis runs over, the one named last changes fastest.
Arguments:
- kernel: bfloat16 [8, 16, 192, 24576], P(None, 'row', None, 'col'), may hold values from -1 to 4
- right_side: float32 [8, 3072, 512], P('col', 'row'), may hold values from -6 to 6
- initial: float32 [8, 3072, 512], P('col', 'row'), may hold values from -3 to 3
- local_inverse: float32 [128, 384, 384], P(('row', 'col')), may hold values from -1 to 2
- block_lists: int32 [128, 3], P(('row', 'col')), may hold values from 0 to 191, as said below
- counts: int32 [192], replicated, may hold values from 1 to 16, as said below
Outputs:
- solution: float32 [8, 3072, 512], P('col', 'row')
- residual: float32 [8, 3072, 512], P('col', 'row')
Inputs may be any that keep to these rules, and one draw needn't show every extreme that they name: `block_lists`: the blocks of one subdomain are different. With d = s // 1 and p = d mod (8), every block of subdomain s lies among blocks p * 24 to (p + 1) * 24 - 1. Every block is named by some subdomain. counts[q] is the number of pairs (s, k) with block_lists[s, k] = q.
All inputs are finite; a program needn't handle non-finite values.
Results may differ from a plain program's by a relative error of at most 0.023.
Values may be sent and summed in bfloat16 or wider, within the bound.
No kernel may reach another device: no remote copies, remote signals or barrier semaphores. Data moves between devices by JAX's collectives and lax.ppermute only.
A program may use at most 128 MiB of HBM per device.

v0:
```python
import jax
import jax.numpy as jnp
from jax import lax
from jax.sharding import PartitionSpec as P

BLOCK = 128


def body(kernel, right_side, initial, local_inverse, block_lists, counts):
    kernel_tile = kernel.reshape(-1, kernel.shape[3])
    target = right_side[0]
    solution = initial[0]
    own_rows = solution.shape[0]
    panel_rows = kernel.shape[3]
    panel_blocks = panel_rows // BLOCK
    rhs_width = right_side.shape[2]
    column_index = lax.axis_index("col")
    row_index = lax.axis_index("row")
    row_counts = jnp.repeat(counts.astype(jnp.float32), BLOCK)
    panel_counts = lax.dynamic_slice_in_dim(row_counts, column_index * panel_rows, panel_rows)
    own_counts = lax.dynamic_slice_in_dim(panel_counts, row_index * own_rows, own_rows)
    local_lists = block_lists - column_index * panel_blocks
    local_ids = local_lists.reshape(-1)
    entry_count = local_ids.shape[0]
    selector = (jnp.arange(panel_blocks)[:, None] == local_ids[None, :]).astype(jnp.float32)
    subdomain_count = local_inverse.shape[0]

    def add_columns(shard_rows):
        return jnp.dot(kernel_tile, shard_rows, preferred_element_type=jnp.float32)

    def apply_kernel(current):
        return add_columns(lax.all_gather(current.astype(jnp.bfloat16), "row", axis=0, tiled=True))

    def residual_of(products):
        return target - lax.psum_scatter(products, "col", scatter_dimension=0, tiled=True)

    def solve_local(picked):
        stacked = picked.astype(jnp.float32).reshape(subdomain_count, -1, rhs_width)
        return jnp.einsum("sab,sbc->sac", local_inverse, stacked, precision=lax.Precision.HIGHEST)

    def corrections(current_residual):
        gathered = lax.all_gather(current_residual.astype(jnp.bfloat16), "row", axis=0, tiled=True)
        blocks = gathered.reshape(panel_blocks, BLOCK, rhs_width)
        fix_blocks = solve_local(jnp.take(blocks, local_ids, axis=0))
        summed = jnp.dot(
            selector, fix_blocks.reshape(entry_count, -1), precision=lax.Precision.HIGHEST
        )
        return summed.reshape(panel_rows, rhs_width)

    def owner_fixes(current_residual):
        return lax.psum_scatter(
            corrections(current_residual), "row", scatter_dimension=0, tiled=True
        )

    def owner_update(current, current_residual):
        return current + owner_fixes(current_residual) / own_counts[:, None]

    solution = owner_update(solution, residual_of(apply_kernel(solution)))
    residual = residual_of(apply_kernel(solution))
    solution = owner_update(solution, residual)
    return (solution[None], residual[None])


def solution(mesh):
    return jax.shard_map(
        body,
        mesh=mesh,
        in_specs=(
            P(None, "row", None, "col"),
            P("col", "row", None),
            P("col", "row", None),
            P(("row", "col"), None, None),
            P(("row", "col"), None),
            P(),
        ),
        out_specs=(P("col", "row", None), P("col", "row", None)),
        check_vma=False,
    )
```

profile of v0, /device:TPU:0, one launch (start us, length us, event | category | flops | bytes accessed | tf_op | source)
XLA Modules:
  0.0 503.1 jit_solution(8227298712247934538)
XLA Ops:
  7.2 0.0 copy-start
  7.2 0.0 all-gather.5.cloned.1.call-start
  7.2 1.8 bitcast_convert_fusion
  9.0 0.0 all-gather.5.cloned.1.call-update
  9.0 0.0 reduce-scatter.5.cloned.1.call-start
  9.0 52.3 %all-gather.5.cloned.1.call-done = bf16[3072,512]{1,0:T(8,128)(2,1)} async-done(((bf16[192,512]{1,0:T(8,128)(2,1)}), bf16[3072,512]{1,0:T(8,128)(2,1)}) %all-gather.5.cloned.1.call-update) | async-done | bytes 3145744 | tf_op jit(solution)/shard_map/all_gather | solution.py:32
  61.3 10.7 %fusion.10 = f32[1536,512]{1,0:T(8,128)} fusion(bf16[1536,3072]{1,0:T(8,128)(2,1)} %bitcast.53, bf16[3072,512]{1,0:T(8,128)(2,1)} %all-gather.5.cloned.1.call-done), kind=kOutput, calls=%fused_computation.28 | convolution fusion | flops 4831838208 | bytes 15728640 | tf_op jit(solution)/shard_map/dot_general | solution.py:29
  72.0 0.0 copy-start.3
  72.0 0.0 copy-start.5
  72.0 0.0 reduce-scatter.5.cloned.1.call-update
  72.1 0.0 all-gather.7.cloned.1.call-start
  72.1 34.7 %reduce-scatter.5.cloned.1.call-done = f32[192,512]{1,0:T(8,128)} async-done(((f32[1536,512]{1,0:T(8,128)}), f32[192,512]{1,0:T(8,128)}) %reduce-scatter.5.cloned.1.call-update) | async-done | bytes 393232 | tf_op jit(solution)/shard_map/reduce_scatter | solution.py:35
  106.8 0.0 copy-done.3
  106.8 1.7 fusion.2
  108.5 0.0 all-gather.7.cloned.1.call-update
  108.5 0.0 reduce-scatter.7.cloned.1.call-start
  108.6 0.0 copy-done.5
  108.6 47.8 %all-gather.7.cloned.1.call-done = bf16[3072,512]{1,0:T(8,128)(2,1)} async-done(((bf16[192,512]{1,0:T(8,128)(2,1)}), bf16[3072,512]{1,0:T(8,128)(2,1)}) %all-gather.7.cloned.1.call-update) | async-done | bytes 3145744 | tf_op jit(solution)/shard_map/all_gather | solution.py:42
  156.5 2.5 gather_fusion
  158.9 0.1 broadcast_select_fusion.1
  159.0 0.0 copy-done
  159.0 1.1 convolution_bitcast_fusion.2
  160.1 0.3 copy.9
  160.4 0.6 reshape.57
  161.0 4.5 fusion.6
  165.4 6.9 %reshape.58 = f32[3072,512]{1,0:T(8,128)} reshape(f32[24,65536]{1,0:T(8,128)} %fusion.6) | data formatting | bytes 12582912 | tf_op jit(solution)/shard_map/reshape | solution.py:48
  172.3 0.0 copy-start.4
  172.3 0.0 copy-start.1
  172.3 0.0 reduce-scatter.7.cloned.1.call-update
  172.3 0.0 all-gather.9.cloned.1.call-start
  172.4 0.6 copy-done.4
  173.0 0.1 broadcast_bitcast_fusion
  173.1 0.1 dynamic_slice.7
  173.1 79.7 %reduce-scatter.7.cloned.1.call-done = f32[192,512]{1,0:T(8,128)} async-done(((f32[3072,512]{1,0:T(8,128)}), f32[192,512]{1,0:T(8,128)}) %reduce-scatter.7.cloned.1.call-update) | async-done | bytes 393232 | tf_op jit(solution)/shard_map/reduce_scatter | solution.py:51
  252.8 0.0 copy-done.1
  252.8 1.8 fusion.9
  254.6 0.0 all-gather.9.cloned.1.call-update
  254.6 0.0 reduce-scatter.9.cloned.1.call-start
  254.7 48.1 %all-gather.9.cloned.1.call-done = bf16[3072,512]{1,0:T(8,128)(2,1)} async-done(((bf16[192,512]{1,0:T(8,128)(2,1)}), bf16[3072,512]{1,0:T(8,128)(2,1)}) %all-gather.9.cloned.1.call-update) | async-done | bytes 3145744 | tf_op jit(solution)/shard_map/all_gather | solution.py:32
  302.8 10.7 %convolution_bitcast_fusion = f32[1536,512]{1,0:T(8,128)} fusion(bf16[1536,3072]{1,0:T(8,128)(2,1)} %bitcast.54, bf16[3072,512]{1,0:T(8,128)(2,1)} %all-gather.9.cloned.1.call-done), kind=kOutput, calls=%fused_computation.2 | convolution fusion | flops 4831838208 | bytes 15728640 | tf_op jit(solution)/shard_map/dot_general | solution.py:29
  313.4 0.0 reduce-scatter.9.cloned.1.call-update
  313.5 0.0 all-gather.11.cloned.1.call-start
  313.5 34.7 %reduce-scatter.9.cloned.1.call-done = f32[192,512]{1,0:T(8,128)} async-done(((f32[1536,512]{1,0:T(8,128)}), f32[192,512]{1,0:T(8,128)}) %reduce-scatter.9.cloned.1.call-update) | async-done | bytes 393232 | tf_op jit(solution)/shard_map/reduce_scatter | solution.py:35
  348.2 1.9 fusion.3
  350.0 0.0 all-gather.11.cloned.1.call-update
  350.1 0.2 reduce-scatter.11.cloned.1.call-start
  350.3 47.6 %all-gather.11.cloned.1.call-done = bf16[3072,512]{1,0:T(8,128)(2,1)} async-done(((bf16[192,512]{1,0:T(8,128)(2,1)}), bf16[3072,512]{1,0:T(8,128)(2,1)}) %all-gather.11.cloned.1.call-update) | async-done | bytes 3145744 | tf_op jit(solution)/shard_map/all_gather | solution.py:42
  397.9 2.5 gather_fusion.1
  400.3 0.1 broadcast_select_fusion
  400.4 1.1 convolution_bitcast_fusion.1
  401.5 0.3 copy.11
  401.8 0.6 reshape.62
  402.3 4.5 fusion.5
  406.8 6.9 %reshape.63 = f32[3072,512]{1,0:T(8,128)} reshape(f32[24,65536]{1,0:T(8,128)} %fusion.5) | data formatting | bytes 12582912 | tf_op jit(solution)/shard_map/reshape | solution.py:48
  413.7 0.0 copy-start.2
  413.7 0.0 reduce-scatter.11.cloned.1.call-update
  413.7 80.6 %reduce-scatter.11.cloned.1.call-done = f32[192,512]{1,0:T(8,128)} async-done(((f32[3072,512]{1,0:T(8,128)}), f32[192,512]{1,0:T(8,128)}) %reduce-scatter.11.cloned.1.call-update) | async-done | bytes 393232 | tf_op jit(solution)/shard_map/reduce_scatter | solution.py:51
  494.3 0.0 copy-done.2
  494.3 1.9 add_bitcast_fusion
  (4 shorter events, 0.0 us)
Async XLA Ops:
  7.2 151.9 %copy-start = (f32[1,384,384]{2,1,0:T(8,128)S(1)}, f32[1,384,384]{2,1,0:T(8,128)}, u32[]{:S(2)}) copy-start(f32[1,384,384]{2,1,0:T(8,128)} %param.11) | copy-start | bytes 1769476
  7.2 54.2 %all-gather.5.cloned.1.call-start = ((), (), s32[]{:S(2)}) async-start(), calls=%async_computation.4 | async-start | bytes 3342336 | tf_op jit(solution)/shard_map/all_gather | solution.py:32
  9.0 97.8 %reduce-scatter.5.cloned.1.call-start = ((), (), s32[]{:S(2)}) async-start(), calls=%async_computation.5 | async-start | bytes 3538944 | tf_op jit(solution)/shard_map/reduce_scatter | solution.py:35
  72.0 34.8 %copy-start.3 = (f32[1,192,512]{2,1,0:T(8,128)S(1)}, f32[1,192,512]{2,1,0:T(8,128)}, u32[]{:S(2)}) copy-start(f32[1,192,512]{2,1,0:T(8,128)} %param.9) | copy-start | bytes 1179652
  72.0 36.6 %copy-start.5 = (s32[1,3]{1,0:T(1,128)S(1)}, s32[1,3]{1,0:T(1,128)}, u32[]{:S(2)}) copy-start(s32[1,3]{1,0:T(1,128)} %param.12) | copy-start | bytes 40
  72.1 84.4 %all-gather.7.cloned.1.call-start = ((), (), s32[]{:S(2)}) async-start(), calls=%async_computation.6 | async-start | bytes 3342336 | tf_op jit(solution)/shard_map/all_gather | solution.py:42
  108.5 144.3 %reduce-scatter.7.cloned.1.call-start = ((), (), s32[]{:S(2)}) async-start(), calls=%async_computation.7 | async-start | bytes 6684672 | tf_op jit(solution)/shard_map/reduce_scatter | solution.py:51
  172.3 0.7 copy-start.4
  172.3 80.5 %copy-start.1 = (f32[1,192,512]{2,1,0:T(8,128)S(1)}, f32[1,192,512]{2,1,0:T(8,128)}, u32[]{:S(2)}) copy-start(f32[1,192,512]{2,1,0:T(8,128)} %param.10) | copy-start | bytes 1179652
  172.3 130.4 %all-gather.9.cloned.1.call-start = ((), (), s32[]{:S(2)}) async-start(), calls=%async_computation.8 | async-start | bytes 3342336 | tf_op jit(solution)/shard_map/all_gather | solution.py:32
  254.6 93.5 %reduce-scatter.9.cloned.1.call-start = ((), (), s32[]{:S(2)}) async-start(), calls=%async_computation.9 | async-start | bytes 3538944 | tf_op jit(solution)/shard_map/reduce_scatter | solution.py:35
  313.5 84.4 %all-gather.11.cloned.1.call-start = ((), (), s32[]{:S(2)}) async-start(), calls=%async_computation.10 | async-start | bytes 3342336 | tf_op jit(solution)/shard_map/all_gather | solution.py:42
  350.1 144.3 %reduce-scatter.11.cloned.1.call-start = ((), (), s32[]{:S(2)}) async-start(), calls=%async_computation.11 | async-start | bytes 6684672 | tf_op jit(solution)/shard_map/reduce_scatter | solution.py:51
  413.7 80.7 %copy-start.2 = (f32[192,512]{1,0:T(8,128)S(1)}, f32[192,512]{1,0:T(8,128)}, u32[]{:S(2)}) copy-start(f32[192,512]{1,0:T(8,128)} %reduce-scatter.7.cloned.1.call-done) | copy-start | bytes 1179652
Sparse Core Ops, SparseCore 0:
  10.8 50.5 all-gather.4
  72.2 34.5 reduce-scatter.4
  109.5 46.8 all-gather.6
  172.4 80.3 reduce-scatter.6
  255.4 47.2 all-gather.8
  313.6 34.5 reduce-scatter.8
  350.9 46.8 all-gather.10
  413.8 80.4 reduce-scatter.10
where the time goes:
time: 504 us; the launch traced here: 503 us
  waiting for transfers between devices  426 us (85%)
  matrix products  32.4 us (6%)
  local copies, waits for them, and re-layouts  21.1 us (4%)
  between operations  14.3 us (3%)
  other arithmetic  9.26 us (2%)
    reduce_scatter x2, waiting for transfers between devices, owner_fixes(): lax.psum_scatter(corrections(current_residual), 'row', scatter_dimension=...  160 us
    all_gather x2, waiting for transfers between devices, apply_kernel(): lax.all_gather(current.astype(jnp.bfloat16), 'row', axis=0, tiled=True)  100 us
    all_gather x2, waiting for transfers between devices, corrections(): lax.all_gather(current_residual.astype(jnp.bfloat16), 'row', axis=0, tile...  95.4 us
    reduce_scatter x2, waiting for transfers between devices, residual_of(): lax.psum_scatter(products, 'col', scatter_dimension=0, tiled=True)  69.3 us
    dot_general x2, matrix products, add_columns(): return jnp.dot(kernel_tile, shard_rows, preferred_element_type=jnp.float32)  21.4 us
    reshape x2, local copies, waits for them, and re-layouts, corrections(): return summed.reshape(panel_rows, rhs_width)  13.7 us
  transfers between devices with their start and end apart: 8, of which 8 were waited for; matrix products, arithmetic and copies ran while one was open for 0% of the time, Pallas kernels for 0%

commit v1 on v0

v1 whole, which is shorter than its diff:
```python
import jax
import jax.numpy as jnp
from jax import lax
from jax.experimental import pallas as pl
from jax.experimental.pallas import tpu as pltpu
from jax.sharding import Mesh, PartitionSpec as P

BLOCK = 128
F32 = jnp.float32
BF16 = jnp.bfloat16
ANY = pl.BlockSpec(memory_space=pl.ANY)
VMEM_LIMIT = 40 * 1024 * 1024
SLOT_STEPS = (0, -1, 1, 2)
PANEL_STEPS = (2, 1, 3, 0)


def ring(value, axis, step):
    return lax.ppermute(value, axis, [(i, (i + step) % 4) for i in range(4)])


def cross(value):
    return lax.ppermute(value, "core", [(0, 1), (1, 0)])


def gather_ring(own, first, second, split):
    left, right = ring(own, first, 1), ring(own, first, -1)
    half = own.shape[split] // 2
    low = ring(lax.slice_in_dim(left, 0, half, axis=split), first, 1)
    high = ring(lax.slice_in_dim(right, half, 2 * half, axis=split), first, -1)
    across = jnp.concatenate([low, high], axis=split)
    bundle = jnp.stack([own, left, right, across])
    left, right = ring(bundle, second, 1), ring(bundle, second, -1)
    low, high = ring(left[:2], second, 1), ring(right[2:], second, -1)
    return bundle, left, right, low, high


def bundle_places():
    places = []
    for slot in range(4):
        for array in range(3):
            places.append((array, slot, slot, array))
        places.append((3 + slot // 2, slot % 2, slot, 3))
    return places


def place_pieces(refs, filled, sems, pos_ref, index_of):
    copies = []
    for half in range(2):
        first, second = (pos_ref[1], pos_ref[0]) if half == 0 else (pos_ref[0], pos_ref[1])
        for array, index, slot_first, slot_second in bundle_places():
            at_first = lax.rem(first + (SLOT_STEPS[slot_first] + 4), 4)
            at_second = lax.rem(second + (SLOT_STEPS[slot_second] + 4), 4)
            x, z = (at_second, at_first) if half == 0 else (at_first, at_second)
            copy = pltpu.make_async_copy(
                refs[half * 5 + array].at[index], filled.at[index_of(x, z, half)], sems.at[len(copies)]
            )
            copy.start()
            copies.append(copy)
    for copy in copies:
        copy.wait()


def product_kernel(transposed, pos_ref, tile_ref, *rest):
    pieces, (other_ref, mine_ref, filled, sems) = rest[:10], rest[10:]
    step = pl.program_id(0)

    if transposed:
        def index_of(x, z, half):
            return pl.ds(pl.multiple_of((z * 4 + x) * 32 + half * 16, 16), 16), slice(None)
    else:
        def index_of(x, z, half):
            return pl.ds(pl.multiple_of((x * 4 + z) * 192, 64), 192), pl.ds(half * 256, 256)

    @pl.when(step == 0)
    def _():
        place_pieces(pieces, filled, sems, pos_ref, index_of)

    dims = (((1,), (1,)), ((), ())) if transposed else (((1,), (0,)), ((), ()))
    product = lax.dot_general(tile_ref[0], filled[...], dims, preferred_element_type=F32).astype(BF16)

    @pl.when(step < 4)
    def _():
        other_ref[0] = product

    @pl.when(step >= 4)
    def _():
        mine_ref[0] = product


def panel_of(step, pos_ref):
    turn = lax.rem(step, 4)
    ahead = jnp.where(turn == 0, 2, jnp.where(turn == 1, 1, jnp.where(turn == 2, 3, 0)))
    core = jnp.where(step < 4, 1 - pos_ref[3], pos_ref[3])
    return lax.rem(pos_ref[2] + ahead, 4) * 2 + core


def product(kernel, pieces, pos, transposed):
    panels, rows, depth = kernel.shape
    width = 512
    out = jax.ShapeDtypeStruct((panels // 2, rows, width), BF16)
    return pl.pallas_call(
        lambda *refs: product_kernel(transposed, *refs),
        grid_spec=pltpu.PrefetchScalarGridSpec(
            num_scalar_prefetch=1,
            grid=(panels,),
            in_specs=[pl.BlockSpec((1, rows, depth), lambda i, p: (panel_of(i, p), 0, 0))] + [ANY] * 10,
            out_specs=[
                pl.BlockSpec((1, rows, width), lambda i, p: (jnp.minimum(i, 3), 0, 0)),
                pl.BlockSpec((1, rows, width), lambda i, p: (jnp.maximum(i - 4, 0), 0, 0)),
            ],
            scratch_shapes=[
                pltpu.VMEM((width, depth) if transposed else (depth, width), BF16),
                pltpu.SemaphoreType.DMA((32,)),
            ],
        ),
        out_shape=(out, out),
        compiler_params=pltpu.CompilerParams(vmem_limit_bytes=VMEM_LIMIT),
        cost_estimate=pl.CostEstimate(
            flops=2 * panels * rows * depth * width, bytes_accessed=16 << 20, transcendentals=0
        ),
    )(pos, kernel, *pieces)


def sum_over_col(other, mine):
    joined = mine.astype(F32) + cross(other).astype(F32)
    sent = joined[:3].astype(BF16)
    far, ahead, behind = ring(sent[0], "y", 2), ring(sent[1], "y", 1), ring(sent[2], "y", -1)
    return joined[3] + (far.astype(F32) + (ahead.astype(F32) + behind.astype(F32)))


def split_kernel(pos_ref, residual_ref, *out_refs):
    for step in range(4):
        column = pl.multiple_of(lax.rem(pos_ref[1] + step, 4) * 128, 128)
        out_refs[step][...] = residual_ref[:, pl.ds(column, 128)].astype(BF16)


def turn_kernel(pos_ref, *refs):
    pieces, out_refs, (tall, wide) = refs[:4], refs[4:8], refs[8:]
    for step in range(4):
        row = pl.multiple_of(lax.rem(pos_ref[1] + (4 - step), 4) * 192, 64)
        tall[pl.ds(row, 192), :] = pieces[step][...].astype(F32)
    wide[...] = tall[...].T
    for step in range(4):
        row = pl.multiple_of(lax.rem(pos_ref[0] + step, 4) * 32, 32)
        out_refs[step][...] = wide[pl.ds(row, 32), :].astype(BF16)


SMEM = pl.BlockSpec(memory_space=pltpu.SMEM)
VMEM = pl.BlockSpec(memory_space=pltpu.VMEM)


def whole_call(body, out_shape, scratch_shapes=(), scalars=1):
    def call(*args):
        return pl.pallas_call(
            body,
            in_specs=[SMEM] * scalars + [VMEM] * (len(args) - scalars),
            out_specs=jax.tree.map(lambda _: VMEM, out_shape),
            out_shape=out_shape,
            scratch_shapes=list(scratch_shapes),
            compiler_params=pltpu.CompilerParams(vmem_limit_bytes=VMEM_LIMIT),
        )(*args)

    return call


def to_columns(residual, pos):
    piece = jax.ShapeDtypeStruct((192, 128), BF16)
    pieces = whole_call(split_kernel, (piece,) * 4)(pos, residual)
    pieces = [pieces[0]] + [ring(pieces[step], "z", step) for step in (1, 2, 3)]
    piece = jax.ShapeDtypeStruct((32, 768), BF16)
    pieces = whole_call(
        turn_kernel, (piece,) * 4, (pltpu.VMEM((768, 128), F32), pltpu.VMEM((128, 768), F32))
    )(pos, *pieces)
    return [pieces[0]] + [ring(pieces[step], "x", step) for step in (1, 2, 3)]


def solve_kernel(last, pos_ref, lists_ref, counts_ref, *refs):
    pieces, inverse_ref, refs = refs[:4], refs[4], refs[5:]
    if last:
        before_ref, out_refs, (held, total) = refs[0], refs[1:5], refs[5:]
    else:
        low_ref, high_ref, full_ref, held, total = refs
    for step in range(4):
        at = pl.multiple_of(lax.rem(pos_ref[0] + (4 - step), 4) * 768, 128)
        held[:, pl.ds(at, 768)] = pieces[step][...]
    total[...] = jnp.zeros_like(total)

    def one(s, carry):
        starts = [pl.multiple_of(lists_ref[s, k] * BLOCK, BLOCK) for k in range(3)]
        picked = jnp.concatenate([held[:, pl.ds(start, BLOCK)] for start in starts], axis=1)
        fix = lax.dot_general(
            inverse_ref[s, :384, :], picked, (((1,), (1,)), ((), ())), preferred_element_type=F32
        )
        for k in range(3):
            total[pl.ds(starts[k], BLOCK), :] += fix[k * BLOCK:(k + 1) * BLOCK]
        return carry

    lax.fori_loop(0, 16, one, 0)
    panel = pos_ref[2] * 2 + pos_ref[3]
    for block in range(24):
        count = counts_ref[panel * 24 + block].astype(F32)
        at = slice(block * BLOCK, (block + 1) * BLOCK)
        mean = total[at, :].T / count
        if last:
            full = (mean + before_ref[:, at]).astype(BF16)
            out_refs[block // 6][:, (block % 6) * BLOCK:(block % 6 + 1) * BLOCK] = full
        else:
            full_ref[:, at] = mean
            low_ref[:, at] = mean[:16].astype(BF16)
            high_ref[:, at] = mean[16:].astype(BF16)


def solve(pieces, inverses, lists, counts, pos, before=None):
    last = before is not None
    if last:
        out_shape = (jax.ShapeDtypeStruct((32, 768), BF16),) * 4
    else:
        half = jax.ShapeDtypeStruct((16, 3072), BF16)
        out_shape = (half, half, jax.ShapeDtypeStruct((32, 3072), F32))
    args = [pos, lists, counts, *pieces, inverses] + ([before] if last else [])
    return whole_call(
        lambda *refs: solve_kernel(last, *refs),
        out_shape,
        (pltpu.VMEM((32, 3072), BF16), pltpu.VMEM((3072, 32), F32)),
        scalars=3,
    )(*args)


def turn_back_kernel(pos_ref, *refs):
    pieces, out_refs, (wide, tall) = refs[:4], refs[4:8], refs[8:]
    for step in range(4):
        row = pl.multiple_of(lax.rem(pos_ref[0] + (4 - step), 4) * 32, 32)
        wide[pl.ds(row, 32), :] = pieces[step][...].astype(F32)
    tall[...] = wide[...].T
    for step in range(4):
        row = pl.multiple_of(lax.rem(pos_ref[1] + step, 4) * 192, 64)
        out_refs[step][...] = tall[pl.ds(row, 192), :].astype(BF16)


def join_kernel(pos_ref, start_ref, *refs):
    pieces, out_ref = refs[:4], refs[4]
    for step in range(4):
        column = pl.multiple_of(lax.rem(pos_ref[1] + (4 - step), 4) * 128, 128)
        at = pl.ds(column, 128)
        out_ref[:, at] = start_ref[:, at] + pieces[step][...].astype(F32)


def from_columns(parts, start, pos):
    stacked = jnp.stack(parts)
    row = pos[0]
    own = [lax.dynamic_index_in_dim(stacked, lax.rem(row + step, 4), 0, keepdims=False) for step in range(4)]
    pieces = [own[0]] + [ring(own[step], "x", step) for step in (1, 2, 3)]
    piece = jax.ShapeDtypeStruct((192, 128), BF16)
    pieces = whole_call(
        turn_back_kernel, (piece,) * 4, (pltpu.VMEM((128, 768), F32), pltpu.VMEM((768, 128), F32))
    )(pos, *pieces)
    pieces = [pieces[0]] + [ring(pieces[step], "z", step) for step in (1, 2, 3)]
    return whole_call(join_kernel, jax.ShapeDtypeStruct((192, 512), F32))(pos, start, *pieces)


def body(kernel, right_side, initial, local_inverse, block_lists, counts):
    kernel, target, start = kernel[:, 0], right_side[0], initial[0]
    pos = jnp.stack([lax.axis_index(name) for name in ("x", "z", "y", "core")]).astype(jnp.int32)
    panel = pos[2] * 2 + pos[3]

    own_list = (block_lists - panel * 24).astype(BF16)
    list_rows = jnp.broadcast_to(jnp.pad(own_list, ((0, 0), (0, 381)))[:, None, :], (1, 16, 384))
    sent = jnp.concatenate([local_inverse.astype(BF16), list_rows], axis=1)
    inverses = lax.all_gather(sent, ("x", "z"), axis=0, tiled=True)
    lists = inverses[:, 384, :3].astype(jnp.int32)

    half = start.astype(BF16)
    pieces = [*gather_ring(half[:, :256], "z", "x", 0), *gather_ring(half[:, 256:], "x", "z", 0)]
    residual = target - sum_over_col(*product(kernel, pieces, pos, False))

    low, high, fix = solve(to_columns(residual, pos), inverses, lists, counts, pos)
    pieces = [*gather_ring(low, "z", "x", 1), *gather_ring(high, "x", "z", 1)]
    residual = residual - sum_over_col(*product(kernel, pieces, pos, True))

    parts = solve(to_columns(residual, pos), inverses, lists, counts, pos, fix)
    return (from_columns(parts, start, pos)[None], residual[None])


def solution(mesh):
    fine = Mesh(mesh.devices.reshape(4, 4, 4, 2), ("x", "z", "y", "core"))
    row, col = ("x", "z"), ("y", "core")
    return jax.shard_map(
        body,
        mesh=fine,
        in_specs=(
            P(None, row, None, col),
            P(col, row, None),
            P(col, row, None),
            P(row + col, None, None),
            P(row + col, None),
            P(),
        ),
        out_specs=(P(col, row, None), P(col, row, None)),
        check_vma=False,
    )
```

time: 504 us -> 228 us (0.45)
  waiting for transfers between devices: 426 us -> 63.1 us
  starting transfers between devices: 0.51 us -> 92 us
  Pallas kernels: 0 us -> 37.5 us
  matrix products: 32.4 us -> 0 us
  other arithmetic: 9.26 us -> 3.8 us
    reduce_scatter x4 -> x0, waiting for transfers between devices: 230 us -> none  [the longest x2 160 us: owner_fixes(): lax.psum_scatter(corrections(current_residual), 'row', scatter_dimension=...]
    all_gather x4 -> x1, waiting for transfers between devices: 196 us -> 0.01 us  [body(): inverses = lax.all_gather(sent, ('x', 'z'), axis=0, tiled=True)]
    ppermute x0 -> x58, starting transfers between devices: none -> 92 us  [the longest x56 91.8 us: ring(): return lax.ppermute(value, axis, [(i, (i + step) % 4) for i in range(4)])]
    ppermute x0 -> x58, waiting for transfers between devices: none -> 63.1 us  [the longest x56 58.6 us: ring(): return lax.ppermute(value, axis, [(i, (i + step) % 4) for i in range(4)])]
    pallas_call x0 -> x10, Pallas kernels: none -> 37.5 us  [the longest x2 23 us: product(): pl.pallas_call(lambda *refs: product_kernel(transposed, *refs), grid_spec...]
    dot_general x6 -> x0, matrix products: 32.4 us -> none  [the longest x2 21.4 us: add_columns(): return jnp.dot(kernel_tile, shard_rows, preferred_element_type=jnp.float32)]
    reshape x5 -> x0, local copies, waits for them, and re-layouts: 15 us -> none  [the longest x2 13.7 us: corrections(): return summed.reshape(panel_rows, rhs_width)]
    unnamed x12 -> x17, local copies, waits for them, and re-layouts: 0.62 us -> 12.4 us
  transfers between devices with their start and end apart: 8 -> 59, of which waited for: 8 -> 29; matrix products, arithmetic and copies ran while one was open for 0% -> 2% of each run, Pallas kernels for 0% -> 4%
where the time goes in v1:
time: 228 us; the launch traced here: 227 us
  starting transfers between devices  92 us (40%)
  waiting for transfers between devices  63.1 us (28%)
  Pallas kernels  37.5 us (16%)
  local copies, waits for them, and re-layouts  16.3 us (7%)
  between operations  14.5 us (6%)
  other arithmetic  3.8 us (2%)
    ppermute x56, starting transfers between devices, ring(): return lax.ppermute(value, axis, [(i, (i + step) % 4) for i in range(4)])  91.8 us
    ppermute x56, waiting for transfers between devices, ring(): return lax.ppermute(value, axis, [(i, (i + step) % 4) for i in range(4)])  58.6 us
    pallas_call x2, Pallas kernels, product(): pl.pallas_call(lambda *refs: product_kernel(transposed, *refs), grid_spec...  23 us
    pallas_call x8, Pallas kernels, call(): pl.pallas_call(body, in_specs=[SMEM] * scalars + [VMEM] * (len(args) - sc...  14.5 us
    unnamed x17, local copies, waits for them, and re-layouts  12.4 us
  transfers between devices with their start and end apart: 59, of which 29 were waited for; matrix products, arithmetic and copies ran while one was open for 2% of the time, Pallas kernels for 4%

profile of v1, /device:TPU:0, one launch (start us, length us, event | category | flops | bytes accessed | tf_op | source)
XLA Modules:
  0.0 227.3 jit_solution(6983813349213113798)
XLA Ops:
  8.0 1.1 convert_element_type.48
  9.9 1.6 collective-permute-start.8
  11.6 1.7 collective-permute-start.9
  13.2 2.0 collective-permute-start
  15.2 2.1 collective-permute-start.1
  17.7 3.0 %collective-permute-start.11 = (bf16[96,256]{1,0:T(8,128)(2,1)S(1)}, bf16[96,256]{1,0:T(8,128)(2,1)S(1)}, u32[]{:S(2)}, u32[]{:S(2)}) collective-permute-start(bf16[96,256]{1,0:T(8,128)(2,1)S(1)} %slice.126), channel_id=1, source_target_pairs={{0,96},{32,0},{64,32},{96,64},{1,97},{33,1},{65,33},{97,65},{2,98}... | collective-permute-start | bytes 147464 | tf_op jit(solution)/shard_map/ppermute | solution.py:18
  21.2 2.9 %collective-permute-start.3 = (bf16[96,256]{1,0:T(8,128)(2,1)S(1)}, bf16[96,256]{1,0:T(8,128)(2,1)S(1)}, u32[]{:S(2)}, u32[]{:S(2)}) collective-permute-start(bf16[96,256]{1,0:T(8,128)(2,1)S(1)} %slice.121), channel_id=1, source_target_pairs={{0,24},{8,0},{16,8},{24,16},{1,25},{9,1},{17,9},{25,17},{2,26},{10... | collective-permute-start | bytes 147464 | tf_op jit(solution)/shard_map/ppermute | solution.py:18
  24.3 3.2 %collective-permute-start.13 = (bf16[4,192,256]{2,1,0:T(8,128)(2,1)S(1)}, bf16[4,192,256]{2,1,0:T(8,128)(2,1)S(1)}, u32[]{:S(2)}, u32[]{:S(2)}) collective-permute-start(bf16[4,192,256]{2,1,0:T(8,128)(2,1)S(1)} %pad_maximum_fusion.1.refs_7_), channel_id=1, source_target_pairs={{0,24},{8,0},{16,8},{24,16},{1,25},{9,1},{17,9},{25,17},{2,26},{10... | collective-permute-start | bytes 1179656 | tf_op jit(solution)/shard_map/ppermute | solution.py:18
  27.7 3.2 %collective-permute-start.5 = (bf16[4,192,256]{2,1,0:T(8,128)(2,1)S(1)}, bf16[4,192,256]{2,1,0:T(8,128)(2,1)S(1)}, u32[]{:S(2)}, u32[]{:S(2)}) collective-permute-start(bf16[4,192,256]{2,1,0:T(8,128)(2,1)S(1)} %pad_maximum_fusion.refs_2_), channel_id=1, source_target_pairs={{0,96},{32,0},{64,32},{96,64},{1,97},{33,1},{65,33},{97,65},{2,98}... | collective-permute-start | bytes 1179656 | tf_op jit(solution)/shard_map/ppermute | solution.py:18
  30.9 8.6 %collective-permute-done.12.refs_8_ = bf16[4,192,256]{2,1,0:T(8,128)(2,1)S(1)} collective-permute-done((bf16[4,192,256]{2,1,0:T(8,128)(2,1)S(1)}, bf16[4,192,256]{2,1,0:T(8,128)(2,1)S(1)}, u32[]{:S(2)}, u32[]{:S(2)}) %collective-permute-start.12) | collective-permute-done | bytes 393248 | tf_op jit(solution)/shard_map/ppermute | solution.py:18
  40.8 3.2 %collective-permute-start.15 = (bf16[2,192,256]{2,1,0:T(8,128)(2,1)}, bf16[2,192,256]{2,1,0:T(8,128)(2,1)S(1)}, u32[]{:S(2)}, u32[]{:S(2)}) collective-permute-start(bf16[2,192,256]{2,1,0:T(8,128)(2,1)} %slice.128), channel_id=1, source_target_pairs={{0,24},{8,0},{16,8},{24,16},{1,25},{9,1},{17,9},{25,17},{2,26},{10... | collective-permute-start | bytes 589832 | tf_op jit(solution)/shard_map/ppermute | solution.py:18
  45.5 3.2 %collective-permute-start.7 = (bf16[2,192,256]{2,1,0:T(8,128)(2,1)}, bf16[2,192,256]{2,1,0:T(8,128)(2,1)S(1)}, u32[]{:S(2)}, u32[]{:S(2)}) collective-permute-start(bf16[2,192,256]{2,1,0:T(8,128)(2,1)} %slice.123), channel_id=1, source_target_pairs={{0,96},{32,0},{64,32},{96,64},{1,97},{33,1},{65,33},{97,65},{2,98}... | collective-permute-start | bytes 589832 | tf_op jit(solution)/shard_map/ppermute | solution.py:18
  49.3 6.4 %collective-permute-done.6.refs_5_ = bf16[2,192,256]{2,1,0:T(8,128)(2,1)S(1)} collective-permute-done((bf16[2,192,256]{2,1,0:T(8,128)(2,1)}, bf16[2,192,256]{2,1,0:T(8,128)(2,1)S(1)}, u32[]{:S(2)}, u32[]{:S(2)}) %collective-permute-start.6) | collective-permute-done | bytes 196640 | tf_op jit(solution)/shard_map/ppermute | solution.py:18
  56.4 3.8 %copy-done.5 = bf16[8,1,192,3072]{3,2,1,0:T(8,128)(2,1)S(1)} copy-done((bf16[8,1,192,3072]{3,2,1,0:T(8,128)(2,1)S(1)}, bf16[8,1,192,3072]{3,2,1,0:T(8,128)(2,1)}, u32[]{:S(2)}) %copy-start.5) | copy-done | bytes 9437208
  60.2 7.9 %shard_map.77 = (bf16[4,192,512]{2,1,0:T(8,128)(2,1)S(1)}, bf16[4,192,512]{2,1,0:T(8,128)(2,1)S(1)}) custom-call(s32[4]{0:T(128)S(1)} %pad_add_fusion.refs_0_.pos_ref, bf16[8,192,3072]{2,1,0:T(8,128)(2,1)S(1)} %bitcast.80, bf16[4,192,256]{2,1,0:T(8,128)(2,1)S(1)} %pad_maximum_fusion.refs_2_, bf16[4,192,256]{2,1,0:T(8,128)(2,1)S(1)} %collective-permute-done.4.refs_3_, ...), custom_call_target="tpu_custom_call" | custom-call | flops 4831838208 | bytes 16777216 | tf_op jit(solution)/shard_map/pallas_call | solution.py:101
  68.2 2.3 collective-permute-done.16
  70.8 3.5 %collective-permute-start.17 = (bf16[192,512]{1,0:T(8,128)(2,1)S(1)}, bf16[192,512]{1,0:T(8,128)(2,1)S(1)}, u32[]{:S(2)}, u32[]{:S(2)}) collective-permute-start(bf16[192,512]{1,0:T(8,128)(2,1)S(1)} %get-tuple-element.71), channel_id=1, source_target_pairs={{0,4},{2,6},{4,0},{6,2},{1,5},{3,7},{5,1},{7,3},{8,12},{10,14},{12... | collective-permute-start | bytes 589832 | tf_op jit(solution)/shard_map/ppermute | solution.py:18
  74.3 1.1 collective-permute-start.18
  75.4 2.2 collective-permute-start.19
  77.5 2.6 %collective-permute-done.17 = bf16[192,512]{1,0:T(8,128)(2,1)S(1)} collective-permute-done((bf16[192,512]{1,0:T(8,128)(2,1)S(1)}, bf16[192,512]{1,0:T(8,128)(2,1)S(1)}, u32[]{:S(2)}, u32[]{:S(2)}) %collective-permute-start.17) | collective-permute-done | bytes 196640 | tf_op jit(solution)/shard_map/ppermute | solution.py:18
  80.1 3.6 %collective-permute-done.18 = bf16[192,512]{1,0:T(8,128)(2,1)S(1)} collective-permute-done((bf16[192,512]{1,0:T(8,128)(2,1)S(1)}, bf16[192,512]{1,0:T(8,128)(2,1)S(1)}, u32[]{:S(2)}, u32[]{:S(2)}) %collective-permute-start.18) | collective-permute-done | bytes 196640 | tf_op jit(solution)/shard_map/ppermute | solution.py:18
  86.0 2.6 %collective-permute-start.22 = (bf16[192,128]{1,0:T(8,128)(2,1)S(1)}, bf16[192,128]{1,0:T(8,128)(2,1)S(1)}, u32[]{:S(2)}, u32[]{:S(2)}) collective-permute-start(bf16[192,128]{1,0:T(8,128)(2,1)S(1)} %get-tuple-element.38), channel_id=1, source_target_pairs={{0,24},{8,0},{16,8},{24,16},{1,25},{9,1},{17,9},{25,17},{2,26},{10... | collective-permute-start | bytes 147464 | tf_op jit(solution)/shard_map/ppermute | solution.py:18
  88.6 2.6 %collective-permute-done.20.refs_1_ = bf16[192,128]{1,0:T(8,128)(2,1)S(1)} collective-permute-done((bf16[192,128]{1,0:T(8,128)(2,1)S(1)}, bf16[192,128]{1,0:T(8,128)(2,1)S(1)}, u32[]{:S(2)}, u32[]{:S(2)}) %collective-permute-start.20) | collective-permute-done | bytes 49184 | tf_op jit(solution)/shard_map/ppermute | solution.py:18
  92.9 5.0 %collective-permute-start.24 = (bf16[32,768]{1,0:T(8,128)(2,1)S(1)}, bf16[32,768]{1,0:T(8,128)(2,1)S(1)}, u32[]{:S(2)}, u32[]{:S(2)}) collective-permute-start(bf16[32,768]{1,0:T(8,128)(2,1)S(1)} %get-tuple-element.41), channel_id=1, source_target_pairs={{0,64},{32,96},{64,0},{96,32},{1,65},{33,97},{65,1},{97,33},{2,66}... | collective-permute-start | bytes 147464 | tf_op jit(solution)/shard_map/ppermute | solution.py:18
  98.8 1.6 collective-permute-done.24.refs_5_
  100.4 1.5 collective-permute-done.25.refs_6_
  101.9 2.4 %copy-done = bf16[16,400,384]{2,1,0:T(8,128)(2,1)S(1)} copy-done((bf16[16,400,384]{2,1,0:T(8,128)(2,1)S(1)}, bf16[16,400,384]{2,1,0:T(8,128)(2,1)}, u32[]{:S(2)}) %copy-start) | copy-done | bytes 4915224
  104.3 4.8 %shard_map.80 = (bf16[16,3072]{1,0:T(8,128)(2,1)S(1)}, bf16[16,3072]{1,0:T(8,128)(2,1)S(1)}, f32[32,3072]{1,0:T(8,128)S(1)}) custom-call(s32[4]{0:T(128)S(1)} %pad_add_fusion.refs_0_.pos_ref, s32[16,3]{1,0:T(8,128)S(1)} %bitcast.74, s32[192]{0:T(256)S(1)} %copy-done.4, bf16[32,768]{1,0:T(8,128)(2,1)S(1)} %get-tuple-element.39.refs_3_, ...), custom_call_target="tpu_custom_call" | custom-call | tf_op jit(solution)/shard_map/pallas_call | solution.py:154
  109.3 3.2 %collective-permute-start.35 = (bf16[16,3072]{1,0:T(8,128)(2,1)S(1)}, bf16[16,3072]{1,0:T(8,128)(2,1)S(1)}, u32[]{:S(2)}, u32[]{:S(2)}) collective-permute-start(bf16[16,3072]{1,0:T(8,128)(2,1)S(1)} %get-tuple-element.44), channel_id=1, source_target_pairs={{0,96},{32,0},{64,32},{96,64},{1,97},{33,1},{65,33},{97,65},{2,98}... | collective-permute-start | bytes 294920 | tf_op jit(solution)/shard_map/ppermute | solution.py:18
  112.5 1.5 collective-permute-start.26
  114.0 1.7 collective-permute-start.27
  115.8 3.3 %collective-permute-start.37 = (bf16[16,1536]{1,0:T(8,128)(2,1)S(1)}, bf16[16,1536]{1,0:T(8,128)(2,1)S(1)}, u32[]{:S(2)}, u32[]{:S(2)}) collective-permute-start(bf16[16,1536]{1,0:T(8,128)(2,1)S(1)} %slice.138), channel_id=1, source_target_pairs={{0,96},{32,0},{64,32},{96,64},{1,97},{33,1},{65,33},{97,65},{2,98}... | collective-permute-start | bytes 147464 | tf_op jit(solution)/shard_map/ppermute | solution.py:18
  119.1 1.4 collective-permute-start.28
  120.5 2.0 collective-permute-start.29
  122.7 3.1 %collective-permute-start.39 = (bf16[4,16,3072]{2,1,0:T(8,128)(2,1)S(1)}, bf16[4,16,3072]{2,1,0:T(8,128)(2,1)S(1)}, u32[]{:S(2)}, u32[]{:S(2)}) collective-permute-start(bf16[4,16,3072]{2,1,0:T(8,128)(2,1)S(1)} %pad_maximum_fusion.3.refs_7_), channel_id=1, source_target_pairs={{0,24},{8,0},{16,8},{24,16},{1,25},{9,1},{17,9},{25,17},{2,26},{10... | collective-permute-start | bytes 1179656 | tf_op jit(solution)/shard_map/ppermute | solution.py:18
  126.0 3.2 %collective-permute-start.31 = (bf16[4,16,3072]{2,1,0:T(8,128)(2,1)S(1)}, bf16[4,16,3072]{2,1,0:T(8,128)(2,1)S(1)}, u32[]{:S(2)}, u32[]{:S(2)}) collective-permute-start(bf16[4,16,3072]{2,1,0:T(8,128)(2,1)S(1)} %pad_maximum_fusion.2.refs_2_), channel_id=1, source_target_pairs={{0,96},{32,0},{64,32},{96,64},{1,97},{33,1},{65,33},{97,65},{2,98}... | collective-permute-start | bytes 1179656 | tf_op jit(solution)/shard_map/ppermute | solution.py:18
  129.3 4.5 %collective-permute-done.38.refs_8_ = bf16[4,16,3072]{2,1,0:T(8,128)(2,1)S(1)} collective-permute-done((bf16[4,16,3072]{2,1,0:T(8,128)(2,1)S(1)}, bf16[4,16,3072]{2,1,0:T(8,128)(2,1)S(1)}, u32[]{:S(2)}, u32[]{:S(2)}) %collective-permute-start.38) | collective-permute-done | bytes 393248 | tf_op jit(solution)/shard_map/ppermute | solution.py:18
  133.9 3.3 %collective-permute-start.41 = (bf16[2,16,3072]{2,1,0:T(8,128)(2,1)S(1)}, bf16[2,16,3072]{2,1,0:T(8,128)(2,1)S(1)}, u32[]{:S(2)}, u32[]{:S(2)}) collective-permute-start(bf16[2,16,3072]{2,1,0:T(8,128)(2,1)S(1)} %slice.140), channel_id=1, source_target_pairs={{0,24},{8,0},{16,8},{24,16},{1,25},{9,1},{17,9},{25,17},{2,26},{10... | collective-permute-start | bytes 589832 | tf_op jit(solution)/shard_map/ppermute | solution.py:18
  137.3 3.3 %collective-permute-start.33 = (bf16[2,16,3072]{2,1,0:T(8,128)(2,1)S(1)}, bf16[2,16,3072]{2,1,0:T(8,128)(2,1)S(1)}, u32[]{:S(2)}, u32[]{:S(2)}) collective-permute-start(bf16[2,16,3072]{2,1,0:T(8,128)(2,1)S(1)} %slice.136), channel_id=1, source_target_pairs={{0,96},{32,0},{64,32},{96,64},{1,97},{33,1},{65,33},{97,65},{2,98}... | collective-permute-start | bytes 589832 | tf_op jit(solution)/shard_map/ppermute | solution.py:18
  140.7 3.4 %collective-permute-done.32.refs_5_ = bf16[2,16,3072]{2,1,0:T(8,128)(2,1)S(1)} collective-permute-done((bf16[2,16,3072]{2,1,0:T(8,128)(2,1)S(1)}, bf16[2,16,3072]{2,1,0:T(8,128)(2,1)S(1)}, u32[]{:S(2)}, u32[]{:S(2)}) %collective-permute-start.32) | collective-permute-done | bytes 196640 | tf_op jit(solution)/shard_map/ppermute | solution.py:18
  144.1 3.7 %copy-done.6 = bf16[8,1,192,3072]{3,2,1,0:T(8,128)(2,1)S(1)} copy-done((bf16[8,1,192,3072]{3,2,1,0:T(8,128)(2,1)S(1)}, bf16[8,1,192,3072]{3,2,1,0:T(8,128)(2,1)}, u32[]{:S(2)}) %copy-start.6) | copy-done | bytes 9437208
  147.8 15.2 %shard_map.81 = (bf16[4,192,512]{2,1,0:T(8,128)(2,1)S(1)}, bf16[4,192,512]{2,1,0:T(8,128)(2,1)S(1)}) custom-call(s32[4]{0:T(128)S(1)} %pad_add_fusion.refs_0_.pos_ref, bf16[8,192,3072]{2,1,0:T(8,128)(2,1)S(1)} %bitcast.81, bf16[4,16,3072]{2,1,0:T(8,128)(2,1)S(1)} %pad_maximum_fusion.2.refs_2_, bf16[4,16,3072]{2,1,0:T(8,128)(2,1)S(1)} %collective-permute-done.30.refs_3_, ...), custom_call_target="tpu_custom_call" | custom-call | flops 4831838208 | bytes 16777216 | tf_op jit(solution)/shard_map/pallas_call | solution.py:101
  163.1 2.3 collective-permute-done.42
  165.7 2.1 collective-permute-start.43
  167.8 0.9 collective-permute-start.44
  168.7 2.3 %collective-permute-start.45 = (bf16[192,512]{1,0:T(8,128)(2,1)S(1)}, bf16[192,512]{1,0:T(8,128)(2,1)S(1)}, u32[]{:S(2)}, u32[]{:S(2)}) collective-permute-start(bf16[192,512]{1,0:T(8,128)(2,1)S(1)} %get-tuple-element.69), channel_id=1, source_target_pairs={{0,6},{2,0},{4,2},{6,4},{1,7},{3,1},{5,3},{7,5},{8,14},{10,8},{12,... | collective-permute-start | bytes 589832 | tf_op jit(solution)/shard_map/ppermute | solution.py:18
  171.0 4.0 %collective-permute-done.43 = bf16[192,512]{1,0:T(8,128)(2,1)S(1)} collective-permute-done((bf16[192,512]{1,0:T(8,128)(2,1)S(1)}, bf16[192,512]{1,0:T(8,128)(2,1)S(1)}, u32[]{:S(2)}, u32[]{:S(2)}) %collective-permute-start.43) | collective-permute-done | bytes 196640 | tf_op jit(solution)/shard_map/ppermute | solution.py:18
  175.0 3.4 %collective-permute-done.44 = bf16[192,512]{1,0:T(8,128)(2,1)S(1)} collective-permute-done((bf16[192,512]{1,0:T(8,128)(2,1)S(1)}, bf16[192,512]{1,0:T(8,128)(2,1)S(1)}, u32[]{:S(2)}, u32[]{:S(2)}) %collective-permute-start.44) | collective-permute-done | bytes 196640 | tf_op jit(solution)/shard_map/ppermute | solution.py:18
  179.3 3.9 %collective-permute-start.47 = (bf16[192,128]{1,0:T(8,128)(2,1)S(1)}, bf16[192,128]{1,0:T(8,128)(2,1)S(1)}, u32[]{:S(2)}, u32[]{:S(2)}) collective-permute-start(bf16[192,128]{1,0:T(8,128)(2,1)S(1)} %get-tuple-element.49), channel_id=1, source_target_pairs={{0,16},{8,24},{16,0},{24,8},{1,17},{9,25},{17,1},{25,9},{2,18},{10... | collective-permute-start | bytes 147464 | tf_op jit(solution)/shard_map/ppermute | solution.py:18
  183.5 1.6 collective-permute-done.46.refs_1_
  185.9 1.4 collective-permute-done.48.refs_3_
  188.1 4.8 %collective-permute-start.50 = (bf16[32,768]{1,0:T(8,128)(2,1)S(1)}, bf16[32,768]{1,0:T(8,128)(2,1)S(1)}, u32[]{:S(2)}, u32[]{:S(2)}) collective-permute-start(bf16[32,768]{1,0:T(8,128)(2,1)S(1)} %get-tuple-element.53), channel_id=1, source_target_pairs={{0,64},{32,96},{64,0},{96,32},{1,65},{33,97},{65,1},{97,33},{2,66}... | collective-permute-start | bytes 147464 | tf_op jit(solution)/shard_map/ppermute | solution.py:18
  193.8 1.7 collective-permute-done.50.refs_5_
  195.5 1.5 collective-permute-done.51.refs_6_
  197.0 2.4 %copy-done.1 = bf16[16,400,384]{2,1,0:T(8,128)(2,1)S(1)} copy-done((bf16[16,400,384]{2,1,0:T(8,128)(2,1)S(1)}, bf16[16,400,384]{2,1,0:T(8,128)(2,1)}, u32[]{:S(2)}) %copy-start.1) | copy-done | bytes 4915224
  199.4 4.8 %shard_map.84 = (bf16[32,768]{1,0:T(8,128)(2,1)S(1)}, bf16[32,768]{1,0:T(8,128)(2,1)S(1)}, bf16[32,768]{1,0:T(8,128)(2,1)S(1)}, bf16[32,768]{1,0:T(8,128)(2,1)S(1)}) custom-call(s32[4]{0:T(128)S(1)} %pad_add_fusion.refs_0_.pos_ref, s32[16,3]{1,0:T(8,128)S(1)} %bitcast.75, s32[192]{0:T(256)S(1)} %copy-done.4, bf16[32,768]{1,0:T(8,128)(2,1)S(1)} %get-tuple-element.51.refs_3_, ...), custom_call_target="tpu_custom_call" | custom-call | tf_op jit(solution)/shard_map/pallas_call | solution.py:154
  204.4 2.6 %collective-permute-start.53 = (bf16[32,768]{1,0:T(8,128)(2,1)S(1)}, bf16[32,768]{1,0:T(8,128)(2,1)S(1)}, u32[]{:S(2)}, u32[]{:S(2)}) collective-permute-start(bf16[32,768]{1,0:T(8,128)(2,1)S(1)} %get-tuple-element.75), channel_id=1, source_target_pairs={{0,64},{32,96},{64,0},{96,32},{1,65},{33,97},{65,1},{97,33},{2,66}... | collective-permute-start | bytes 147464 | tf_op jit(solution)/shard_map/ppermute | solution.py:18
  207.0 1.5 collective-permute-start.54
  208.5 1.7 collective-permute-done.52.refs_1_
  212.2 2.8 %collective-permute-start.56 = (bf16[192,128]{1,0:T(8,128)(2,1)S(1)}, bf16[192,128]{1,0:T(8,128)(2,1)S(1)}, u32[]{:S(2)}, u32[]{:S(2)}) collective-permute-start(bf16[192,128]{1,0:T(8,128)(2,1)S(1)} %get-tuple-element.62), channel_id=1, source_target_pairs={{0,16},{8,24},{16,0},{24,8},{1,17},{9,25},{17,1},{25,9},{2,18},{10... | collective-permute-start | bytes 147464 | tf_op jit(solution)/shard_map/ppermute | solution.py:18
  215.0 1.1 collective-permute-start.57
  216.1 1.1 collective-permute-done.55.refs_1_
  217.8 1.3 collective-permute-done.57.refs_3_
  219.1 1.4 shard_map.86
  (125 shorter events, 19.8 us)
Async XLA Ops:
  7.2 90.7 %all-gather.2.cloned.1.call-start = ((), (), s32[]{:S(2)}) async-start(), calls=%async_computation | async-start | bytes 5222400 | tf_op jit(solution)/shard_map/all_gather | solution.py:269
  9.9 7.4 %collective-permute-start.8 = (bf16[192,256]{1,0:T(8,128)(2,1)S(1)}, bf16[192,256]{1,0:T(8,128)(2,1)S(1)}, u32[]{:S(2)}, u32[]{:S(2)}) collective-permute-start(bf16[192,256]{1,0:T(8,128)(2,1)S(1)} %get-tuple-element.80), channel_id=1, source_target_pairs={{0,32},{32,64},{64,96},{96,0},{1,33},{33,65},{65,97},{97,1},{2,34}... | collective-permute-start | bytes 294920 | tf_op jit(solution)/shard_map/ppermute | solution.py:18
  11.6 6.1 %collective-permute-start.9 = (bf16[192,256]{1,0:T(8,128)(2,1)S(1)}, bf16[192,256]{1,0:T(8,128)(2,1)S(1)}, u32[]{:S(2)}, u32[]{:S(2)}) collective-permute-start(bf16[192,256]{1,0:T(8,128)(2,1)S(1)} %get-tuple-element.80), channel_id=1, source_target_pairs={{0,96},{32,0},{64,32},{96,64},{1,97},{33,1},{65,33},{97,65},{2,98}... | collective-permute-start | bytes 294920 | tf_op jit(solution)/shard_map/ppermute | solution.py:18
  13.2 7.5 %collective-permute-start = (bf16[192,256]{1,0:T(8,128)(2,1)S(1)}, bf16[192,256]{1,0:T(8,128)(2,1)S(1)}, u32[]{:S(2)}, u32[]{:S(2)}) collective-permute-start(bf16[192,256]{1,0:T(8,128)(2,1)S(1)} %get-tuple-element.81), channel_id=1, source_target_pairs={{0,8},{8,16},{16,24},{24,0},{1,9},{9,17},{17,25},{25,1},{2,10},{10... | collective-permute-start | bytes 294920 | tf_op jit(solution)/shard_map/ppermute | solution.py:18
  15.2 6.0 %collective-permute-start.1 = (bf16[192,256]{1,0:T(8,128)(2,1)S(1)}, bf16[192,256]{1,0:T(8,128)(2,1)S(1)}, u32[]{:S(2)}, u32[]{:S(2)}) collective-permute-start(bf16[192,256]{1,0:T(8,128)(2,1)S(1)} %get-tuple-element.81), channel_id=1, source_target_pairs={{0,24},{8,0},{16,8},{24,16},{1,25},{9,1},{17,9},{25,17},{2,26},{10... | collective-permute-start | bytes 294920 | tf_op jit(solution)/shard_map/ppermute | solution.py:18
  17.4 6.8 %collective-permute-start.10 = (bf16[96,256]{1,0:T(8,128)(2,1)S(1)}, bf16[96,256]{1,0:T(8,128)(2,1)S(1)}, u32[]{:S(2)}, u32[]{:S(2)}) collective-permute-start(bf16[96,256]{1,0:T(8,128)(2,1)S(1)} %slice.125), channel_id=1, source_target_pairs={{0,32},{32,64},{64,96},{96,0},{1,33},{33,65},{65,97},{97,1},{2,34}... | collective-permute-start | bytes 147464 | tf_op jit(solution)/shard_map/ppermute | solution.py:18
  17.7 6.4 %collective-permute-start.11 = (bf16[96,256]{1,0:T(8,128)(2,1)S(1)}, bf16[96,256]{1,0:T(8,128)(2,1)S(1)}, u32[]{:S(2)}, u32[]{:S(2)}) collective-permute-start(bf16[96,256]{1,0:T(8,128)(2,1)S(1)} %slice.126), channel_id=1, source_target_pairs={{0,96},{32,0},{64,32},{96,64},{1,97},{33,1},{65,33},{97,65},{2,98}... | collective-permute-start | bytes 147464 | tf_op jit(solution)/shard_map/ppermute | solution.py:18
  20.7 6.8 %collective-permute-start.2 = (bf16[96,256]{1,0:T(8,128)(2,1)S(1)}, bf16[96,256]{1,0:T(8,128)(2,1)S(1)}, u32[]{:S(2)}, u32[]{:S(2)}) collective-permute-start(bf16[96,256]{1,0:T(8,128)(2,1)S(1)} %slice.120), channel_id=1, source_target_pairs={{0,8},{8,16},{16,24},{24,0},{1,9},{9,17},{17,25},{25,1},{2,10},{10... | collective-permute-start | bytes 147464 | tf_op jit(solution)/shard_map/ppermute | solution.py:18
  21.2 6.3 %collective-permute-start.3 = (bf16[96,256]{1,0:T(8,128)(2,1)S(1)}, bf16[96,256]{1,0:T(8,128)(2,1)S(1)}, u32[]{:S(2)}, u32[]{:S(2)}) collective-permute-start(bf16[96,256]{1,0:T(8,128)(2,1)S(1)} %slice.121), channel_id=1, source_target_pairs={{0,24},{8,0},{16,8},{24,16},{1,25},{9,1},{17,9},{25,17},{2,26},{10... | collective-permute-start | bytes 147464 | tf_op jit(solution)/shard_map/ppermute | solution.py:18
  24.2 15.3 %collective-permute-start.12 = (bf16[4,192,256]{2,1,0:T(8,128)(2,1)S(1)}, bf16[4,192,256]{2,1,0:T(8,128)(2,1)S(1)}, u32[]{:S(2)}, u32[]{:S(2)}) collective-permute-start(bf16[4,192,256]{2,1,0:T(8,128)(2,1)S(1)} %pad_maximum_fusion.1.refs_7_), channel_id=1, source_target_pairs={{0,8},{8,16},{16,24},{24,0},{1,9},{9,17},{17,25},{25,1},{2,10},{10... | collective-permute-start | bytes 1179656 | tf_op jit(solution)/shard_map/ppermute | solution.py:18
  24.3 15.9 %collective-permute-start.13 = (bf16[4,192,256]{2,1,0:T(8,128)(2,1)S(1)}, bf16[4,192,256]{2,1,0:T(8,128)(2,1)S(1)}, u32[]{:S(2)}, u32[]{:S(2)}) collective-permute-start(bf16[4,192,256]{2,1,0:T(8,128)(2,1)S(1)} %pad_maximum_fusion.1.refs_7_), channel_id=1, source_target_pairs={{0,24},{8,0},{16,8},{24,16},{1,25},{9,1},{17,9},{25,17},{2,26},{10... | collective-permute-start | bytes 1179656 | tf_op jit(solution)/shard_map/ppermute | solution.py:18
  27.6 16.5 %collective-permute-start.4 = (bf16[4,192,256]{2,1,0:T(8,128)(2,1)S(1)}, bf16[4,192,256]{2,1,0:T(8,128)(2,1)S(1)}, u32[]{:S(2)}, u32[]{:S(2)}) collective-permute-start(bf16[4,192,256]{2,1,0:T(8,128)(2,1)S(1)} %pad_maximum_fusion.refs_2_), channel_id=1, source_target_pairs={{0,32},{32,64},{64,96},{96,0},{1,33},{33,65},{65,97},{97,1},{2,34}... | collective-permute-start | bytes 1179656 | tf_op jit(solution)/shard_map/ppermute | solution.py:18
  27.7 17.1 %collective-permute-start.5 = (bf16[4,192,256]{2,1,0:T(8,128)(2,1)S(1)}, bf16[4,192,256]{2,1,0:T(8,128)(2,1)S(1)}, u32[]{:S(2)}, u32[]{:S(2)}) collective-permute-start(bf16[4,192,256]{2,1,0:T(8,128)(2,1)S(1)} %pad_maximum_fusion.refs_2_), channel_id=1, source_target_pairs={{0,96},{32,0},{64,32},{96,64},{1,97},{33,1},{65,33},{97,65},{2,98}... | collective-permute-start | bytes 1179656 | tf_op jit(solution)/shard_map/ppermute | solution.py:18
  40.1 8.6 %collective-permute-start.14 = (bf16[2,192,256]{2,1,0:T(8,128)(2,1)}, bf16[2,192,256]{2,1,0:T(8,128)(2,1)S(1)}, u32[]{:S(2)}, u32[]{:S(2)}) collective-permute-start(bf16[2,192,256]{2,1,0:T(8,128)(2,1)} %slice.127), channel_id=1, source_target_pairs={{0,8},{8,16},{16,24},{24,0},{1,9},{9,17},{17,25},{25,1},{2,10},{10... | collective-permute-start | bytes 589832 | tf_op jit(solution)/shard_map/ppermute | solution.py:18
  40.8 8.4 %collective-permute-start.15 = (bf16[2,192,256]{2,1,0:T(8,128)(2,1)}, bf16[2,192,256]{2,1,0:T(8,128)(2,1)S(1)}, u32[]{:S(2)}, u32[]{:S(2)}) collective-permute-start(bf16[2,192,256]{2,1,0:T(8,128)(2,1)} %slice.128), channel_id=1, source_target_pairs={{0,24},{8,0},{16,8},{24,16},{1,25},{9,1},{17,9},{25,17},{2,26},{10... | collective-permute-start | bytes 589832 | tf_op jit(solution)/shard_map/ppermute | solution.py:18
  44.8 10.9 %collective-permute-start.6 = (bf16[2,192,256]{2,1,0:T(8,128)(2,1)}, bf16[2,192,256]{2,1,0:T(8,128)(2,1)S(1)}, u32[]{:S(2)}, u32[]{:S(2)}) collective-permute-start(bf16[2,192,256]{2,1,0:T(8,128)(2,1)} %slice.122), channel_id=1, source_target_pairs={{0,32},{32,64},{64,96},{96,0},{1,33},{33,65},{65,97},{97,1},{2,34}... | collective-permute-start | bytes 589832 | tf_op jit(solution)/shard_map/ppermute | solution.py:18
  45.5 10.9 %collective-permute-start.7 = (bf16[2,192,256]{2,1,0:T(8,128)(2,1)}, bf16[2,192,256]{2,1,0:T(8,128)(2,1)S(1)}, u32[]{:S(2)}, u32[]{:S(2)}) collective-permute-start(bf16[2,192,256]{2,1,0:T(8,128)(2,1)} %slice.123), channel_id=1, source_target_pairs={{0,96},{32,0},{64,32},{96,64},{1,97},{33,1},{65,33},{97,65},{2,98}... | collective-permute-start | bytes 589832 | tf_op jit(solution)/shard_map/ppermute | solution.py:18
  56.4 3.8 %copy-start.5 = (bf16[8,1,192,3072]{3,2,1,0:T(8,128)(2,1)S(1)}, bf16[8,1,192,3072]{3,2,1,0:T(8,128)(2,1)}, u32[]{:S(2)}) copy-start(bf16[8,1,192,3072]{3,2,1,0:T(8,128)(2,1)} %param.6) | copy-start | bytes 28311556
  68.1 2.4 %collective-permute-start.16 = (bf16[4,192,512]{2,1,0:T(8,128)(2,1)S(1)}, bf16[4,192,512]{2,1,0:T(8,128)(2,1)S(1)}, u32[]{:S(2)}, u32[]{:S(2)}) collective-permute-start(bf16[4,192,512]{2,1,0:T(8,128)(2,1)S(1)} %get-tuple-element.34), channel_id=1, source_target_pairs={{0,1},{1,0},{2,3},{3,2},{4,5},{5,4},{6,7},{7,6},{8,9},{9,8},{10,11... | collective-permute-start | bytes 2359304 | tf_op jit(solution)/shard_map/ppermute | solution.py:22
  70.5 14.0 %copy-start.7 = (f32[1,192,512]{2,1,0:T(8,128)S(1)}, f32[1,192,512]{2,1,0:T(8,128)}, u32[]{:S(2)}) copy-start(f32[1,192,512]{2,1,0:T(8,128)} %param.7) | copy-start | bytes 1179652
  70.8 31.2 %copy-start.4 = (s32[192]{0:T(256)S(1)}, s32[192]{0:T(256)}, u32[]{:S(2)}) copy-start(s32[192]{0:T(256)} %refs_2_.3) | copy-start | bytes 2308
  70.8 9.3 %collective-permute-start.17 = (bf16[192,512]{1,0:T(8,128)(2,1)S(1)}, bf16[192,512]{1,0:T(8,128)(2,1)S(1)}, u32[]{:S(2)}, u32[]{:S(2)}) collective-permute-start(bf16[192,512]{1,0:T(8,128)(2,1)S(1)} %get-tuple-element.71), channel_id=1, source_target_pairs={{0,4},{2,6},{4,0},{6,2},{1,5},{3,7},{5,1},{7,3},{8,12},{10,14},{12... | collective-permute-start | bytes 589832 | tf_op jit(solution)/shard_map/ppermute | solution.py:18
  74.3 9.4 %collective-permute-start.18 = (bf16[192,512]{1,0:T(8,128)(2,1)S(1)}, bf16[192,512]{1,0:T(8,128)(2,1)S(1)}, u32[]{:S(2)}, u32[]{:S(2)}) collective-permute-start(bf16[192,512]{1,0:T(8,128)(2,1)S(1)} %get-tuple-element.73), channel_id=1, source_target_pairs={{0,2},{2,4},{4,6},{6,0},{1,3},{3,5},{5,7},{7,1},{8,10},{10,12},{12... | collective-permute-start | bytes 589832 | tf_op jit(solution)/shard_map/ppermute | solution.py:18
  75.4 9.1 %collective-permute-start.19 = (bf16[192,512]{1,0:T(8,128)(2,1)S(1)}, bf16[192,512]{1,0:T(8,128)(2,1)S(1)}, u32[]{:S(2)}, u32[]{:S(2)}) collective-permute-start(bf16[192,512]{1,0:T(8,128)(2,1)S(1)} %get-tuple-element.72), channel_id=1, source_target_pairs={{0,6},{2,0},{4,2},{6,4},{1,7},{3,1},{5,3},{7,5},{8,14},{10,8},{12,... | collective-permute-start | bytes 589832 | tf_op jit(solution)/shard_map/ppermute | solution.py:18
  85.3 5.9 %collective-permute-start.20 = (bf16[192,128]{1,0:T(8,128)(2,1)S(1)}, bf16[192,128]{1,0:T(8,128)(2,1)S(1)}, u32[]{:S(2)}, u32[]{:S(2)}) collective-permute-start(bf16[192,128]{1,0:T(8,128)(2,1)S(1)} %get-tuple-element.36), channel_id=1, source_target_pairs={{0,8},{8,16},{16,24},{24,0},{1,9},{9,17},{17,25},{25,1},{2,10},{10... | collective-permute-start | bytes 147464 | tf_op jit(solution)/shard_map/ppermute | solution.py:18
  85.3 5.8 %collective-permute-start.21 = (bf16[192,128]{1,0:T(8,128)(2,1)S(1)}, bf16[192,128]{1,0:T(8,128)(2,1)S(1)}, u32[]{:S(2)}, u32[]{:S(2)}) collective-permute-start(bf16[192,128]{1,0:T(8,128)(2,1)S(1)} %get-tuple-element.37), channel_id=1, source_target_pairs={{0,16},{8,24},{16,0},{24,8},{1,17},{9,25},{17,1},{25,9},{2,18},{10... | collective-permute-start | bytes 147464 | tf_op jit(solution)/shard_map/ppermute | solution.py:18
  86.0 6.0 %collective-permute-start.22 = (bf16[192,128]{1,0:T(8,128)(2,1)S(1)}, bf16[192,128]{1,0:T(8,128)(2,1)S(1)}, u32[]{:S(2)}, u32[]{:S(2)}) collective-permute-start(bf16[192,128]{1,0:T(8,128)(2,1)S(1)} %get-tuple-element.38), channel_id=1, source_target_pairs={{0,24},{8,0},{16,8},{24,16},{1,25},{9,1},{17,9},{25,17},{2,26},{10... | collective-permute-start | bytes 147464 | tf_op jit(solution)/shard_map/ppermute | solution.py:18
  92.8 6.0 %collective-permute-start.23 = (bf16[32,768]{1,0:T(8,128)(2,1)S(1)}, bf16[32,768]{1,0:T(8,128)(2,1)S(1)}, u32[]{:S(2)}, u32[]{:S(2)}) collective-permute-start(bf16[32,768]{1,0:T(8,128)(2,1)S(1)} %get-tuple-element.40), channel_id=1, source_target_pairs={{0,32},{32,64},{64,96},{96,0},{1,33},{33,65},{65,97},{97,1},{2,34}... | collective-permute-start | bytes 147464 | tf_op jit(solution)/shard_map/ppermute | solution.py:18
  92.9 7.6 %collective-permute-start.24 = (bf16[32,768]{1,0:T(8,128)(2,1)S(1)}, bf16[32,768]{1,0:T(8,128)(2,1)S(1)}, u32[]{:S(2)}, u32[]{:S(2)}) collective-permute-start(bf16[32,768]{1,0:T(8,128)(2,1)S(1)} %get-tuple-element.41), channel_id=1, source_target_pairs={{0,64},{32,96},{64,0},{96,32},{1,65},{33,97},{65,1},{97,33},{2,66}... | collective-permute-start | bytes 147464 | tf_op jit(solution)/shard_map/ppermute | solution.py:18
  97.9 4.1 %collective-permute-start.25 = (bf16[32,768]{1,0:T(8,128)(2,1)S(1)}, bf16[32,768]{1,0:T(8,128)(2,1)S(1)}, u32[]{:S(2)}, u32[]{:S(2)}) collective-permute-start(bf16[32,768]{1,0:T(8,128)(2,1)S(1)} %get-tuple-element.42), channel_id=1, source_target_pairs={{0,96},{32,0},{64,32},{96,64},{1,97},{33,1},{65,33},{97,65},{2,98}... | collective-permute-start | bytes 147464 | tf_op jit(solution)/shard_map/ppermute | solution.py:18
  109.2 6.5 %collective-permute-start.34 = (bf16[16,3072]{1,0:T(8,128)(2,1)S(1)}, bf16[16,3072]{1,0:T(8,128)(2,1)S(1)}, u32[]{:S(2)}, u32[]{:S(2)}) collective-permute-start(bf16[16,3072]{1,0:T(8,128)(2,1)S(1)} %get-tuple-element.44), channel_id=1, source_target_pairs={{0,32},{32,64},{64,96},{96,0},{1,33},{33,65},{65,97},{97,1},{2,34}... | collective-permute-start | bytes 294920 | tf_op jit(solution)/shard_map/ppermute | solution.py:18
  109.3 6.5 %collective-permute-start.35 = (bf16[16,3072]{1,0:T(8,128)(2,1)S(1)}, bf16[16,3072]{1,0:T(8,128)(2,1)S(1)}, u32[]{:S(2)}, u32[]{:S(2)}) collective-permute-start(bf16[16,3072]{1,0:T(8,128)(2,1)S(1)} %get-tuple-element.44), channel_id=1, source_target_pairs={{0,96},{32,0},{64,32},{96,64},{1,97},{33,1},{65,33},{97,65},{2,98}... | collective-permute-start | bytes 294920 | tf_op jit(solution)/shard_map/ppermute | solution.py:18
  112.5 6.6 %collective-permute-start.26 = (bf16[16,3072]{1,0:T(8,128)(2,1)S(1)}, bf16[16,3072]{1,0:T(8,128)(2,1)S(1)}, u32[]{:S(2)}, u32[]{:S(2)}) collective-permute-start(bf16[16,3072]{1,0:T(8,128)(2,1)S(1)} %get-tuple-element.43), channel_id=1, source_target_pairs={{0,8},{8,16},{16,24},{24,0},{1,9},{9,17},{17,25},{25,1},{2,10},{10... | collective-permute-start | bytes 294920 | tf_op jit(solution)/shard_map/ppermute | solution.py:18
  114.0 6.5 %collective-permute-start.27 = (bf16[16,3072]{1,0:T(8,128)(2,1)S(1)}, bf16[16,3072]{1,0:T(8,128)(2,1)S(1)}, u32[]{:S(2)}, u32[]{:S(2)}) collective-permute-start(bf16[16,3072]{1,0:T(8,128)(2,1)S(1)} %get-tuple-element.43), channel_id=1, source_target_pairs={{0,24},{8,0},{16,8},{24,16},{1,25},{9,1},{17,9},{25,17},{2,26},{10... | collective-permute-start | bytes 294920 | tf_op jit(solution)/shard_map/ppermute | solution.py:18
  115.7 6.8 %collective-permute-start.36 = (bf16[16,1536]{1,0:T(8,128)(2,1)S(1)}, bf16[16,1536]{1,0:T(8,128)(2,1)S(1)}, u32[]{:S(2)}, u32[]{:S(2)}) collective-permute-start(bf16[16,1536]{1,0:T(8,128)(2,1)S(1)} %slice.137), channel_id=1, source_target_pairs={{0,32},{32,64},{64,96},{96,0},{1,33},{33,65},{65,97},{97,1},{2,34}... | collective-permute-start | bytes 147464 | tf_op jit(solution)/shard_map/ppermute | solution.py:18
  115.8 6.7 %collective-permute-start.37 = (bf16[16,1536]{1,0:T(8,128)(2,1)S(1)}, bf16[16,1536]{1,0:T(8,128)(2,1)S(1)}, u32[]{:S(2)}, u32[]{:S(2)}) collective-permute-start(bf16[16,1536]{1,0:T(8,128)(2,1)S(1)} %slice.138), channel_id=1, source_target_pairs={{0,96},{32,0},{64,32},{96,64},{1,97},{33,1},{65,33},{97,65},{2,98}... | collective-permute-start | bytes 147464 | tf_op jit(solution)/shard_map/ppermute | solution.py:18
  119.1 6.8 %collective-permute-start.28 = (bf16[16,1536]{1,0:T(8,128)(2,1)S(1)}, bf16[16,1536]{1,0:T(8,128)(2,1)S(1)}, u32[]{:S(2)}, u32[]{:S(2)}) collective-permute-start(bf16[16,1536]{1,0:T(8,128)(2,1)S(1)} %slice.133), channel_id=1, source_target_pairs={{0,8},{8,16},{16,24},{24,0},{1,9},{9,17},{17,25},{25,1},{2,10},{10... | collective-permute-start | bytes 147464 | tf_op jit(solution)/shard_map/ppermute | solution.py:18
  120.5 5.4 %collective-permute-start.29 = (bf16[16,1536]{1,0:T(8,128)(2,1)S(1)}, bf16[16,1536]{1,0:T(8,128)(2,1)S(1)}, u32[]{:S(2)}, u32[]{:S(2)}) collective-permute-start(bf16[16,1536]{1,0:T(8,128)(2,1)S(1)} %slice.134), channel_id=1, source_target_pairs={{0,24},{8,0},{16,8},{24,16},{1,25},{9,1},{17,9},{25,17},{2,26},{10... | collective-permute-start | bytes 147464 | tf_op jit(solution)/shard_map/ppermute | solution.py:18
  122.6 11.2 %collective-permute-start.38 = (bf16[4,16,3072]{2,1,0:T(8,128)(2,1)S(1)}, bf16[4,16,3072]{2,1,0:T(8,128)(2,1)S(1)}, u32[]{:S(2)}, u32[]{:S(2)}) collective-permute-start(bf16[4,16,3072]{2,1,0:T(8,128)(2,1)S(1)} %pad_maximum_fusion.3.refs_7_), channel_id=1, source_target_pairs={{0,8},{8,16},{16,24},{24,0},{1,9},{9,17},{17,25},{25,1},{2,10},{10... | collective-permute-start | bytes 1179656 | tf_op jit(solution)/shard_map/ppermute | solution.py:18
  122.7 11.1 %collective-permute-start.39 = (bf16[4,16,3072]{2,1,0:T(8,128)(2,1)S(1)}, bf16[4,16,3072]{2,1,0:T(8,128)(2,1)S(1)}, u32[]{:S(2)}, u32[]{:S(2)}) collective-permute-start(bf16[4,16,3072]{2,1,0:T(8,128)(2,1)S(1)} %pad_maximum_fusion.3.refs_7_), channel_id=1, source_target_pairs={{0,24},{8,0},{16,8},{24,16},{1,25},{9,1},{17,9},{25,17},{2,26},{10... | collective-permute-start | bytes 1179656 | tf_op jit(solution)/shard_map/ppermute | solution.py:18
  126.0 11.2 %collective-permute-start.30 = (bf16[4,16,3072]{2,1,0:T(8,128)(2,1)S(1)}, bf16[4,16,3072]{2,1,0:T(8,128)(2,1)S(1)}, u32[]{:S(2)}, u32[]{:S(2)}) collective-permute-start(bf16[4,16,3072]{2,1,0:T(8,128)(2,1)S(1)} %pad_maximum_fusion.2.refs_2_), channel_id=1, source_target_pairs={{0,32},{32,64},{64,96},{96,0},{1,33},{33,65},{65,97},{97,1},{2,34}... | collective-permute-start | bytes 1179656 | tf_op jit(solution)/shard_map/ppermute | solution.py:18
  126.0 11.2 %collective-permute-start.31 = (bf16[4,16,3072]{2,1,0:T(8,128)(2,1)S(1)}, bf16[4,16,3072]{2,1,0:T(8,128)(2,1)S(1)}, u32[]{:S(2)}, u32[]{:S(2)}) collective-permute-start(bf16[4,16,3072]{2,1,0:T(8,128)(2,1)S(1)} %pad_maximum_fusion.2.refs_2_), channel_id=1, source_target_pairs={{0,96},{32,0},{64,32},{96,64},{1,97},{33,1},{65,33},{97,65},{2,98}... | collective-permute-start | bytes 1179656 | tf_op jit(solution)/shard_map/ppermute | solution.py:18
  133.7 7.0 %collective-permute-start.40 = (bf16[2,16,3072]{2,1,0:T(8,128)(2,1)S(1)}, bf16[2,16,3072]{2,1,0:T(8,128)(2,1)S(1)}, u32[]{:S(2)}, u32[]{:S(2)}) collective-permute-start(bf16[2,16,3072]{2,1,0:T(8,128)(2,1)S(1)} %slice.139), channel_id=1, source_target_pairs={{0,8},{8,16},{16,24},{24,0},{1,9},{9,17},{17,25},{25,1},{2,10},{10... | collective-permute-start | bytes 589832 | tf_op jit(solution)/shard_map/ppermute | solution.py:18
  133.9 6.8 %collective-permute-start.41 = (bf16[2,16,3072]{2,1,0:T(8,128)(2,1)S(1)}, bf16[2,16,3072]{2,1,0:T(8,128)(2,1)S(1)}, u32[]{:S(2)}, u32[]{:S(2)}) collective-permute-start(bf16[2,16,3072]{2,1,0:T(8,128)(2,1)S(1)} %slice.140), channel_id=1, source_target_pairs={{0,24},{8,0},{16,8},{24,16},{1,25},{9,1},{17,9},{25,17},{2,26},{10... | collective-permute-start | bytes 589832 | tf_op jit(solution)/shard_map/ppermute | solution.py:18
  137.2 6.9 %collective-permute-start.32 = (bf16[2,16,3072]{2,1,0:T(8,128)(2,1)S(1)}, bf16[2,16,3072]{2,1,0:T(8,128)(2,1)S(1)}, u32[]{:S(2)}, u32[]{:S(2)}) collective-permute-start(bf16[2,16,3072]{2,1,0:T(8,128)(2,1)S(1)} %slice.135), channel_id=1, source_target_pairs={{0,32},{32,64},{64,96},{96,0},{1,33},{33,65},{65,97},{97,1},{2,34}... | collective-permute-start | bytes 589832 | tf_op jit(solution)/shard_map/ppermute | solution.py:18
  137.3 6.8 %collective-permute-start.33 = (bf16[2,16,3072]{2,1,0:T(8,128)(2,1)S(1)}, bf16[2,16,3072]{2,1,0:T(8,128)(2,1)S(1)}, u32[]{:S(2)}, u32[]{:S(2)}) collective-permute-start(bf16[2,16,3072]{2,1,0:T(8,128)(2,1)S(1)} %slice.136), channel_id=1, source_target_pairs={{0,96},{32,0},{64,32},{96,64},{1,97},{33,1},{65,33},{97,65},{2,98}... | collective-permute-start | bytes 589832 | tf_op jit(solution)/shard_map/ppermute | solution.py:18
  144.1 3.7 %copy-start.6 = (bf16[8,1,192,3072]{3,2,1,0:T(8,128)(2,1)S(1)}, bf16[8,1,192,3072]{3,2,1,0:T(8,128)(2,1)}, u32[]{:S(2)}) copy-start(bf16[8,1,192,3072]{3,2,1,0:T(8,128)(2,1)} %param.6) | copy-start | bytes 28311556
  163.0 2.4 %collective-permute-start.42 = (bf16[4,192,512]{2,1,0:T(8,128)(2,1)S(1)}, bf16[4,192,512]{2,1,0:T(8,128)(2,1)S(1)}, u32[]{:S(2)}, u32[]{:S(2)}) collective-permute-start(bf16[4,192,512]{2,1,0:T(8,128)(2,1)S(1)} %get-tuple-element.46), channel_id=1, source_target_pairs={{0,1},{1,0},{2,3},{3,2},{4,5},{5,4},{6,7},{7,6},{8,9},{9,8},{10,11... | collective-permute-start | bytes 2359304 | tf_op jit(solution)/shard_map/ppermute | solution.py:22
  165.7 9.4 %collective-permute-start.43 = (bf16[192,512]{1,0:T(8,128)(2,1)S(1)}, bf16[192,512]{1,0:T(8,128)(2,1)S(1)}, u32[]{:S(2)}, u32[]{:S(2)}) collective-permute-start(bf16[192,512]{1,0:T(8,128)(2,1)S(1)} %get-tuple-element.68), channel_id=1, source_target_pairs={{0,4},{2,6},{4,0},{6,2},{1,5},{3,7},{5,1},{7,3},{8,12},{10,14},{12... | collective-permute-start | bytes 589832 | tf_op jit(solution)/shard_map/ppermute | solution.py:18
  167.8 10.6 %collective-permute-start.44 = (bf16[192,512]{1,0:T(8,128)(2,1)S(1)}, bf16[192,512]{1,0:T(8,128)(2,1)S(1)}, u32[]{:S(2)}, u32[]{:S(2)}) collective-permute-start(bf16[192,512]{1,0:T(8,128)(2,1)S(1)} %get-tuple-element.70), channel_id=1, source_target_pairs={{0,2},{2,4},{4,6},{6,0},{1,3},{3,5},{5,7},{7,1},{8,10},{10,12},{12... | collective-permute-start | bytes 589832 | tf_op jit(solution)/shard_map/ppermute | solution.py:18
  168.7 9.7 %collective-permute-start.45 = (bf16[192,512]{1,0:T(8,128)(2,1)S(1)}, bf16[192,512]{1,0:T(8,128)(2,1)S(1)}, u32[]{:S(2)}, u32[]{:S(2)}) collective-permute-start(bf16[192,512]{1,0:T(8,128)(2,1)S(1)} %get-tuple-element.69), channel_id=1, source_target_pairs={{0,6},{2,0},{4,2},{6,4},{1,7},{3,1},{5,3},{7,5},{8,14},{10,8},{12,... | collective-permute-start | bytes 589832 | tf_op jit(solution)/shard_map/ppermute | solution.py:18
  178.6 25.7 %copy-start.3 = (f32[192,512]{1,0:T(8,128)}, f32[192,512]{1,0:T(8,128)S(1)}, u32[]{:S(2)}) copy-start(f32[192,512]{1,0:T(8,128)S(1)} %fusion.1.residual_ref) | copy-start | bytes 1179652
  179.2 5.9 %collective-permute-start.46 = (bf16[192,128]{1,0:T(8,128)(2,1)S(1)}, bf16[192,128]{1,0:T(8,128)(2,1)S(1)}, u32[]{:S(2)}, u32[]{:S(2)}) collective-permute-start(bf16[192,128]{1,0:T(8,128)(2,1)S(1)} %get-tuple-element.48), channel_id=1, source_target_pairs={{0,8},{8,16},{16,24},{24,0},{1,9},{9,17},{17,25},{25,1},{2,10},{10... | collective-permute-start | bytes 147464 | tf_op jit(solution)/shard_map/ppermute | solution.py:18
  179.3 6.6 %collective-permute-start.47 = (bf16[192,128]{1,0:T(8,128)(2,1)S(1)}, bf16[192,128]{1,0:T(8,128)(2,1)S(1)}, u32[]{:S(2)}, u32[]{:S(2)}) collective-permute-start(bf16[192,128]{1,0:T(8,128)(2,1)S(1)} %get-tuple-element.49), channel_id=1, source_target_pairs={{0,16},{8,24},{16,0},{24,8},{1,17},{9,25},{17,1},{25,9},{2,18},{10... | collective-permute-start | bytes 147464 | tf_op jit(solution)/shard_map/ppermute | solution.py:18
  183.2 4.1 %collective-permute-start.48 = (bf16[192,128]{1,0:T(8,128)(2,1)S(1)}, bf16[192,128]{1,0:T(8,128)(2,1)S(1)}, u32[]{:S(2)}, u32[]{:S(2)}) collective-permute-start(bf16[192,128]{1,0:T(8,128)(2,1)S(1)} %get-tuple-element.50), channel_id=1, source_target_pairs={{0,24},{8,0},{16,8},{24,16},{1,25},{9,1},{17,9},{25,17},{2,26},{10... | collective-permute-start | bytes 147464 | tf_op jit(solution)/shard_map/ppermute | solution.py:18
  188.1 5.7 %collective-permute-start.49 = (bf16[32,768]{1,0:T(8,128)(2,1)S(1)}, bf16[32,768]{1,0:T(8,128)(2,1)S(1)}, u32[]{:S(2)}, u32[]{:S(2)}) collective-permute-start(bf16[32,768]{1,0:T(8,128)(2,1)S(1)} %get-tuple-element.52), channel_id=1, source_target_pairs={{0,32},{32,64},{64,96},{96,0},{1,33},{33,65},{65,97},{97,1},{2,34}... | collective-permute-start | bytes 147464 | tf_op jit(solution)/shard_map/ppermute | solution.py:18
  188.1 7.4 %collective-permute-start.50 = (bf16[32,768]{1,0:T(8,128)(2,1)S(1)}, bf16[32,768]{1,0:T(8,128)(2,1)S(1)}, u32[]{:S(2)}, u32[]{:S(2)}) collective-permute-start(bf16[32,768]{1,0:T(8,128)(2,1)S(1)} %get-tuple-element.53), channel_id=1, source_target_pairs={{0,64},{32,96},{64,0},{96,32},{1,65},{33,97},{65,1},{97,33},{2,66}... | collective-permute-start | bytes 147464 | tf_op jit(solution)/shard_map/ppermute | solution.py:18
  192.9 4.1 %collective-permute-start.51 = (bf16[32,768]{1,0:T(8,128)(2,1)S(1)}, bf16[32,768]{1,0:T(8,128)(2,1)S(1)}, u32[]{:S(2)}, u32[]{:S(2)}) collective-permute-start(bf16[32,768]{1,0:T(8,128)(2,1)S(1)} %get-tuple-element.54), channel_id=1, source_target_pairs={{0,96},{32,0},{64,32},{96,64},{1,97},{33,1},{65,33},{97,65},{2,98}... | collective-permute-start | bytes 147464 | tf_op jit(solution)/shard_map/ppermute | solution.py:18
  204.3 5.9 %collective-permute-start.52 = (bf16[32,768]{1,0:T(8,128)(2,1)S(1)}, bf16[32,768]{1,0:T(8,128)(2,1)S(1)}, u32[]{:S(2)}, u32[]{:S(2)}) collective-permute-start(bf16[32,768]{1,0:T(8,128)(2,1)S(1)} %get-tuple-element.76), channel_id=1, source_target_pairs={{0,32},{32,64},{64,96},{96,0},{1,33},{33,65},{65,97},{97,1},{2,34}... | collective-permute-start | bytes 147464 | tf_op jit(solution)/shard_map/ppermute | solution.py:18
  204.4 5.8 %collective-permute-start.53 = (bf16[32,768]{1,0:T(8,128)(2,1)S(1)}, bf16[32,768]{1,0:T(8,128)(2,1)S(1)}, u32[]{:S(2)}, u32[]{:S(2)}) collective-permute-start(bf16[32,768]{1,0:T(8,128)(2,1)S(1)} %get-tuple-element.75), channel_id=1, source_target_pairs={{0,64},{32,96},{64,0},{96,32},{1,65},{33,97},{65,1},{97,33},{2,66}... | collective-permute-start | bytes 147464 | tf_op jit(solution)/shard_map/ppermute | solution.py:18
  207.0 4.1 %collective-permute-start.54 = (bf16[32,768]{1,0:T(8,128)(2,1)S(1)}, bf16[32,768]{1,0:T(8,128)(2,1)S(1)}, u32[]{:S(2)}, u32[]{:S(2)}) collective-permute-start(bf16[32,768]{1,0:T(8,128)(2,1)S(1)} %get-tuple-element.74), channel_id=1, source_target_pairs={{0,96},{32,0},{64,32},{96,64},{1,97},{33,1},{65,33},{97,65},{2,98}... | collective-permute-start | bytes 147464 | tf_op jit(solution)/shard_map/ppermute | solution.py:18
  211.9 5.4 %collective-permute-start.55 = (bf16[192,128]{1,0:T(8,128)(2,1)S(1)}, bf16[192,128]{1,0:T(8,128)(2,1)S(1)}, u32[]{:S(2)}, u32[]{:S(2)}) collective-permute-start(bf16[192,128]{1,0:T(8,128)(2,1)S(1)} %get-tuple-element.61), channel_id=1, source_target_pairs={{0,8},{8,16},{16,24},{24,0},{1,9},{9,17},{17,25},{25,1},{2,10},{10... | collective-permute-start | bytes 147464 | tf_op jit(solution)/shard_map/ppermute | solution.py:18
  212.2 5.6 %collective-permute-start.56 = (bf16[192,128]{1,0:T(8,128)(2,1)S(1)}, bf16[192,128]{1,0:T(8,128)(2,1)S(1)}, u32[]{:S(2)}, u32[]{:S(2)}) collective-permute-start(bf16[192,128]{1,0:T(8,128)(2,1)S(1)} %get-tuple-element.62), channel_id=1, source_target_pairs={{0,16},{8,24},{16,0},{24,8},{1,17},{9,25},{17,1},{25,9},{2,18},{10... | collective-permute-start | bytes 147464 | tf_op jit(solution)/shard_map/ppermute | solution.py:18
  215.0 4.1 %collective-permute-start.57 = (bf16[192,128]{1,0:T(8,128)(2,1)S(1)}, bf16[192,128]{1,0:T(8,128)(2,1)S(1)}, u32[]{:S(2)}, u32[]{:S(2)}) collective-permute-start(bf16[192,128]{1,0:T(8,128)(2,1)S(1)} %get-tuple-element.63), channel_id=1, source_target_pairs={{0,24},{8,0},{16,8},{24,16},{1,25},{9,1},{17,9},{25,17},{2,26},{10... | collective-permute-start | bytes 147464 | tf_op jit(solution)/shard_map/ppermute | solution.py:18
  (3 other events, 7.5 us)
Sparse Core Ops, SparseCore 0:
  10.8 61.2 all-gather.1

commit v2 on v0

v2 whole, which is shorter than its diff:
```python
import jax
import jax.numpy as jnp
from jax import lax
from jax.experimental import pallas as pl
from jax.experimental.pallas import tpu as pltpu
from jax.sharding import Mesh, PartitionSpec as P

BLOCK = 128
F32 = jnp.float32
BF16 = jnp.bfloat16
SMEM = pl.BlockSpec(memory_space=pltpu.SMEM)
VMEM = pl.BlockSpec(memory_space=pltpu.VMEM)
ANY = pl.BlockSpec(memory_space=pl.ANY)
VMEM_LIMIT = 24 * 1024 * 1024
QUARTER_STEPS = (
    (("z", 1), ("z", 3), ("x", 1), ("x", 3)),
    (("z", 3), ("z", 1), ("x", 3), ("x", 1)),
    (("x", 1), ("x", 3), ("z", 1), ("z", 3)),
    (("x", 3), ("x", 1), ("z", 3), ("z", 1)),
)


def swap(value, axis, mask):
    size = 2 if axis == "core" else 4
    return lax.ppermute(value, axis, [(i, i ^ mask) for i in range(size)])


def whole_call(body, out_shape, scratch_shapes=(), scalars=0, flops=1 << 20):
    def call(*args):
        return pl.pallas_call(
            body,
            in_specs=[SMEM] * scalars + [VMEM] * (len(args) - scalars),
            out_specs=jax.tree.map(lambda _: VMEM, out_shape),
            out_shape=out_shape,
            scratch_shapes=list(scratch_shapes),
            compiler_params=pltpu.CompilerParams(vmem_limit_bytes=VMEM_LIMIT),
            cost_estimate=pl.CostEstimate(flops=flops, bytes_accessed=1 << 20, transcendentals=0),
        )(*args)

    return call


def swap_turn(held, turn):
    return [swap(bundle, *QUARTER_STEPS[p][turn]) for p, bundle in enumerate(held)]


def joined(held, got):
    return [jnp.concatenate(pair) for pair in zip(held, got)]


def gather_swaps(parts, between=lambda turn, held: held):
    held = [part[None] for part in parts]
    for turn in range(3):
        held = between(turn, joined(held, swap_turn(held, turn)))
    return [bundle for pair in zip(held, swap_turn(held, 3)) for bundle in pair]


def source_masks(part, index):
    masks = {"x": 0, "z": 0}
    for turn, (axis, mask) in enumerate(QUARTER_STEPS[part]):
        if index >> turn & 1:
            masks[axis] ^= mask
    return masks["x"], masks["z"]


def hold_kernel(tile_ref, held_ref, sem):
    copy = pltpu.make_async_copy(tile_ref, held_ref, sem)
    copy.start()
    copy.wait()


def hold(tile):
    return pl.pallas_call(
        hold_kernel,
        in_specs=[ANY],
        out_specs=VMEM,
        out_shape=pltpu.VMEM(tile.shape, tile.dtype),
        scratch_shapes=[pltpu.SemaphoreType.DMA],
        compiler_params=pltpu.CompilerParams(vmem_limit_bytes=1024 * 1024),
    )(tile)


def fill_kernel(by_columns, pos_ref, bundles, filled):
    for part in range(4):
        for index in range(16):
            x_mask, z_mask = source_masks(part, index)
            x, z = pos_ref[0] ^ x_mask, pos_ref[1] ^ z_mask
            piece = bundles[part * 2 + index // 8]
            if by_columns:
                lanes = pl.ds(pl.multiple_of(x * 128, 128), 128)
                for half_block in range(12):
                    filled[(part * 12 + half_block) * 4 + z, :, lanes] = piece[index % 8, half_block]
            else:
                filled[pl.ds((x * 4 + z) * 12 + part * 3, 3)] = piece[index % 8]


def multiply(masks, pos_ref, tile_ref, filled, other_ref, mine_ref):
    def one(turn, carry):
        rows = tile_ref[pos_ref[2] ^ (masks[0] + turn)]
        vectors = filled[...].reshape(rows.shape[1], -1)
        result = jnp.dot(rows, vectors, preferred_element_type=F32).astype(BF16)
        for core in range(2):
            @pl.when(pos_ref[3] == core)
            def _():
                mine_ref[turn] = result[core * 192:(core + 1) * 192]
                other_ref[turn] = result[(1 - core) * 192:(2 - core) * 192]
        return carry

    lax.fori_loop(0, len(masks), one, 0)


def far_product_kernel(by_columns, pos_ref, tile_ref, *rest):
    bundles, (other_ref, mine_ref, filled) = rest[:8], rest[8:]
    fill_kernel(by_columns, pos_ref, bundles, filled)
    multiply((1, 2, 3), pos_ref, tile_ref, filled, other_ref, mine_ref)


def near_product_kernel(pos_ref, tile_ref, filled, other_ref, mine_ref):
    multiply((0,), pos_ref, tile_ref, filled, other_ref, mine_ref)


def product(tile, bundles, pos, by_columns):
    far = jax.ShapeDtypeStruct((3, 192, 512), BF16)
    near = jax.ShapeDtypeStruct((1, 192, 512), BF16)
    filled = jax.ShapeDtypeStruct((192, 16, 512), BF16)
    other, mine, filled = whole_call(
        lambda *refs: far_product_kernel(by_columns, *refs), (far, far, filled), scalars=1, flops=3 << 30
    )(pos, tile, *bundles)
    other_near, mine_near = whole_call(near_product_kernel, (near, near), scalars=1, flops=1 << 30)(pos, tile, filled)
    got = swap(other, "core", 1)
    sent = [(mine[at].astype(F32) + got[at].astype(F32)).astype(BF16) for at in range(3)]
    return sent, mine_near[0].astype(F32) + swap(other_near, "core", 1)[0].astype(F32)


def residual_kernel(pos_ref, before_ref, own_ref, *refs):
    sums, out_ref, column_refs = refs[:3], refs[3], refs[4:]
    total = own_ref[...] + (sums[0][...].astype(F32) + (sums[1][...].astype(F32) + sums[2][...].astype(F32)))
    out_ref[...] = before_ref[...] - total
    for mask in range(4):
        lanes = pl.ds(pl.multiple_of((pos_ref[0] ^ mask) * 128, 128), 128)
        column_refs[mask][...] = out_ref[:, lanes].astype(BF16)


def sums_over_y(sent):
    return [swap(sent[mask - 1], "y", mask) for mask in (1, 2, 3)]


def residual_of(before, near, sums, pos):
    piece = jax.ShapeDtypeStruct((192, 128), BF16)
    out_shape = (jax.ShapeDtypeStruct((192, 512), F32),) + (piece,) * 4
    return whole_call(residual_kernel, out_shape, scalars=1)(pos, before, near, *sums)


def exchange(pieces):
    bundle = jnp.stack([pieces[0]] + [swap(pieces[mask], "x", mask) for mask in (1, 2, 3)])
    return [bundle] + [swap(bundle, "z", mask) for mask in (1, 2, 3)]


def inverse_kernel(pos_ref, lists_ref, inverse_ref, *out_refs):
    panel = pos_ref[2] * 2 + pos_ref[3]
    lane = lax.broadcasted_iota(jnp.int32, (16, 384), 1)
    ids = [lists_ref[0, k] - panel * 24 for k in range(3)]
    row = jnp.where(lane == 0, ids[0], jnp.where(lane == 1, ids[1], ids[2])).astype(F32).astype(BF16)
    for mask in range(4):
        for half_block in range(6):
            at = pl.multiple_of(half_block * 64 + (pos_ref[1] ^ mask) * 16, 16)
            out_refs[mask][half_block * 16:(half_block + 1) * 16, :] = inverse_ref[pl.ds(at, 16), :].astype(BF16)
        out_refs[mask][96:, :] = row


def solve_kernel(last, pos_ref, lists_ref, counts_ref, *refs):
    bundles, inverse_refs, refs = refs[:4], refs[4:6], refs[6:]
    if last:
        before_ref, sent_ref, held, total = refs
    else:
        full_ref, *quarter_refs, held, total = refs
    for z_mask in range(4):
        for x_mask in range(4):
            group = (pos_ref[0] ^ x_mask) * 4 + (pos_ref[1] ^ z_mask)
            held[pl.ds(pl.multiple_of(group * 192, 64), 192), :] = bundles[z_mask][x_mask]
    total[...] = jnp.zeros_like(total)
    for s in range(16):
        ids = [lists_ref[s, k] for k in range(3)]
        picked = jnp.concatenate([held[pl.ds(pl.multiple_of(q * BLOCK, BLOCK), BLOCK), :] for q in ids])
        fix = jnp.dot(inverse_refs[s // 8][s % 8, :96, :], picked, preferred_element_type=F32)
        for k in range(3):
            total[ids[k]] += fix[k * 32:(k + 1) * 32]
    panel = pos_ref[2] * 2 + pos_ref[3]
    for block in range(24):
        mean = total[block] / counts_ref[panel * 24 + block].astype(F32)
        if last:
            mean = (mean + before_ref[block]).astype(BF16)
            for half in range(2):
                at = block * 2 + half
                sent_ref[at // 3, at % 3 * 16:(at % 3 + 1) * 16, :] = mean[half * 16:(half + 1) * 16]
        else:
            full_ref[block] = mean
            for half in range(2):
                quarter_refs[block // 6][block % 6 * 2 + half] = mean[half * 16:(half + 1) * 16].astype(BF16)


def solve(bundles, inverses, lists, counts, pos, before=None):
    last = before is not None
    if last:
        out_shape = jax.ShapeDtypeStruct((16, 48, 128), BF16)
    else:
        out_shape = (jax.ShapeDtypeStruct((24, 32, 128), F32),) + (jax.ShapeDtypeStruct((12, 16, 128), BF16),) * 4
    scratch = [pltpu.VMEM((3072, 128), BF16), pltpu.VMEM((24, 32, 128), F32)]
    args = [pos, lists, counts, *bundles, *inverses] + ([before] if last else [])
    return whole_call(lambda *refs: solve_kernel(last, *refs), out_shape, scratch, scalars=3)(*args)


def join_kernel(start_ref, pieces_ref, out_ref):
    for x in range(4):
        for z in range(4):
            for third in range(3):
                at = slice(third * 64 + z * 16, third * 64 + z * 16 + 16), slice(x * 128, (x + 1) * 128)
                piece = pieces_ref[x * 4 + z, third * 16:(third + 1) * 16, :]
                out_ref[at] = start_ref[at] + piece.astype(F32)


def body(kernel, right_side, initial, local_inverse, block_lists, counts):
    target, start = right_side[0], initial[0]
    pos = jnp.stack([lax.axis_index(name) for name in ("x", "z", "y", "core")]).astype(jnp.int32)
    rows = kernel.reshape(4, 384, 3072)

    piece = jax.ShapeDtypeStruct((112, 384), BF16)
    sent = whole_call(inverse_kernel, (piece,) * 4, scalars=2)(pos, block_lists, local_inverse[0])
    inverse = [sent]

    def between(turn, held):
        if turn == 0:
            inverse.append(swap(jnp.stack(sent[1:3]), "z", 1))
        elif turn == 1:
            inverse.append(swap(jnp.stack([sent[3], inverse[1][1]]), "z", 3))
        else:
            inverse.append(jnp.stack([sent[0], inverse[1][0], inverse[2][0], inverse[2][1]]))
            inverse.append(swap(inverse[3], "x", 1))
        held, inverse[-1] = lax.optimization_barrier((held, inverse[-1]))
        return held

    half = start.astype(BF16).reshape(4, 3, 16, 512)
    bundles = gather_swaps([half[at] for at in range(4)], between)
    tile, bundles = lax.optimization_barrier((hold(rows), bundles))
    far, near = product(tile, bundles, pos, False)
    inverses = jnp.concatenate(inverse[3:])
    inverses = inverses, swap(inverses, "x", 3)
    sums, inverses = lax.optimization_barrier((sums_over_y(far), inverses))
    lists = jnp.concatenate([bundle[:, 96, :3] for bundle in inverses]).astype(jnp.int32)

    residual, *pieces = residual_of(target, near, sums, pos)
    fix, *quarters = solve(exchange(pieces), inverses, lists, counts, pos)
    held = []

    def between(turn, parts):
        if turn == 2:
            tied = lax.optimization_barrier((parts, rows))
            held.append(tied[1])
            return tied[0]
        return parts

    bundles = gather_swaps(quarters, between)
    tile, bundles = lax.optimization_barrier((hold(held[0]), bundles))
    far, near = product(tile, bundles, pos, True)
    residual, *pieces = residual_of(residual, near, sums_over_y(far), pos)
    sent = solve(exchange(pieces), inverses, lists, counts, pos, fix)
    pieces = lax.all_to_all(sent, ("x", "z"), 0, 0, tiled=True)
    result = whole_call(join_kernel, jax.ShapeDtypeStruct((192, 512), F32))(start, pieces)
    return (result[None], residual[None])


def solution(mesh):
    fine = Mesh(mesh.devices.reshape(4, 4, 4, 2), ("x", "z", "y", "core"))
    row, col = ("x", "z"), ("y", "core")
    return jax.shard_map(
        body,
        mesh=fine,
        in_specs=(
            P(None, row, None, col),
            P(col, row, None),
            P(col, row, None),
            P(row + col, None, None),
            P(row + col, None),
            P(),
        ),
        out_specs=(P(col, row, None), P(col, row, None)),
        check_vma=False,
    )
```

time: 504 us -> 190 us (0.38)
  waiting for transfers between devices: 426 us -> 65 us
  starting transfers between devices: 0.51 us -> 76.6 us
  matrix products: 32.4 us -> 0 us
  Pallas kernels: 0 us -> 21.8 us
  between operations: 14.3 us -> 1.06 us
  blocking collectives: 0 us -> 12.8 us
  local copies, waits for them, and re-layouts: 21.1 us -> 9.44 us
  other arithmetic: 9.26 us -> 2.4 us
    reduce_scatter x4 -> x0, waiting for transfers between devices: 230 us -> none  [the longest x2 160 us: owner_fixes(): lax.psum_scatter(corrections(current_residual), 'row', scatter_dimension=...]
    all_gather x4 -> x0, waiting for transfers between devices: 196 us -> none  [the longest x2 100 us: apply_kernel(): lax.all_gather(current.astype(jnp.bfloat16), 'row', axis=0, tiled=True)]
    ppermute x0 -> x58, starting transfers between devices: none -> 76.6 us  [swap(): return lax.ppermute(value, axis, [(i, i ^ mask) for i in range(size)])]
    ppermute x0 -> x58, waiting for transfers between devices: none -> 65 us  [swap(): return lax.ppermute(value, axis, [(i, i ^ mask) for i in range(size)])]
    dot_general x6 -> x0, matrix products: 32.4 us -> none  [the longest x2 21.4 us: add_columns(): return jnp.dot(kernel_tile, shard_rows, preferred_element_type=jnp.float32)]
    pallas_call x0 -> x12, Pallas kernels: none -> 21.8 us  [the longest x10 20.5 us: call(): pl.pallas_call(body, in_specs=[SMEM] * scalars + [VMEM] * (len(args) - sc...]
    reshape x5 -> x0, local copies, waits for them, and re-layouts: 15 us -> none  [the longest x2 13.7 us: corrections(): return summed.reshape(panel_rows, rhs_width)]
    all_to_all x0 -> x1, blocking collectives: none -> 12.8 us  [body(): pieces = lax.all_to_all(sent, ('x', 'z'), 0, 0, tiled=True)]
  transfers between devices with their start and end apart: 8 -> 58, of which waited for: 8 -> 33; matrix products, arithmetic and copies ran while one was open for 0% -> 1% of each run, Pallas kernels for 0% -> 3%
where the time goes in v2:
time: 190 us; the launch traced here: 189 us
  starting transfers between devices  76.6 us (40%)
  waiting for transfers between devices  65 us (34%)
  Pallas kernels  21.8 us (11%)
  blocking collectives  12.8 us (7%)
  local copies, waits for them, and re-layouts  9.44 us (5%)
  other arithmetic  2.4 us (1%)
    ppermute x58, starting transfers between devices, swap(): return lax.ppermute(value, axis, [(i, i ^ mask) for i in range(size)])  76.6 us
    ppermute x58, waiting for transfers between devices, swap(): return lax.ppermute(value, axis, [(i, i ^ mask) for i in range(size)])  65 us
    pallas_call x10, Pallas kernels, call(): pl.pallas_call(body, in_specs=[SMEM] * scalars + [VMEM] * (len(args) - sc...  20.5 us
    all_to_all x1, blocking collectives, body(): pieces = lax.all_to_all(sent, ('x', 'z'), 0, 0, tiled=True)  12.8 us
    unnamed x14, local copies, waits for them, and re-layouts  9.1 us
  transfers between devices with their start and end apart: 58, of which 33 were waited for; matrix products, arithmetic and copies ran while one was open for 1% of the time, Pallas kernels for 3%

profile of v2, /device:TPU:0, one launch (start us, length us, event | category | flops | bytes accessed | tf_op | source)
XLA Modules:
  0.0 189.2 jit_solution(3430861477314360450)
XLA Ops:
  0.6 1.0 bitcast_convert_fusion
  1.7 1.7 collective-permute-start.2
  3.3 2.1 %collective-permute-start.3 = (bf16[1,3,16,512]{3,2,1,0:T(8,128)(2,1)S(1)}, bf16[1,3,16,512]{3,2,1,0:T(8,128)(2,1)S(1)}, u32[]{:S(2)}, u32[]{:S(2)}) collective-permute-start(bf16[1,3,16,512]{3,2,1,0:T(8,128)(2,1)S(1)} %bitcast.82), channel_id=1, source_target_pairs={{0,96},{32,64},{64,32},{96,0},{1,97},{33,65},{65,33},{97,1},{2,98}... | collective-permute-start | bytes 147464 | tf_op jit(solution)/shard_map/ppermute | solution.py:25
  5.4 4.0 %collective-permute-start.1 = (bf16[1,3,16,512]{3,2,1,0:T(8,128)(2,1)S(1)}, bf16[1,3,16,512]{3,2,1,0:T(8,128)(2,1)S(1)}, u32[]{:S(2)}, u32[]{:S(2)}) collective-permute-start(bf16[1,3,16,512]{3,2,1,0:T(8,128)(2,1)S(1)} %bitcast.80), channel_id=1, source_target_pairs={{0,24},{8,16},{16,8},{24,0},{1,25},{9,17},{17,9},{25,1},{2,26},{10... | collective-permute-start | bytes 147464 | tf_op jit(solution)/shard_map/ppermute | solution.py:25
  9.5 1.1 copy-done.3
  11.9 2.1 %collective-permute-start.4 = (bf16[2,112,384]{2,1,0:T(8,128)(2,1)S(1)}, bf16[2,112,384]{2,1,0:T(8,128)(2,1)S(1)}, u32[]{:S(2)}, u32[]{:S(2)}) collective-permute-start(bf16[2,112,384]{2,1,0:T(8,128)(2,1)S(1)} %pad_maximum_fusion.20), channel_id=1, source_target_pairs={{0,8},{8,0},{16,24},{24,16},{1,9},{9,1},{17,25},{25,17},{2,10},{10... | collective-permute-start | bytes 516104 | tf_op jit(solution)/shard_map/ppermute | solution.py:25
  14.1 3.3 %collective-permute-done.4 = bf16[2,112,384]{2,1,0:T(8,128)(2,1)S(1)} collective-permute-done((bf16[2,112,384]{2,1,0:T(8,128)(2,1)S(1)}, bf16[2,112,384]{2,1,0:T(8,128)(2,1)S(1)}, u32[]{:S(2)}, u32[]{:S(2)}) %collective-permute-start.4) | collective-permute-done | bytes 172064 | tf_op jit(solution)/shard_map/ppermute | solution.py:25
  18.0 1.6 collective-permute-start.6
  19.6 1.1 collective-permute-start.7
  20.8 2.6 %collective-permute-start.9 = (bf16[2,112,384]{2,1,0:T(8,128)(2,1)S(1)}, bf16[2,112,384]{2,1,0:T(8,128)(2,1)S(1)}, u32[]{:S(2)}, u32[]{:S(2)}) collective-permute-start(bf16[2,112,384]{2,1,0:T(8,128)(2,1)S(1)} %pad_maximum_fusion.21), channel_id=1, source_target_pairs={{0,24},{8,16},{16,8},{24,0},{1,25},{9,17},{17,9},{25,1},{2,26},{10... | collective-permute-start | bytes 516104 | tf_op jit(solution)/shard_map/ppermute | solution.py:25
  23.4 0.9 collective-permute-done.5
  24.4 1.0 collective-permute-done.7
  25.5 2.0 %collective-permute-done.9 = bf16[2,112,384]{2,1,0:T(8,128)(2,1)S(1)} collective-permute-done((bf16[2,112,384]{2,1,0:T(8,128)(2,1)S(1)}, bf16[2,112,384]{2,1,0:T(8,128)(2,1)S(1)}, u32[]{:S(2)}, u32[]{:S(2)}) %collective-permute-start.9) | collective-permute-done | bytes 172064 | tf_op jit(solution)/shard_map/ppermute | solution.py:25
  27.5 2.0 %collective-permute-start.10 = (bf16[4,3,16,512]{3,2,1,0:T(8,128)(2,1)S(1)}, bf16[4,3,16,512]{3,2,1,0:T(8,128)(2,1)S(1)}, u32[]{:S(2)}, u32[]{:S(2)}) collective-permute-start(bf16[4,3,16,512]{3,2,1,0:T(8,128)(2,1)S(1)} %pad_maximum_fusion.10), channel_id=1, source_target_pairs={{0,32},{32,0},{64,96},{96,64},{1,33},{33,1},{65,97},{97,65},{2,34}... | collective-permute-start | bytes 589832 | tf_op jit(solution)/shard_map/ppermute | solution.py:25
  29.5 2.1 %collective-permute-start.11 = (bf16[4,3,16,512]{3,2,1,0:T(8,128)(2,1)S(1)}, bf16[4,3,16,512]{3,2,1,0:T(8,128)(2,1)S(1)}, u32[]{:S(2)}, u32[]{:S(2)}) collective-permute-start(bf16[4,3,16,512]{3,2,1,0:T(8,128)(2,1)S(1)} %pad_maximum_fusion.11), channel_id=1, source_target_pairs={{0,96},{32,64},{64,32},{96,0},{1,97},{33,65},{65,33},{97,1},{2,98}... | collective-permute-start | bytes 589832 | tf_op jit(solution)/shard_map/ppermute | solution.py:25
  31.6 2.5 %collective-permute-start.13 = (bf16[4,3,16,512]{3,2,1,0:T(8,128)(2,1)S(1)}, bf16[4,3,16,512]{3,2,1,0:T(8,128)(2,1)S(1)}, u32[]{:S(2)}, u32[]{:S(2)}) collective-permute-start(bf16[4,3,16,512]{3,2,1,0:T(8,128)(2,1)S(1)} %pad_maximum_fusion.13), channel_id=1, source_target_pairs={{0,24},{8,16},{16,8},{24,0},{1,25},{9,17},{17,9},{25,1},{2,26},{10... | collective-permute-start | bytes 589832 | tf_op jit(solution)/shard_map/ppermute | solution.py:25
  35.0 1.4 collective-permute-done.11
  37.3 1.2 collective-permute-done.13
  38.5 3.8 %collective-permute-done.14 = bf16[4,112,384]{2,1,0:T(8,128)(2,1)S(1)} collective-permute-done((bf16[4,112,384]{2,1,0:T(8,128)(2,1)S(1)}, bf16[4,112,384]{2,1,0:T(8,128)(2,1)S(1)}, u32[]{:S(2)}, u32[]{:S(2)}) %collective-permute-start.14) | collective-permute-done | bytes 344096 | tf_op jit(solution)/shard_map/ppermute | solution.py:25
  43.5 2.8 %collective-permute-start.18 = (bf16[8,3,16,512]{3,2,1,0:T(8,128)(2,1)S(1)}, bf16[8,3,16,512]{3,2,1,0:T(8,128)(2,1)S(1)}, u32[]{:S(2)}, u32[]{:S(2)}) collective-permute-start(bf16[8,3,16,512]{3,2,1,0:T(8,128)(2,1)S(1)} %pad_maximum_fusion.4.refs_8_), channel_id=1, source_target_pairs={{0,8},{8,0},{16,24},{24,16},{1,9},{9,1},{17,25},{25,17},{2,10},{10... | collective-permute-start | bytes 1179656 | tf_op jit(solution)/shard_map/ppermute | solution.py:25
  46.3 3.7 %copy-done = bf16[8,1,192,3072]{3,2,1,0:T(8,128)(2,1)S(1)} copy-done((bf16[8,1,192,3072]{3,2,1,0:T(8,128)(2,1)S(1)}, bf16[8,1,192,3072]{3,2,1,0:T(8,128)(2,1)}, u32[]{:S(2)}) %copy-start) | copy-done | bytes 9437208
  52.0 5.0 %shard_map.79 = (bf16[3,192,512]{2,1,0:T(8,128)(2,1)S(1)}, bf16[3,192,512]{2,1,0:T(8,128)(2,1)S(1)}, bf16[192,16,512]{2,1,0:T(8,128)(2,1)S(1)}) custom-call(s32[4]{0:T(128)S(1)} %pad_add_fusion.pos_ref.refs_0_, bf16[4,384,3072]{2,1,0:T(8,128)(2,1)S(1)} %shard_map.77.refs_1_.tile_ref, bf16[8,3,16,512]{3,2,1,0:T(8,128)(2,1)S(1)} %pad_maximum_fusion.1.refs_2_, ...), custom_call_target="tpu_custom_call" | custom-call | flops 3221225472 | bytes 1048576 | tf_op jit(solution)/shard_map/pallas_call | solution.py:30
  57.3 2.6 %collective-permute-start.23 = (bf16[8,112,384]{2,1,0:T(8,128)(2,1)S(1)}, bf16[8,112,384]{2,1,0:T(8,128)(2,1)S(1)}, u32[]{:S(2)}, u32[]{:S(2)}) collective-permute-start(bf16[8,112,384]{2,1,0:T(8,128)(2,1)S(1)} %pad_maximum_fusion.refs_7_), channel_id=1, source_target_pairs={{0,96},{32,64},{64,32},{96,0},{1,97},{33,65},{65,33},{97,1},{2,98}... | collective-permute-start | bytes 2064392 | tf_op jit(solution)/shard_map/ppermute | solution.py:25
  59.8 2.0 %shard_map.80 = (bf16[1,192,512]{2,1,0:T(8,128)(2,1)S(1)}, bf16[1,192,512]{2,1,0:T(8,128)(2,1)S(1)}) custom-call(s32[4]{0:T(128)S(1)} %pad_add_fusion.pos_ref.refs_0_, bf16[4,384,3072]{2,1,0:T(8,128)(2,1)S(1)} %shard_map.77.refs_1_.tile_ref, bf16[192,16,512]{2,1,0:T(8,128)(2,1)S(1)} %get-tuple-element.106.filled), custom_call_target="tpu_custom_call" | custom-call | flops 1073741824 | bytes 1048576 | tf_op jit(solution)/shard_map/pallas_call | solution.py:30
  62.2 3.1 %collective-permute-start.22 = (bf16[192,512]{1,0:T(8,128)(2,1)S(1)}, bf16[192,512]{1,0:T(8,128)(2,1)S(1)}, u32[]{:S(2)}, u32[]{:S(2)}) collective-permute-start(bf16[192,512]{1,0:T(8,128)(2,1)S(1)} %get-tuple-element.149), channel_id=1, source_target_pairs={{0,6},{2,4},{4,2},{6,0},{1,7},{3,5},{5,3},{7,1},{8,14},{10,12},{12... | collective-permute-start | bytes 589832 | tf_op jit(solution)/shard_map/ppermute | solution.py:25
  66.5 9.9 %collective-permute-done.23.refs_8_ = bf16[8,112,384]{2,1,0:T(8,128)(2,1)S(1)} collective-permute-done((bf16[8,112,384]{2,1,0:T(8,128)(2,1)S(1)}, bf16[8,112,384]{2,1,0:T(8,128)(2,1)S(1)}, u32[]{:S(2)}, u32[]{:S(2)}) %collective-permute-start.23) | collective-permute-done | bytes 688160 | tf_op jit(solution)/shard_map/ppermute | solution.py:25
  77.2 1.0 collective-permute-start.25
  78.2 3.0 %collective-permute-start.26 = (bf16[192,128]{1,0:T(8,128)(2,1)S(1)}, bf16[192,128]{1,0:T(8,128)(2,1)S(1)}, u32[]{:S(2)}, u32[]{:S(2)}) collective-permute-start(bf16[192,128]{1,0:T(8,128)(2,1)S(1)} %get-tuple-element.115), channel_id=1, source_target_pairs={{0,64},{32,96},{64,0},{96,32},{1,65},{33,97},{65,1},{97,33},{2,66}... | collective-permute-start | bytes 147464 | tf_op jit(solution)/shard_map/ppermute | solution.py:25
  82.0 1.8 collective-permute-done.26
  83.8 2.7 %collective-permute-done.27 = bf16[192,128]{1,0:T(8,128)(2,1)S(1)} collective-permute-done((bf16[192,128]{1,0:T(8,128)(2,1)S(1)}, bf16[192,128]{1,0:T(8,128)(2,1)S(1)}, u32[]{:S(2)}, u32[]{:S(2)}) %collective-permute-start.27) | collective-permute-done | bytes 49184 | tf_op jit(solution)/shard_map/ppermute | solution.py:25
  86.6 2.3 %collective-permute-start.30 = (bf16[4,192,128]{2,1,0:T(8,128)(2,1)S(1)}, bf16[4,192,128]{2,1,0:T(8,128)(2,1)S(1)}, u32[]{:S(2)}, u32[]{:S(2)}) collective-permute-start(bf16[4,192,128]{2,1,0:T(8,128)(2,1)S(1)} %pad_maximum_fusion.14.refs_3_), channel_id=1, source_target_pairs={{0,24},{8,16},{16,8},{24,0},{1,25},{9,17},{17,9},{25,1},{2,26},{10... | collective-permute-start | bytes 589832 | tf_op jit(solution)/shard_map/ppermute | solution.py:25
  88.9 1.6 collective-permute-start.29
  91.1 4.7 %collective-permute-done.30.refs_6_ = bf16[4,192,128]{2,1,0:T(8,128)(2,1)S(1)} collective-permute-done((bf16[4,192,128]{2,1,0:T(8,128)(2,1)S(1)}, bf16[4,192,128]{2,1,0:T(8,128)(2,1)S(1)}, u32[]{:S(2)}, u32[]{:S(2)}) %collective-permute-start.30) | collective-permute-done | bytes 196640 | tf_op jit(solution)/shard_map/ppermute | solution.py:25
  95.8 1.2 collective-permute-done.29.refs_5_
  97.5 1.3 shard_map.82
  98.8 2.2 %collective-permute-start.34 = (bf16[1,12,16,128]{3,2,1,0:T(8,128)(2,1)S(1)}, bf16[1,12,16,128]{3,2,1,0:T(8,128)(2,1)S(1)}, u32[]{:S(2)}, u32[]{:S(2)}) collective-permute-start(bf16[1,12,16,128]{3,2,1,0:T(8,128)(2,1)S(1)} %bitcast.65), channel_id=1, source_target_pairs={{0,24},{8,16},{16,8},{24,0},{1,25},{9,17},{17,9},{25,1},{2,26},{10... | collective-permute-start | bytes 147464 | tf_op jit(solution)/shard_map/ppermute | solution.py:25
  101.0 1.5 collective-permute-start.31
  102.5 1.8 collective-permute-start.40
  105.2 2.7 %collective-permute-start.32 = (bf16[2,12,16,128]{3,2,1,0:T(8,128)(2,1)S(1)}, bf16[2,12,16,128]{3,2,1,0:T(8,128)(2,1)S(1)}, u32[]{:S(2)}, u32[]{:S(2)}) collective-permute-start(bf16[2,12,16,128]{3,2,1,0:T(8,128)(2,1)S(1)} %pad_maximum_fusion.26), channel_id=1, source_target_pairs={{0,24},{8,16},{16,8},{24,0},{1,25},{9,17},{17,9},{25,1},{2,26},{10... | collective-permute-start | bytes 294920 | tf_op jit(solution)/shard_map/ppermute | solution.py:25
  107.8 1.4 collective-permute-start.38
  109.4 2.0 %collective-permute-start.36 = (bf16[4,12,16,128]{3,2,1,0:T(8,128)(2,1)S(1)}, bf16[4,12,16,128]{3,2,1,0:T(8,128)(2,1)S(1)}, u32[]{:S(2)}, u32[]{:S(2)}) collective-permute-start(bf16[4,12,16,128]{3,2,1,0:T(8,128)(2,1)S(1)} %pad_maximum_fusion.16), channel_id=1, source_target_pairs={{0,96},{32,64},{64,32},{96,0},{1,97},{33,65},{65,33},{97,1},{2,98}... | collective-permute-start | bytes 589832 | tf_op jit(solution)/shard_map/ppermute | solution.py:25
  111.4 1.5 collective-permute-start.33
  114.0 1.6 collective-permute-start.42
  117.2 2.3 %collective-permute-done.39 = bf16[4,12,16,128]{3,2,1,0:T(8,128)(2,1)S(1)} collective-permute-done((bf16[4,12,16,128]{3,2,1,0:T(8,128)(2,1)S(1)}, bf16[4,12,16,128]{3,2,1,0:T(8,128)(2,1)S(1)}, u32[]{:S(2)}, u32[]{:S(2)}) %collective-permute-start.39) | collective-permute-done | bytes 196640 | tf_op jit(solution)/shard_map/ppermute | solution.py:25
  119.6 1.4 collective-permute-done.42
  121.0 2.6 %collective-permute-start.43 = (bf16[8,12,16,128]{3,2,1,0:T(8,128)(2,1)S(1)}, bf16[8,12,16,128]{3,2,1,0:T(8,128)(2,1)S(1)}, u32[]{:S(2)}, u32[]{:S(2)}) collective-permute-start(bf16[8,12,16,128]{3,2,1,0:T(8,128)(2,1)S(1)} %pad_maximum_fusion.5.refs_2_), channel_id=1, source_target_pairs={{0,96},{32,64},{64,32},{96,0},{1,97},{33,65},{65,33},{97,1},{2,98}... | collective-permute-start | bytes 1179656 | tf_op jit(solution)/shard_map/ppermute | solution.py:25
  124.5 1.1 collective-permute-start.46
  125.7 3.7 %copy-done.1 = bf16[8,1,192,3072]{3,2,1,0:T(8,128)(2,1)S(1)} copy-done((bf16[8,1,192,3072]{3,2,1,0:T(8,128)(2,1)S(1)}, bf16[8,1,192,3072]{3,2,1,0:T(8,128)(2,1)}, u32[]{:S(2)}) %copy-start.1) | copy-done | bytes 9437208
  130.1 1.4 collective-permute-done.44.refs_5_
  131.5 1.2 collective-permute-done.45.refs_7_
  132.7 5.4 %shard_map.84 = (bf16[3,192,512]{2,1,0:T(8,128)(2,1)S(1)}, bf16[3,192,512]{2,1,0:T(8,128)(2,1)S(1)}, bf16[192,16,512]{2,1,0:T(8,128)(2,1)S(1)}) custom-call(s32[4]{0:T(128)S(1)} %pad_add_fusion.pos_ref.refs_0_, bf16[4,384,3072]{2,1,0:T(8,128)(2,1)S(1)} %shard_map.83.refs_1_.tile_ref, bf16[8,12,16,128]{3,2,1,0:T(8,128)(2,1)S(1)} %pad_maximum_fusion.5.refs_2_, ...), custom_call_target="tpu_custom_call" | custom-call | flops 3221225472 | bytes 1048576 | tf_op jit(solution)/shard_map/pallas_call | solution.py:30
  138.2 2.0 %shard_map.85 = (bf16[1,192,512]{2,1,0:T(8,128)(2,1)S(1)}, bf16[1,192,512]{2,1,0:T(8,128)(2,1)S(1)}) custom-call(s32[4]{0:T(128)S(1)} %pad_add_fusion.pos_ref.refs_0_, bf16[4,384,3072]{2,1,0:T(8,128)(2,1)S(1)} %shard_map.83.refs_1_.tile_ref, bf16[192,16,512]{2,1,0:T(8,128)(2,1)S(1)} %get-tuple-element.135.filled), custom_call_target="tpu_custom_call" | custom-call | flops 1073741824 | bytes 1048576 | tf_op jit(solution)/shard_map/pallas_call | solution.py:30
  140.8 3.1 %collective-permute-start.51 = (bf16[192,512]{1,0:T(8,128)(2,1)S(1)}, bf16[192,512]{1,0:T(8,128)(2,1)S(1)}, u32[]{:S(2)}, u32[]{:S(2)}) collective-permute-start(bf16[192,512]{1,0:T(8,128)(2,1)S(1)} %get-tuple-element.146), channel_id=1, source_target_pairs={{0,6},{2,4},{4,2},{6,0},{1,7},{3,5},{5,3},{7,1},{8,14},{10,12},{12... | collective-permute-start | bytes 589832 | tf_op jit(solution)/shard_map/ppermute | solution.py:25
  145.1 8.2 %collective-permute-done.51.refs_2_ = bf16[192,512]{1,0:T(8,128)(2,1)S(1)} collective-permute-done((bf16[192,512]{1,0:T(8,128)(2,1)S(1)}, bf16[192,512]{1,0:T(8,128)(2,1)S(1)}, u32[]{:S(2)}, u32[]{:S(2)}) %collective-permute-start.51) | collective-permute-done | bytes 196640 | tf_op jit(solution)/shard_map/ppermute | solution.py:25
  154.0 1.5 shard_map.86
  155.4 2.0 %collective-permute-start.52 = (bf16[192,128]{1,0:T(8,128)(2,1)S(1)}, bf16[192,128]{1,0:T(8,128)(2,1)S(1)}, u32[]{:S(2)}, u32[]{:S(2)}) collective-permute-start(bf16[192,128]{1,0:T(8,128)(2,1)S(1)} %get-tuple-element.141), channel_id=1, source_target_pairs={{0,32},{32,0},{64,96},{96,64},{1,33},{33,1},{65,97},{97,65},{2,34}... | collective-permute-start | bytes 147464 | tf_op jit(solution)/shard_map/ppermute | solution.py:25
  158.3 1.9 collective-permute-start.54
  160.2 2.9 %collective-permute-done.53 = bf16[192,128]{1,0:T(8,128)(2,1)S(1)} collective-permute-done((bf16[192,128]{1,0:T(8,128)(2,1)S(1)}, bf16[192,128]{1,0:T(8,128)(2,1)S(1)}, u32[]{:S(2)}, u32[]{:S(2)}) %collective-permute-start.53) | collective-permute-done | bytes 49184 | tf_op jit(solution)/shard_map/ppermute | solution.py:25
  163.6 2.0 %collective-permute-start.57 = (bf16[4,192,128]{2,1,0:T(8,128)(2,1)S(1)}, bf16[4,192,128]{2,1,0:T(8,128)(2,1)S(1)}, u32[]{:S(2)}, u32[]{:S(2)}) collective-permute-start(bf16[4,192,128]{2,1,0:T(8,128)(2,1)S(1)} %pad_maximum_fusion.19.refs_3_), channel_id=1, source_target_pairs={{0,24},{8,16},{16,8},{24,0},{1,25},{9,17},{17,9},{25,1},{2,26},{10... | collective-permute-start | bytes 589832 | tf_op jit(solution)/shard_map/ppermute | solution.py:25
  165.6 1.0 collective-permute-start.56
  166.6 1.2 collective-permute-start.55
  167.8 5.8 %collective-permute-done.57.refs_6_ = bf16[4,192,128]{2,1,0:T(8,128)(2,1)S(1)} collective-permute-done((bf16[4,192,128]{2,1,0:T(8,128)(2,1)S(1)}, bf16[4,192,128]{2,1,0:T(8,128)(2,1)S(1)}, u32[]{:S(2)}, u32[]{:S(2)}) %collective-permute-start.57) | collective-permute-done | bytes 196640 | tf_op jit(solution)/shard_map/ppermute | solution.py:25
  174.3 1.3 shard_map.87
  175.6 12.8 %all_to_all.5.pieces_ref = bf16[16,48,128]{2,1,0:T(8,128)(2,1)S(1)} all-to-all(bf16[16,48,128]{2,1,0:T(8,128)(2,1)S(1)} %shard_map.87), channel_id=1, replica_groups=mesh['x'=4,'z'=4,'y'=4,'core'=2] {'x','z'}, dimensions={0} | all-to-all | bytes 393216 | tf_op jit(solution)/shard_map/all_to_all | solution.py:267
  (124 shorter events, 22.6 us)
Async XLA Ops:
  1.7 12.3 %collective-permute-start.2 = (bf16[1,3,16,512]{3,2,1,0:T(8,128)(2,1)S(1)}, bf16[1,3,16,512]{3,2,1,0:T(8,128)(2,1)S(1)}, u32[]{:S(2)}, u32[]{:S(2)}) collective-permute-start(bf16[1,3,16,512]{3,2,1,0:T(8,128)(2,1)S(1)} %bitcast.84), channel_id=1, source_target_pairs={{0,32},{32,0},{64,96},{96,64},{1,33},{33,1},{65,97},{97,65},{2,34}... | collective-permute-start | bytes 147464 | tf_op jit(solution)/shard_map/ppermute | solution.py:25
  3.3 10.7 %collective-permute-start.3 = (bf16[1,3,16,512]{3,2,1,0:T(8,128)(2,1)S(1)}, bf16[1,3,16,512]{3,2,1,0:T(8,128)(2,1)S(1)}, u32[]{:S(2)}, u32[]{:S(2)}) collective-permute-start(bf16[1,3,16,512]{3,2,1,0:T(8,128)(2,1)S(1)} %bitcast.82), channel_id=1, source_target_pairs={{0,96},{32,64},{64,32},{96,0},{1,97},{33,65},{65,33},{97,1},{2,98}... | collective-permute-start | bytes 147464 | tf_op jit(solution)/shard_map/ppermute | solution.py:25
  5.4 8.6 %collective-permute-start.1 = (bf16[1,3,16,512]{3,2,1,0:T(8,128)(2,1)S(1)}, bf16[1,3,16,512]{3,2,1,0:T(8,128)(2,1)S(1)}, u32[]{:S(2)}, u32[]{:S(2)}) collective-permute-start(bf16[1,3,16,512]{3,2,1,0:T(8,128)(2,1)S(1)} %bitcast.80), channel_id=1, source_target_pairs={{0,24},{8,16},{16,8},{24,0},{1,25},{9,17},{17,9},{25,1},{2,26},{10... | collective-permute-start | bytes 147464 | tf_op jit(solution)/shard_map/ppermute | solution.py:25
  9.5 4.6 %collective-permute-start = (bf16[1,3,16,512]{3,2,1,0:T(8,128)(2,1)S(1)}, bf16[1,3,16,512]{3,2,1,0:T(8,128)(2,1)S(1)}, u32[]{:S(2)}, u32[]{:S(2)}) collective-permute-start(bf16[1,3,16,512]{3,2,1,0:T(8,128)(2,1)S(1)} %bitcast.78), channel_id=1, source_target_pairs={{0,8},{8,0},{16,24},{24,16},{1,9},{9,1},{17,25},{25,17},{2,10},{10... | collective-permute-start | bytes 147464 | tf_op jit(solution)/shard_map/ppermute | solution.py:25
  9.5 1.1 copy-start.3
  11.9 5.5 %collective-permute-start.4 = (bf16[2,112,384]{2,1,0:T(8,128)(2,1)S(1)}, bf16[2,112,384]{2,1,0:T(8,128)(2,1)S(1)}, u32[]{:S(2)}, u32[]{:S(2)}) collective-permute-start(bf16[2,112,384]{2,1,0:T(8,128)(2,1)S(1)} %pad_maximum_fusion.20), channel_id=1, source_target_pairs={{0,8},{8,0},{16,24},{24,16},{1,9},{9,1},{17,25},{25,17},{2,10},{10... | collective-permute-start | bytes 516104 | tf_op jit(solution)/shard_map/ppermute | solution.py:25
  17.4 6.9 %collective-permute-start.5 = (bf16[2,3,16,512]{3,2,1,0:T(8,128)(2,1)S(1)}, bf16[2,3,16,512]{3,2,1,0:T(8,128)(2,1)S(1)}, u32[]{:S(2)}, u32[]{:S(2)}) collective-permute-start(bf16[2,3,16,512]{3,2,1,0:T(8,128)(2,1)S(1)} %pad_maximum_fusion.22), channel_id=1, source_target_pairs={{0,24},{8,16},{16,8},{24,0},{1,25},{9,17},{17,9},{25,1},{2,26},{10... | collective-permute-start | bytes 294920 | tf_op jit(solution)/shard_map/ppermute | solution.py:25
  18.0 6.4 %collective-permute-start.6 = (bf16[2,3,16,512]{3,2,1,0:T(8,128)(2,1)S(1)}, bf16[2,3,16,512]{3,2,1,0:T(8,128)(2,1)S(1)}, u32[]{:S(2)}, u32[]{:S(2)}) collective-permute-start(bf16[2,3,16,512]{3,2,1,0:T(8,128)(2,1)S(1)} %pad_maximum_fusion.23), channel_id=1, source_target_pairs={{0,8},{8,0},{16,24},{24,16},{1,9},{9,1},{17,25},{25,17},{2,10},{10... | collective-permute-start | bytes 294920 | tf_op jit(solution)/shard_map/ppermute | solution.py:25
  19.6 5.8 %collective-permute-start.7 = (bf16[2,3,16,512]{3,2,1,0:T(8,128)(2,1)S(1)}, bf16[2,3,16,512]{3,2,1,0:T(8,128)(2,1)S(1)}, u32[]{:S(2)}, u32[]{:S(2)}) collective-permute-start(bf16[2,3,16,512]{3,2,1,0:T(8,128)(2,1)S(1)} %pad_maximum_fusion.24), channel_id=1, source_target_pairs={{0,96},{32,64},{64,32},{96,0},{1,97},{33,65},{65,33},{97,1},{2,98}... | collective-permute-start | bytes 294920 | tf_op jit(solution)/shard_map/ppermute | solution.py:25
  20.7 4.7 %collective-permute-start.8 = (bf16[2,3,16,512]{3,2,1,0:T(8,128)(2,1)S(1)}, bf16[2,3,16,512]{3,2,1,0:T(8,128)(2,1)S(1)}, u32[]{:S(2)}, u32[]{:S(2)}) collective-permute-start(bf16[2,3,16,512]{3,2,1,0:T(8,128)(2,1)S(1)} %pad_maximum_fusion.25), channel_id=1, source_target_pairs={{0,32},{32,0},{64,96},{96,64},{1,33},{33,1},{65,97},{97,65},{2,34}... | collective-permute-start | bytes 294920 | tf_op jit(solution)/shard_map/ppermute | solution.py:25
  20.8 6.7 %collective-permute-start.9 = (bf16[2,112,384]{2,1,0:T(8,128)(2,1)S(1)}, bf16[2,112,384]{2,1,0:T(8,128)(2,1)S(1)}, u32[]{:S(2)}, u32[]{:S(2)}) collective-permute-start(bf16[2,112,384]{2,1,0:T(8,128)(2,1)S(1)} %pad_maximum_fusion.21), channel_id=1, source_target_pairs={{0,24},{8,16},{16,8},{24,0},{1,25},{9,17},{17,9},{25,1},{2,26},{10... | collective-permute-start | bytes 516104 | tf_op jit(solution)/shard_map/ppermute | solution.py:25
  27.5 7.5 %collective-permute-start.10 = (bf16[4,3,16,512]{3,2,1,0:T(8,128)(2,1)S(1)}, bf16[4,3,16,512]{3,2,1,0:T(8,128)(2,1)S(1)}, u32[]{:S(2)}, u32[]{:S(2)}) collective-permute-start(bf16[4,3,16,512]{3,2,1,0:T(8,128)(2,1)S(1)} %pad_maximum_fusion.10), channel_id=1, source_target_pairs={{0,32},{32,0},{64,96},{96,64},{1,33},{33,1},{65,97},{97,65},{2,34}... | collective-permute-start | bytes 589832 | tf_op jit(solution)/shard_map/ppermute | solution.py:25
  29.5 6.9 %collective-permute-start.11 = (bf16[4,3,16,512]{3,2,1,0:T(8,128)(2,1)S(1)}, bf16[4,3,16,512]{3,2,1,0:T(8,128)(2,1)S(1)}, u32[]{:S(2)}, u32[]{:S(2)}) collective-permute-start(bf16[4,3,16,512]{3,2,1,0:T(8,128)(2,1)S(1)} %pad_maximum_fusion.11), channel_id=1, source_target_pairs={{0,96},{32,64},{64,32},{96,0},{1,97},{33,65},{65,33},{97,1},{2,98}... | collective-permute-start | bytes 589832 | tf_op jit(solution)/shard_map/ppermute | solution.py:25
  31.6 5.7 %collective-permute-start.12 = (bf16[4,3,16,512]{3,2,1,0:T(8,128)(2,1)S(1)}, bf16[4,3,16,512]{3,2,1,0:T(8,128)(2,1)S(1)}, u32[]{:S(2)}, u32[]{:S(2)}) collective-permute-start(bf16[4,3,16,512]{3,2,1,0:T(8,128)(2,1)S(1)} %pad_maximum_fusion.12), channel_id=1, source_target_pairs={{0,8},{8,0},{16,24},{24,16},{1,9},{9,1},{17,25},{25,17},{2,10},{10... | collective-permute-start | bytes 589832 | tf_op jit(solution)/shard_map/ppermute | solution.py:25
  31.6 6.9 %collective-permute-start.13 = (bf16[4,3,16,512]{3,2,1,0:T(8,128)(2,1)S(1)}, bf16[4,3,16,512]{3,2,1,0:T(8,128)(2,1)S(1)}, u32[]{:S(2)}, u32[]{:S(2)}) collective-permute-start(bf16[4,3,16,512]{3,2,1,0:T(8,128)(2,1)S(1)} %pad_maximum_fusion.13), channel_id=1, source_target_pairs={{0,24},{8,16},{16,8},{24,0},{1,25},{9,17},{17,9},{25,1},{2,26},{10... | collective-permute-start | bytes 589832 | tf_op jit(solution)/shard_map/ppermute | solution.py:25
  34.2 8.1 %collective-permute-start.14 = (bf16[4,112,384]{2,1,0:T(8,128)(2,1)S(1)}, bf16[4,112,384]{2,1,0:T(8,128)(2,1)S(1)}, u32[]{:S(2)}, u32[]{:S(2)}) collective-permute-start(bf16[4,112,384]{2,1,0:T(8,128)(2,1)S(1)} %pad_maximum_fusion.9), channel_id=1, source_target_pairs={{0,32},{32,0},{64,96},{96,64},{1,33},{33,1},{65,97},{97,65},{2,34}... | collective-permute-start | bytes 1032200 | tf_op jit(solution)/shard_map/ppermute | solution.py:25
  42.3 9.0 %collective-permute-start.15 = (bf16[8,3,16,512]{3,2,1,0:T(8,128)(2,1)S(1)}, bf16[8,3,16,512]{3,2,1,0:T(8,128)(2,1)S(1)}, u32[]{:S(2)}, u32[]{:S(2)}) collective-permute-start(bf16[8,3,16,512]{3,2,1,0:T(8,128)(2,1)S(1)} %pad_maximum_fusion.1.refs_2_), channel_id=1, source_target_pairs={{0,96},{32,64},{64,32},{96,0},{1,97},{33,65},{65,33},{97,1},{2,98}... | collective-permute-start | bytes 1179656 | tf_op jit(solution)/shard_map/ppermute | solution.py:25
  42.7 8.5 %collective-permute-start.16 = (bf16[8,3,16,512]{3,2,1,0:T(8,128)(2,1)S(1)}, bf16[8,3,16,512]{3,2,1,0:T(8,128)(2,1)S(1)}, u32[]{:S(2)}, u32[]{:S(2)}) collective-permute-start(bf16[8,3,16,512]{3,2,1,0:T(8,128)(2,1)S(1)} %pad_maximum_fusion.2.refs_4_), channel_id=1, source_target_pairs={{0,32},{32,0},{64,96},{96,64},{1,33},{33,1},{65,97},{97,65},{2,34}... | collective-permute-start | bytes 1179656 | tf_op jit(solution)/shard_map/ppermute | solution.py:25
  42.7 9.0 %collective-permute-start.17 = (bf16[8,3,16,512]{3,2,1,0:T(8,128)(2,1)S(1)}, bf16[8,3,16,512]{3,2,1,0:T(8,128)(2,1)S(1)}, u32[]{:S(2)}, u32[]{:S(2)}) collective-permute-start(bf16[8,3,16,512]{3,2,1,0:T(8,128)(2,1)S(1)} %pad_maximum_fusion.3.refs_6_), channel_id=1, source_target_pairs={{0,24},{8,16},{16,8},{24,0},{1,25},{9,17},{17,9},{25,1},{2,26},{10... | collective-permute-start | bytes 1179656 | tf_op jit(solution)/shard_map/ppermute | solution.py:25
  43.5 8.6 %collective-permute-start.18 = (bf16[8,3,16,512]{3,2,1,0:T(8,128)(2,1)S(1)}, bf16[8,3,16,512]{3,2,1,0:T(8,128)(2,1)S(1)}, u32[]{:S(2)}, u32[]{:S(2)}) collective-permute-start(bf16[8,3,16,512]{3,2,1,0:T(8,128)(2,1)S(1)} %pad_maximum_fusion.4.refs_8_), channel_id=1, source_target_pairs={{0,8},{8,0},{16,24},{24,16},{1,9},{9,1},{17,25},{25,17},{2,10},{10... | collective-permute-start | bytes 1179656 | tf_op jit(solution)/shard_map/ppermute | solution.py:25
  46.3 3.7 %copy-start = (bf16[8,1,192,3072]{3,2,1,0:T(8,128)(2,1)S(1)}, bf16[8,1,192,3072]{3,2,1,0:T(8,128)(2,1)}, u32[]{:S(2)}) copy-start(bf16[8,1,192,3072]{3,2,1,0:T(8,128)(2,1)} %param.6) | copy-start | bytes 28311556
  57.1 19.4 %copy-start.4 = (f32[1,192,512]{2,1,0:T(8,128)S(1)}, f32[1,192,512]{2,1,0:T(8,128)}, u32[]{:S(2)}) copy-start(f32[1,192,512]{2,1,0:T(8,128)} %param.7) | copy-start | bytes 1179652
  57.1 40.5 %copy-start.5 = (s32[192]{0:T(256)S(1)}, s32[192]{0:T(256)}, u32[]{:S(2)}) copy-start(s32[192]{0:T(256)} %refs_2_.3) | copy-start | bytes 2308
  57.1 5.0 %collective-permute-start.19 = (bf16[3,192,512]{2,1,0:T(8,128)(2,1)S(1)}, bf16[3,192,512]{2,1,0:T(8,128)(2,1)S(1)}, u32[]{:S(2)}, u32[]{:S(2)}) collective-permute-start(bf16[3,192,512]{2,1,0:T(8,128)(2,1)S(1)} %get-tuple-element.102), channel_id=1, source_target_pairs={{0,1},{1,0},{2,3},{3,2},{4,5},{5,4},{6,7},{7,6},{8,9},{9,8},{10,11... | collective-permute-start | bytes 1769480 | tf_op jit(solution)/shard_map/ppermute | solution.py:25
  57.3 19.1 %collective-permute-start.23 = (bf16[8,112,384]{2,1,0:T(8,128)(2,1)S(1)}, bf16[8,112,384]{2,1,0:T(8,128)(2,1)S(1)}, u32[]{:S(2)}, u32[]{:S(2)}) collective-permute-start(bf16[8,112,384]{2,1,0:T(8,128)(2,1)S(1)} %pad_maximum_fusion.refs_7_), channel_id=1, source_target_pairs={{0,96},{32,64},{64,32},{96,0},{1,97},{33,65},{65,33},{97,1},{2,98}... | collective-permute-start | bytes 2064392 | tf_op jit(solution)/shard_map/ppermute | solution.py:25
  61.8 4.6 %collective-permute-start.24 = (bf16[1,192,512]{2,1,0:T(8,128)(2,1)S(1)}, bf16[1,192,512]{2,1,0:T(8,128)(2,1)S(1)}, u32[]{:S(2)}, u32[]{:S(2)}) collective-permute-start(bf16[1,192,512]{2,1,0:T(8,128)(2,1)S(1)} %get-tuple-element.108), channel_id=1, source_target_pairs={{0,1},{1,0},{2,3},{3,2},{4,5},{5,4},{6,7},{7,6},{8,9},{9,8},{10,11... | collective-permute-start | bytes 589832 | tf_op jit(solution)/shard_map/ppermute | solution.py:25
  62.2 14.2 %collective-permute-start.22 = (bf16[192,512]{1,0:T(8,128)(2,1)S(1)}, bf16[192,512]{1,0:T(8,128)(2,1)S(1)}, u32[]{:S(2)}, u32[]{:S(2)}) collective-permute-start(bf16[192,512]{1,0:T(8,128)(2,1)S(1)} %get-tuple-element.149), channel_id=1, source_target_pairs={{0,6},{2,4},{4,2},{6,0},{1,7},{3,5},{5,3},{7,1},{8,14},{10,12},{12... | collective-permute-start | bytes 589832 | tf_op jit(solution)/shard_map/ppermute | solution.py:25
  65.3 11.1 %collective-permute-start.21 = (bf16[192,512]{1,0:T(8,128)(2,1)S(1)}, bf16[192,512]{1,0:T(8,128)(2,1)S(1)}, u32[]{:S(2)}, u32[]{:S(2)}) collective-permute-start(bf16[192,512]{1,0:T(8,128)(2,1)S(1)} %get-tuple-element.150), channel_id=1, source_target_pairs={{0,4},{2,6},{4,0},{6,2},{1,5},{3,7},{5,1},{7,3},{8,12},{10,14},{12... | collective-permute-start | bytes 589832 | tf_op jit(solution)/shard_map/ppermute | solution.py:25
  66.0 10.4 %collective-permute-start.20 = (bf16[192,512]{1,0:T(8,128)(2,1)S(1)}, bf16[192,512]{1,0:T(8,128)(2,1)S(1)}, u32[]{:S(2)}, u32[]{:S(2)}) collective-permute-start(bf16[192,512]{1,0:T(8,128)(2,1)S(1)} %get-tuple-element.151), channel_id=1, source_target_pairs={{0,2},{2,0},{4,6},{6,4},{1,3},{3,1},{5,7},{7,5},{8,10},{10,8},{12,... | collective-permute-start | bytes 589832 | tf_op jit(solution)/shard_map/ppermute | solution.py:25
  77.2 4.8 %collective-permute-start.25 = (bf16[192,128]{1,0:T(8,128)(2,1)S(1)}, bf16[192,128]{1,0:T(8,128)(2,1)S(1)}, u32[]{:S(2)}, u32[]{:S(2)}) collective-permute-start(bf16[192,128]{1,0:T(8,128)(2,1)S(1)} %get-tuple-element.114), channel_id=1, source_target_pairs={{0,32},{32,0},{64,96},{96,64},{1,33},{33,1},{65,97},{97,65},{2,34}... | collective-permute-start | bytes 147464 | tf_op jit(solution)/shard_map/ppermute | solution.py:25
  78.2 5.6 %collective-permute-start.26 = (bf16[192,128]{1,0:T(8,128)(2,1)S(1)}, bf16[192,128]{1,0:T(8,128)(2,1)S(1)}, u32[]{:S(2)}, u32[]{:S(2)}) collective-permute-start(bf16[192,128]{1,0:T(8,128)(2,1)S(1)} %get-tuple-element.115), channel_id=1, source_target_pairs={{0,64},{32,96},{64,0},{96,32},{1,65},{33,97},{65,1},{97,33},{2,66}... | collective-permute-start | bytes 147464 | tf_op jit(solution)/shard_map/ppermute | solution.py:25
  81.2 5.3 %collective-permute-start.27 = (bf16[192,128]{1,0:T(8,128)(2,1)S(1)}, bf16[192,128]{1,0:T(8,128)(2,1)S(1)}, u32[]{:S(2)}, u32[]{:S(2)}) collective-permute-start(bf16[192,128]{1,0:T(8,128)(2,1)S(1)} %get-tuple-element.116), channel_id=1, source_target_pairs={{0,96},{32,64},{64,32},{96,0},{1,97},{33,65},{65,33},{97,1},{2,98}... | collective-permute-start | bytes 147464 | tf_op jit(solution)/shard_map/ppermute | solution.py:25
  86.6 9.2 %collective-permute-start.30 = (bf16[4,192,128]{2,1,0:T(8,128)(2,1)S(1)}, bf16[4,192,128]{2,1,0:T(8,128)(2,1)S(1)}, u32[]{:S(2)}, u32[]{:S(2)}) collective-permute-start(bf16[4,192,128]{2,1,0:T(8,128)(2,1)S(1)} %pad_maximum_fusion.14.refs_3_), channel_id=1, source_target_pairs={{0,24},{8,16},{16,8},{24,0},{1,25},{9,17},{17,9},{25,1},{2,26},{10... | collective-permute-start | bytes 589832 | tf_op jit(solution)/shard_map/ppermute | solution.py:25
  88.9 8.1 %collective-permute-start.29 = (bf16[4,192,128]{2,1,0:T(8,128)(2,1)S(1)}, bf16[4,192,128]{2,1,0:T(8,128)(2,1)S(1)}, u32[]{:S(2)}, u32[]{:S(2)}) collective-permute-start(bf16[4,192,128]{2,1,0:T(8,128)(2,1)S(1)} %pad_maximum_fusion.14.refs_3_), channel_id=1, source_target_pairs={{0,16},{8,24},{16,0},{24,8},{1,17},{9,25},{17,1},{25,9},{2,18},{10... | collective-permute-start | bytes 589832 | tf_op jit(solution)/shard_map/ppermute | solution.py:25
  90.4 7.1 %collective-permute-start.28 = (bf16[4,192,128]{2,1,0:T(8,128)(2,1)S(1)}, bf16[4,192,128]{2,1,0:T(8,128)(2,1)S(1)}, u32[]{:S(2)}, u32[]{:S(2)}) collective-permute-start(bf16[4,192,128]{2,1,0:T(8,128)(2,1)S(1)} %pad_maximum_fusion.14.refs_3_), channel_id=1, source_target_pairs={{0,8},{8,0},{16,24},{24,16},{1,9},{9,1},{17,25},{25,17},{2,10},{10... | collective-permute-start | bytes 589832 | tf_op jit(solution)/shard_map/ppermute | solution.py:25
  98.8 5.5 %collective-permute-start.34 = (bf16[1,12,16,128]{3,2,1,0:T(8,128)(2,1)S(1)}, bf16[1,12,16,128]{3,2,1,0:T(8,128)(2,1)S(1)}, u32[]{:S(2)}, u32[]{:S(2)}) collective-permute-start(bf16[1,12,16,128]{3,2,1,0:T(8,128)(2,1)S(1)} %bitcast.65), channel_id=1, source_target_pairs={{0,24},{8,16},{16,8},{24,0},{1,25},{9,17},{17,9},{25,1},{2,26},{10... | collective-permute-start | bytes 147464 | tf_op jit(solution)/shard_map/ppermute | solution.py:25
  101.0 4.1 %collective-permute-start.31 = (bf16[1,12,16,128]{3,2,1,0:T(8,128)(2,1)S(1)}, bf16[1,12,16,128]{3,2,1,0:T(8,128)(2,1)S(1)}, u32[]{:S(2)}, u32[]{:S(2)}) collective-permute-start(bf16[1,12,16,128]{3,2,1,0:T(8,128)(2,1)S(1)} %bitcast.61), channel_id=1, source_target_pairs={{0,8},{8,0},{16,24},{24,16},{1,9},{9,1},{17,25},{25,17},{2,10},{10... | collective-permute-start | bytes 147464 | tf_op jit(solution)/shard_map/ppermute | solution.py:25
  102.5 5.3 %collective-permute-start.37 = (bf16[1,12,16,128]{3,2,1,0:T(8,128)(2,1)S(1)}, bf16[1,12,16,128]{3,2,1,0:T(8,128)(2,1)S(1)}, u32[]{:S(2)}, u32[]{:S(2)}) collective-permute-start(bf16[1,12,16,128]{3,2,1,0:T(8,128)(2,1)S(1)} %bitcast.57), channel_id=1, source_target_pairs={{0,32},{32,0},{64,96},{96,64},{1,33},{33,1},{65,97},{97,65},{2,34}... | collective-permute-start | bytes 147464 | tf_op jit(solution)/shard_map/ppermute | solution.py:25
  102.5 6.7 %collective-permute-start.40 = (bf16[1,12,16,128]{3,2,1,0:T(8,128)(2,1)S(1)}, bf16[1,12,16,128]{3,2,1,0:T(8,128)(2,1)S(1)}, u32[]{:S(2)}, u32[]{:S(2)}) collective-permute-start(bf16[1,12,16,128]{3,2,1,0:T(8,128)(2,1)S(1)} %bitcast.53), channel_id=1, source_target_pairs={{0,96},{32,64},{64,32},{96,0},{1,97},{33,65},{65,33},{97,1},{2,98}... | collective-permute-start | bytes 147464 | tf_op jit(solution)/shard_map/ppermute | solution.py:25
  104.3 5.1 %collective-permute-start.35 = (bf16[2,12,16,128]{3,2,1,0:T(8,128)(2,1)S(1)}, bf16[2,12,16,128]{3,2,1,0:T(8,128)(2,1)S(1)}, u32[]{:S(2)}, u32[]{:S(2)}) collective-permute-start(bf16[2,12,16,128]{3,2,1,0:T(8,128)(2,1)S(1)} %pad_maximum_fusion.27), channel_id=1, source_target_pairs={{0,8},{8,0},{16,24},{24,16},{1,9},{9,1},{17,25},{25,17},{2,10},{10... | collective-permute-start | bytes 294920 | tf_op jit(solution)/shard_map/ppermute | solution.py:25
  105.2 6.2 %collective-permute-start.32 = (bf16[2,12,16,128]{3,2,1,0:T(8,128)(2,1)S(1)}, bf16[2,12,16,128]{3,2,1,0:T(8,128)(2,1)S(1)}, u32[]{:S(2)}, u32[]{:S(2)}) collective-permute-start(bf16[2,12,16,128]{3,2,1,0:T(8,128)(2,1)S(1)} %pad_maximum_fusion.26), channel_id=1, source_target_pairs={{0,24},{8,16},{16,8},{24,0},{1,25},{9,17},{17,9},{25,1},{2,26},{10... | collective-permute-start | bytes 294920 | tf_op jit(solution)/shard_map/ppermute | solution.py:25
  107.8 5.9 %collective-permute-start.38 = (bf16[2,12,16,128]{3,2,1,0:T(8,128)(2,1)S(1)}, bf16[2,12,16,128]{3,2,1,0:T(8,128)(2,1)S(1)}, u32[]{:S(2)}, u32[]{:S(2)}) collective-permute-start(bf16[2,12,16,128]{3,2,1,0:T(8,128)(2,1)S(1)} %pad_maximum_fusion.28), channel_id=1, source_target_pairs={{0,96},{32,64},{64,32},{96,0},{1,97},{33,65},{65,33},{97,1},{2,98}... | collective-permute-start | bytes 294920 | tf_op jit(solution)/shard_map/ppermute | solution.py:25
  109.3 4.7 %collective-permute-start.41 = (bf16[2,12,16,128]{3,2,1,0:T(8,128)(2,1)S(1)}, bf16[2,12,16,128]{3,2,1,0:T(8,128)(2,1)S(1)}, u32[]{:S(2)}, u32[]{:S(2)}) collective-permute-start(bf16[2,12,16,128]{3,2,1,0:T(8,128)(2,1)S(1)} %pad_maximum_fusion.29), channel_id=1, source_target_pairs={{0,32},{32,0},{64,96},{96,64},{1,33},{33,1},{65,97},{97,65},{2,34}... | collective-permute-start | bytes 294920 | tf_op jit(solution)/shard_map/ppermute | solution.py:25
  109.4 7.0 %collective-permute-start.36 = (bf16[4,12,16,128]{3,2,1,0:T(8,128)(2,1)S(1)}, bf16[4,12,16,128]{3,2,1,0:T(8,128)(2,1)S(1)}, u32[]{:S(2)}, u32[]{:S(2)}) collective-permute-start(bf16[4,12,16,128]{3,2,1,0:T(8,128)(2,1)S(1)} %pad_maximum_fusion.16), channel_id=1, source_target_pairs={{0,96},{32,64},{64,32},{96,0},{1,97},{33,65},{65,33},{97,1},{2,98}... | collective-permute-start | bytes 589832 | tf_op jit(solution)/shard_map/ppermute | solution.py:25
  111.4 5.7 %collective-permute-start.33 = (bf16[4,12,16,128]{3,2,1,0:T(8,128)(2,1)S(1)}, bf16[4,12,16,128]{3,2,1,0:T(8,128)(2,1)S(1)}, u32[]{:S(2)}, u32[]{:S(2)}) collective-permute-start(bf16[4,12,16,128]{3,2,1,0:T(8,128)(2,1)S(1)} %pad_maximum_fusion.15), channel_id=1, source_target_pairs={{0,32},{32,0},{64,96},{96,64},{1,33},{33,1},{65,97},{97,65},{2,34}... | collective-permute-start | bytes 589832 | tf_op jit(solution)/shard_map/ppermute | solution.py:25
  113.8 5.8 %collective-permute-start.39 = (bf16[4,12,16,128]{3,2,1,0:T(8,128)(2,1)S(1)}, bf16[4,12,16,128]{3,2,1,0:T(8,128)(2,1)S(1)}, u32[]{:S(2)}, u32[]{:S(2)}) collective-permute-start(bf16[4,12,16,128]{3,2,1,0:T(8,128)(2,1)S(1)} %pad_maximum_fusion.17), channel_id=1, source_target_pairs={{0,8},{8,0},{16,24},{24,16},{1,9},{9,1},{17,25},{25,17},{2,10},{10... | collective-permute-start | bytes 589832 | tf_op jit(solution)/shard_map/ppermute | solution.py:25
  114.0 7.0 %collective-permute-start.42 = (bf16[4,12,16,128]{3,2,1,0:T(8,128)(2,1)S(1)}, bf16[4,12,16,128]{3,2,1,0:T(8,128)(2,1)S(1)}, u32[]{:S(2)}, u32[]{:S(2)}) collective-permute-start(bf16[4,12,16,128]{3,2,1,0:T(8,128)(2,1)S(1)} %pad_maximum_fusion.18), channel_id=1, source_target_pairs={{0,24},{8,16},{16,8},{24,0},{1,25},{9,17},{17,9},{25,1},{2,26},{10... | collective-permute-start | bytes 589832 | tf_op jit(solution)/shard_map/ppermute | solution.py:25
  121.0 9.1 %collective-permute-start.43 = (bf16[8,12,16,128]{3,2,1,0:T(8,128)(2,1)S(1)}, bf16[8,12,16,128]{3,2,1,0:T(8,128)(2,1)S(1)}, u32[]{:S(2)}, u32[]{:S(2)}) collective-permute-start(bf16[8,12,16,128]{3,2,1,0:T(8,128)(2,1)S(1)} %pad_maximum_fusion.5.refs_2_), channel_id=1, source_target_pairs={{0,96},{32,64},{64,32},{96,0},{1,97},{33,65},{65,33},{97,1},{2,98}... | collective-permute-start | bytes 1179656 | tf_op jit(solution)/shard_map/ppermute | solution.py:25
  123.7 7.8 %collective-permute-start.44 = (bf16[8,12,16,128]{3,2,1,0:T(8,128)(2,1)S(1)}, bf16[8,12,16,128]{3,2,1,0:T(8,128)(2,1)S(1)}, u32[]{:S(2)}, u32[]{:S(2)}) collective-permute-start(bf16[8,12,16,128]{3,2,1,0:T(8,128)(2,1)S(1)} %pad_maximum_fusion.6.refs_4_), channel_id=1, source_target_pairs={{0,32},{32,0},{64,96},{96,64},{1,33},{33,1},{65,97},{97,65},{2,34}... | collective-permute-start | bytes 1179656 | tf_op jit(solution)/shard_map/ppermute | solution.py:25
  123.7 9.0 %collective-permute-start.45 = (bf16[8,12,16,128]{3,2,1,0:T(8,128)(2,1)S(1)}, bf16[8,12,16,128]{3,2,1,0:T(8,128)(2,1)S(1)}, u32[]{:S(2)}, u32[]{:S(2)}) collective-permute-start(bf16[8,12,16,128]{3,2,1,0:T(8,128)(2,1)S(1)} %pad_maximum_fusion.7.refs_6_), channel_id=1, source_target_pairs={{0,24},{8,16},{16,8},{24,0},{1,25},{9,17},{17,9},{25,1},{2,26},{10... | collective-permute-start | bytes 1179656 | tf_op jit(solution)/shard_map/ppermute | solution.py:25
  124.5 8.1 %collective-permute-start.46 = (bf16[8,12,16,128]{3,2,1,0:T(8,128)(2,1)S(1)}, bf16[8,12,16,128]{3,2,1,0:T(8,128)(2,1)S(1)}, u32[]{:S(2)}, u32[]{:S(2)}) collective-permute-start(bf16[8,12,16,128]{3,2,1,0:T(8,128)(2,1)S(1)} %pad_maximum_fusion.8.refs_8_), channel_id=1, source_target_pairs={{0,8},{8,0},{16,24},{24,16},{1,9},{9,1},{17,25},{25,17},{2,10},{10... | collective-permute-start | bytes 1179656 | tf_op jit(solution)/shard_map/ppermute | solution.py:25
  125.7 3.7 %copy-start.1 = (bf16[8,1,192,3072]{3,2,1,0:T(8,128)(2,1)S(1)}, bf16[8,1,192,3072]{3,2,1,0:T(8,128)(2,1)}, u32[]{:S(2)}) copy-start(bf16[8,1,192,3072]{3,2,1,0:T(8,128)(2,1)} %param.6) | copy-start | bytes 28311556
  138.0 2.6 %collective-permute-start.48 = (bf16[3,192,512]{2,1,0:T(8,128)(2,1)S(1)}, bf16[3,192,512]{2,1,0:T(8,128)(2,1)S(1)}, u32[]{:S(2)}, u32[]{:S(2)}) collective-permute-start(bf16[3,192,512]{2,1,0:T(8,128)(2,1)S(1)} %get-tuple-element.139), channel_id=1, source_target_pairs={{0,1},{1,0},{2,3},{3,2},{4,5},{5,4},{6,7},{7,6},{8,9},{9,8},{10,11... | collective-permute-start | bytes 1769480 | tf_op jit(solution)/shard_map/ppermute | solution.py:25
  138.1 50.3 %copy-start.2 = (f32[1,192,512]{2,1,0:T(8,128)S(1)}, f32[1,192,512]{2,1,0:T(8,128)}, u32[]{:S(2)}) copy-start(f32[1,192,512]{2,1,0:T(8,128)} %param.8) | copy-start | bytes 1179652
  140.1 4.9 %collective-permute-start.47 = (bf16[1,192,512]{2,1,0:T(8,128)(2,1)S(1)}, bf16[1,192,512]{2,1,0:T(8,128)(2,1)S(1)}, u32[]{:S(2)}, u32[]{:S(2)}) collective-permute-start(bf16[1,192,512]{2,1,0:T(8,128)(2,1)S(1)} %get-tuple-element.137), channel_id=1, source_target_pairs={{0,1},{1,0},{2,3},{3,2},{4,5},{5,4},{6,7},{7,6},{8,9},{9,8},{10,11... | collective-permute-start | bytes 589832 | tf_op jit(solution)/shard_map/ppermute | solution.py:25
  140.8 12.4 %collective-permute-start.51 = (bf16[192,512]{1,0:T(8,128)(2,1)S(1)}, bf16[192,512]{1,0:T(8,128)(2,1)S(1)}, u32[]{:S(2)}, u32[]{:S(2)}) collective-permute-start(bf16[192,512]{1,0:T(8,128)(2,1)S(1)} %get-tuple-element.146), channel_id=1, source_target_pairs={{0,6},{2,4},{4,2},{6,0},{1,7},{3,5},{5,3},{7,1},{8,14},{10,12},{12... | collective-permute-start | bytes 589832 | tf_op jit(solution)/shard_map/ppermute | solution.py:25
  144.0 9.3 %collective-permute-start.50 = (bf16[192,512]{1,0:T(8,128)(2,1)S(1)}, bf16[192,512]{1,0:T(8,128)(2,1)S(1)}, u32[]{:S(2)}, u32[]{:S(2)}) collective-permute-start(bf16[192,512]{1,0:T(8,128)(2,1)S(1)} %get-tuple-element.147), channel_id=1, source_target_pairs={{0,4},{2,6},{4,0},{6,2},{1,5},{3,7},{5,1},{7,3},{8,12},{10,14},{12... | collective-permute-start | bytes 589832 | tf_op jit(solution)/shard_map/ppermute | solution.py:25
  144.6 9.4 %collective-permute-start.49 = (bf16[192,512]{1,0:T(8,128)(2,1)S(1)}, bf16[192,512]{1,0:T(8,128)(2,1)S(1)}, u32[]{:S(2)}, u32[]{:S(2)}) collective-permute-start(bf16[192,512]{1,0:T(8,128)(2,1)S(1)} %get-tuple-element.148), channel_id=1, source_target_pairs={{0,2},{2,0},{4,6},{6,4},{1,3},{3,1},{5,7},{7,5},{8,10},{10,8},{12,... | collective-permute-start | bytes 589832 | tf_op jit(solution)/shard_map/ppermute | solution.py:25
  155.4 4.7 %collective-permute-start.52 = (bf16[192,128]{1,0:T(8,128)(2,1)S(1)}, bf16[192,128]{1,0:T(8,128)(2,1)S(1)}, u32[]{:S(2)}, u32[]{:S(2)}) collective-permute-start(bf16[192,128]{1,0:T(8,128)(2,1)S(1)} %get-tuple-element.141), channel_id=1, source_target_pairs={{0,32},{32,0},{64,96},{96,64},{1,33},{33,1},{65,97},{97,65},{2,34}... | collective-permute-start | bytes 147464 | tf_op jit(solution)/shard_map/ppermute | solution.py:25
  157.5 5.6 %collective-permute-start.53 = (bf16[192,128]{1,0:T(8,128)(2,1)S(1)}, bf16[192,128]{1,0:T(8,128)(2,1)S(1)}, u32[]{:S(2)}, u32[]{:S(2)}) collective-permute-start(bf16[192,128]{1,0:T(8,128)(2,1)S(1)} %get-tuple-element.142), channel_id=1, source_target_pairs={{0,64},{32,96},{64,0},{96,32},{1,65},{33,97},{65,1},{97,33},{2,66}... | collective-permute-start | bytes 147464 | tf_op jit(solution)/shard_map/ppermute | solution.py:25
  158.3 5.3 %collective-permute-start.54 = (bf16[192,128]{1,0:T(8,128)(2,1)S(1)}, bf16[192,128]{1,0:T(8,128)(2,1)S(1)}, u32[]{:S(2)}, u32[]{:S(2)}) collective-permute-start(bf16[192,128]{1,0:T(8,128)(2,1)S(1)} %get-tuple-element.143), channel_id=1, source_target_pairs={{0,96},{32,64},{64,32},{96,0},{1,97},{33,65},{65,33},{97,1},{2,98}... | collective-permute-start | bytes 147464 | tf_op jit(solution)/shard_map/ppermute | solution.py:25
  163.6 10.0 %collective-permute-start.57 = (bf16[4,192,128]{2,1,0:T(8,128)(2,1)S(1)}, bf16[4,192,128]{2,1,0:T(8,128)(2,1)S(1)}, u32[]{:S(2)}, u32[]{:S(2)}) collective-permute-start(bf16[4,192,128]{2,1,0:T(8,128)(2,1)S(1)} %pad_maximum_fusion.19.refs_3_), channel_id=1, source_target_pairs={{0,24},{8,16},{16,8},{24,0},{1,25},{9,17},{17,9},{25,1},{2,26},{10... | collective-permute-start | bytes 589832 | tf_op jit(solution)/shard_map/ppermute | solution.py:25
  165.6 8.0 %collective-permute-start.56 = (bf16[4,192,128]{2,1,0:T(8,128)(2,1)S(1)}, bf16[4,192,128]{2,1,0:T(8,128)(2,1)S(1)}, u32[]{:S(2)}, u32[]{:S(2)}) collective-permute-start(bf16[4,192,128]{2,1,0:T(8,128)(2,1)S(1)} %pad_maximum_fusion.19.refs_3_), channel_id=1, source_target_pairs={{0,16},{8,24},{16,0},{24,8},{1,17},{9,25},{17,1},{25,9},{2,18},{10... | collective-permute-start | bytes 589832 | tf_op jit(solution)/shard_map/ppermute | solution.py:25
  166.6 7.7 %collective-permute-start.55 = (bf16[4,192,128]{2,1,0:T(8,128)(2,1)S(1)}, bf16[4,192,128]{2,1,0:T(8,128)(2,1)S(1)}, u32[]{:S(2)}, u32[]{:S(2)}) collective-permute-start(bf16[4,192,128]{2,1,0:T(8,128)(2,1)S(1)} %pad_maximum_fusion.19.refs_3_), channel_id=1, source_target_pairs={{0,8},{8,0},{16,24},{24,16},{1,9},{9,1},{17,25},{25,17},{2,10},{10... | collective-permute-start | bytes 589832 | tf_op jit(solution)/shard_map/ppermute | solution.py:25
  (1 other events, 0.7 us)

commit v3 on v2

--- a/solution.py
+++ b/solution.py
@@ -63,6 +63,10 @@
     return masks["x"], masks["z"]
 
 
+def after(done, value):
+    return lax.optimization_barrier((done, value))[1]
+
+
 def hold_kernel(tile_ref, held_ref, sem):
     copy = pltpu.make_async_copy(tile_ref, held_ref, sem)
     copy.start()
@@ -132,28 +136,28 @@
     return sent, mine_near[0].astype(F32) + swap(other_near, "core", 1)[0].astype(F32)
 
 
-def residual_kernel(pos_ref, before_ref, own_ref, *refs):
-    sums, out_ref, column_refs = refs[:3], refs[3], refs[4:]
+def residual_kernel(before_ref, own_ref, *refs):
+    sums, (out_ref, sent_ref) = refs[:3], refs[3:]
     total = own_ref[...] + (sums[0][...].astype(F32) + (sums[1][...].astype(F32) + sums[2][...].astype(F32)))
-    out_ref[...] = before_ref[...] - total
-    for mask in range(4):
-        lanes = pl.ds(pl.multiple_of((pos_ref[0] ^ mask) * 128, 128), 128)
-        column_refs[mask][...] = out_ref[:, lanes].astype(BF16)
+    left = before_ref[...] - total
+    out_ref[...] = left
+    half = left.astype(BF16)
+    for x in range(4):
+        for z in range(4):
+            sent_ref[x * 4 + z] = half[:, x * 128:(x + 1) * 128]
 
 
 def sums_over_y(sent):
     return [swap(sent[mask - 1], "y", mask) for mask in (1, 2, 3)]
 
 
-def residual_of(before, near, sums, pos):
-    piece = jax.ShapeDtypeStruct((192, 128), BF16)
-    out_shape = (jax.ShapeDtypeStruct((192, 512), F32),) + (piece,) * 4
-    return whole_call(residual_kernel, out_shape, scalars=1)(pos, before, near, *sums)
-
-
-def exchange(pieces):
-    bundle = jnp.stack([pieces[0]] + [swap(pieces[mask], "x", mask) for mask in (1, 2, 3)])
-    return [bundle] + [swap(bundle, "z", mask) for mask in (1, 2, 3)]
+def residual_of(before, near, sums):
+    out_shape = (jax.ShapeDtypeStruct((192, 512), F32), jax.ShapeDtypeStruct((16, 192, 128), BF16))
+    return whole_call(residual_kernel, out_shape)(before, near, *sums)
+
+
+def exchange(sent):
+    return lax.all_to_all(sent, ("x", "z"), 0, 0, tiled=True).reshape(3072, 128)
 
 
 def inverse_kernel(pos_ref, lists_ref, inverse_ref, *out_refs):
@@ -169,20 +173,17 @@
 
 
 def solve_kernel(last, pos_ref, lists_ref, counts_ref, *refs):
-    bundles, inverse_refs, refs = refs[:4], refs[4:6], refs[6:]
+    held, *inverse_refs = refs[:5]
+    refs = refs[5:]
     if last:
-        before_ref, sent_ref, held, total = refs
+        before_ref, sent_ref, total = refs
     else:
-        full_ref, *quarter_refs, held, total = refs
-    for z_mask in range(4):
-        for x_mask in range(4):
-            group = (pos_ref[0] ^ x_mask) * 4 + (pos_ref[1] ^ z_mask)
-            held[pl.ds(pl.multiple_of(group * 192, 64), 192), :] = bundles[z_mask][x_mask]
+        full_ref, *quarter_refs, total = refs
     total[...] = jnp.zeros_like(total)
     for s in range(16):
         ids = [lists_ref[s, k] for k in range(3)]
         picked = jnp.concatenate([held[pl.ds(pl.multiple_of(q * BLOCK, BLOCK), BLOCK), :] for q in ids])
-        fix = jnp.dot(inverse_refs[s // 8][s % 8, :96, :], picked, preferred_element_type=F32)
+        fix = jnp.dot(inverse_refs[s // 4][s % 4, :96, :], picked, preferred_element_type=F32)
         for k in range(3):
             total[ids[k]] += fix[k * 32:(k + 1) * 32]
     panel = pos_ref[2] * 2 + pos_ref[3]
@@ -199,14 +200,14 @@
                 quarter_refs[block // 6][block % 6 * 2 + half] = mean[half * 16:(half + 1) * 16].astype(BF16)
 
 
-def solve(bundles, inverses, lists, counts, pos, before=None):
+def solve(held, inverses, lists, counts, pos, before=None):
     last = before is not None
     if last:
         out_shape = jax.ShapeDtypeStruct((16, 48, 128), BF16)
     else:
         out_shape = (jax.ShapeDtypeStruct((24, 32, 128), F32),) + (jax.ShapeDtypeStruct((12, 16, 128), BF16),) * 4
-    scratch = [pltpu.VMEM((3072, 128), BF16), pltpu.VMEM((24, 32, 128), F32)]
-    args = [pos, lists, counts, *bundles, *inverses] + ([before] if last else [])
+    scratch = [pltpu.VMEM((24, 32, 128), F32)]
+    args = [pos, lists, counts, held, *inverses] + ([before] if last else [])
     return whole_call(lambda *refs: solve_kernel(last, *refs), out_shape, scratch, scalars=3)(*args)
 
 
@@ -226,30 +227,35 @@
 
     piece = jax.ShapeDtypeStruct((112, 384), BF16)
     sent = whole_call(inverse_kernel, (piece,) * 4, scalars=2)(pos, block_lists, local_inverse[0])
-    inverse = [sent]
+    near = {}
 
     def between(turn, held):
         if turn == 0:
-            inverse.append(swap(jnp.stack(sent[1:3]), "z", 1))
+            near["sent"] = after(held, sent)
+            near["first"] = swap(jnp.stack(near["sent"][1:3]), "z", 1)
         elif turn == 1:
-            inverse.append(swap(jnp.stack([sent[3], inverse[1][1]]), "z", 3))
+            start, first = after(held, (near["sent"], near["first"]))
+            near["second"] = swap(jnp.stack([start[3], first[1]]), "z", 3)
+            near["low"] = jnp.stack([start[0], first[0]])
+            near["low_far"] = swap(near["low"], "x", 1)
         else:
-            inverse.append(jnp.stack([sent[0], inverse[1][0], inverse[2][0], inverse[2][1]]))
-            inverse.append(swap(inverse[3], "x", 1))
-        held, inverse[-1] = lax.optimization_barrier((held, inverse[-1]))
+            near["high"] = after(held, near["second"])
+            near["high_far"] = swap(near["high"], "x", 3)
         return held
 
     half = start.astype(BF16).reshape(4, 3, 16, 512)
     bundles = gather_swaps([half[at] for at in range(4)], between)
-    tile, bundles = lax.optimization_barrier((hold(rows), bundles))
+    tile, bundles, low, high = lax.optimization_barrier(
+        (hold(rows), bundles, [near["low"], near["low_far"]], [near["high"], near["high_far"]])
+    )
     far, near = product(tile, bundles, pos, False)
-    inverses = jnp.concatenate(inverse[3:])
-    inverses = inverses, swap(inverses, "x", 3)
+    low, high = jnp.concatenate(low), jnp.concatenate(high)
+    inverses = low, swap(low, "x", 3), high, swap(high, "x", 1)
     sums, inverses = lax.optimization_barrier((sums_over_y(far), inverses))
     lists = jnp.concatenate([bundle[:, 96, :3] for bundle in inverses]).astype(jnp.int32)
 
-    residual, *pieces = residual_of(target, near, sums, pos)
-    fix, *quarters = solve(exchange(pieces), inverses, lists, counts, pos)
+    residual, sent = residual_of(target, near, sums)
+    fix, *quarters = solve(exchange(sent), inverses, lists, counts, pos)
     held = []
 
     def between(turn, parts):
@@ -262,8 +268,8 @@
     bundles = gather_swaps(quarters, between)
     tile, bundles = lax.optimization_barrier((hold(held[0]), bundles))
     far, near = product(tile, bundles, pos, True)
-    residual, *pieces = residual_of(residual, near, sums_over_y(far), pos)
-    sent = solve(exchange(pieces), inverses, lists, counts, pos, fix)
+    residual, sent = residual_of(residual, near, sums_over_y(far))
+    sent = solve(exchange(sent), inverses, lists, counts, pos, fix)
     pieces = lax.all_to_all(sent, ("x", "z"), 0, 0, tiled=True)
     result = whole_call(join_kernel, jax.ShapeDtypeStruct((192, 512), F32))(start, pieces)
     return (result[None], residual[None])

time: 190 us -> 180 us (0.947)
  blocking collectives: 12.8 us -> 31.2 us
  starting transfers between devices: 76.6 us -> 60.1 us
  waiting for transfers between devices: 65 us -> 54.5 us
    ppermute x58 -> x48, waiting for transfers between devices: 65 us -> 40.6 us  [swap(): return lax.ppermute(value, axis, [(i, i ^ mask) for i in range(size)])]
    ppermute x58 -> x48, starting transfers between devices: 76.6 us -> 55.3 us  [swap(): return lax.ppermute(value, axis, [(i, i ^ mask) for i in range(size)])]
    all_to_all x0 -> x1, blocking collectives: none -> 19.7 us  [exchange(): return lax.all_to_all(sent, ('x', 'z'), 0, 0, tiled=True).reshape(3072, 128)]
    all_to_all x0 -> x1, waiting for transfers between devices: none -> 13.9 us  [exchange(): return lax.all_to_all(sent, ('x', 'z'), 0, 0, tiled=True).reshape(3072, 128)]
    all_to_all x0 -> x1, starting transfers between devices: none -> 4.84 us  [exchange(): return lax.all_to_all(sent, ('x', 'z'), 0, 0, tiled=True).reshape(3072, 128)]
    unnamed x14 -> x18, local copies, waits for them, and re-layouts: 9.1 us -> 9.14 us
  transfers between devices with their start and end apart: 58 -> 49, of which waited for: 33 -> 22; matrix products, arithmetic and copies ran while one was open for 1% -> 1% of each run, Pallas kernels for 3% -> 3%
where the time goes in v3:
time: 180 us
  starting transfers between devices  60.1 us (33%)
  waiting for transfers between devices  54.5 us (30%)
  blocking collectives  31.2 us (17%)
  Pallas kernels  21.4 us (12%)
  local copies, waits for them, and re-layouts  9.26 us (5%)
  other arithmetic  2.19 us (1%)
    ppermute x48, starting transfers between devices, swap(): return lax.ppermute(value, axis, [(i, i ^ mask) for i in range(size)])  55.3 us
    ppermute x48, waiting for transfers between devices, swap(): return lax.ppermute(value, axis, [(i, i ^ mask) for i in range(size)])  40.6 us
    pallas_call x10, Pallas kernels, call(): pl.pallas_call(body, in_specs=[SMEM] * scalars + [VMEM] * (len(args) - sc...  20.1 us
    all_to_all x1, blocking collectives, exchange(): return lax.all_to_all(sent, ('x', 'z'), 0, 0, tiled=True).reshape(3072, 128)  19.7 us
    all_to_all x1, waiting for transfers between devices, exchange(): return lax.all_to_all(sent, ('x', 'z'), 0, 0, tiled=True).reshape(3072, 128)  13.9 us
    all_to_all x1, blocking collectives, body(): pieces = lax.all_to_all(sent, ('x', 'z'), 0, 0, tiled=True)  11.5 us
    unnamed x18, local copies, waits for them, and re-layouts  9.14 us
    all_to_all x1, starting transfers between devices, exchange(): return lax.all_to_all(sent, ('x', 'z'), 0, 0, tiled=True).reshape(3072, 128)  4.84 us
  transfers between devices with their start and end apart: 49, of which 22 were waited for; matrix products, arithmetic and copies ran while one was open for 1% of the time, Pallas kernels for 3%

profile of v3, /device:TPU:0, one launch (start us, length us, event | category | flops | bytes accessed | tf_op | source)
XLA Modules:
  0.0 179.8 jit_solution(622455249096154500)
XLA Ops:
  0.6 1.0 bitcast_convert_fusion
  1.7 1.7 collective-permute-start.8
  3.3 2.1 %collective-permute-start.12 = (bf16[1,3,16,512]{3,2,1,0:T(8,128)(2,1)S(1)}, bf16[1,3,16,512]{3,2,1,0:T(8,128)(2,1)S(1)}, u32[]{:S(2)}, u32[]{:S(2)}) collective-permute-start(bf16[1,3,16,512]{3,2,1,0:T(8,128)(2,1)S(1)} %bitcast.80), channel_id=1, source_target_pairs={{0,96},{32,64},{64,32},{96,0},{1,97},{33,65},{65,33},{97,1},{2,98}... | collective-permute-start | bytes 147464 | tf_op jit(solution)/shard_map/ppermute | solution.py:25
  5.4 4.0 %collective-permute-start.4 = (bf16[1,3,16,512]{3,2,1,0:T(8,128)(2,1)S(1)}, bf16[1,3,16,512]{3,2,1,0:T(8,128)(2,1)S(1)}, u32[]{:S(2)}, u32[]{:S(2)}) collective-permute-start(bf16[1,3,16,512]{3,2,1,0:T(8,128)(2,1)S(1)} %bitcast.84), channel_id=1, source_target_pairs={{0,24},{8,16},{16,8},{24,0},{1,25},{9,17},{17,9},{25,1},{2,26},{10... | collective-permute-start | bytes 147464 | tf_op jit(solution)/shard_map/ppermute | solution.py:25
  9.5 1.1 copy-done.3
  10.6 0.7 copy-done.6
  11.9 1.2 collective-permute-start.9
  13.3 2.1 %collective-permute-start.5 = (bf16[2,3,16,512]{3,2,1,0:T(8,128)(2,1)S(1)}, bf16[2,3,16,512]{3,2,1,0:T(8,128)(2,1)S(1)}, u32[]{:S(2)}, u32[]{:S(2)}) collective-permute-start(bf16[2,3,16,512]{3,2,1,0:T(8,128)(2,1)S(1)} %pad_maximum_fusion.20), channel_id=1, source_target_pairs={{0,8},{8,0},{16,24},{24,16},{1,9},{9,1},{17,25},{25,17},{2,10},{10... | collective-permute-start | bytes 294920 | tf_op jit(solution)/shard_map/ppermute | solution.py:25
  15.5 1.0 collective-permute-start.16
  16.5 1.3 collective-permute-done.9
  17.8 2.1 %collective-permute-start.10 = (bf16[4,3,16,512]{3,2,1,0:T(8,128)(2,1)S(1)}, bf16[4,3,16,512]{3,2,1,0:T(8,128)(2,1)S(1)}, u32[]{:S(2)}, u32[]{:S(2)}) collective-permute-start(bf16[4,3,16,512]{3,2,1,0:T(8,128)(2,1)S(1)} %pad_maximum_fusion.10), channel_id=1, source_target_pairs={{0,8},{8,0},{16,24},{24,16},{1,9},{9,1},{17,25},{25,17},{2,10},{10... | collective-permute-start | bytes 589832 | tf_op jit(solution)/shard_map/ppermute | solution.py:25
  20.0 1.1 collective-permute-start.14
  21.1 2.2 %collective-permute-start.6 = (bf16[4,3,16,512]{3,2,1,0:T(8,128)(2,1)S(1)}, bf16[4,3,16,512]{3,2,1,0:T(8,128)(2,1)S(1)}, u32[]{:S(2)}, u32[]{:S(2)}) collective-permute-start(bf16[4,3,16,512]{3,2,1,0:T(8,128)(2,1)S(1)} %pad_maximum_fusion.9), channel_id=1, source_target_pairs={{0,96},{32,64},{64,32},{96,0},{1,97},{33,65},{65,33},{97,1},{2,98}... | collective-permute-start | bytes 589832 | tf_op jit(solution)/shard_map/ppermute | solution.py:25
  23.3 1.5 collective-permute-start.2
  25.4 3.9 %collective-permute-done.2 = bf16[4,3,16,512]{3,2,1,0:T(8,128)(2,1)S(1)} collective-permute-done((bf16[4,3,16,512]{3,2,1,0:T(8,128)(2,1)S(1)}, bf16[4,3,16,512]{3,2,1,0:T(8,128)(2,1)S(1)}, u32[]{:S(2)}, u32[]{:S(2)}) %collective-permute-start.2) | collective-permute-done | bytes 196640 | tf_op jit(solution)/shard_map/ppermute | solution.py:25
  29.4 0.9 collective-permute-start.3
  30.4 1.9 %collective-permute-start.7 = (bf16[8,3,16,512]{3,2,1,0:T(8,128)(2,1)S(1)}, bf16[8,3,16,512]{3,2,1,0:T(8,128)(2,1)S(1)}, u32[]{:S(2)}, u32[]{:S(2)}) collective-permute-start(bf16[8,3,16,512]{3,2,1,0:T(8,128)(2,1)S(1)} %pad_maximum_fusion.1.refs_4_), channel_id=1, source_target_pairs={{0,32},{32,0},{64,96},{96,64},{1,33},{33,1},{65,97},{97,65},{2,34}... | collective-permute-start | bytes 1179656 | tf_op jit(solution)/shard_map/ppermute | solution.py:25
  32.6 0.7 collective-permute-start.11
  33.3 2.1 %collective-permute-start.17 = (bf16[2,112,384]{2,1,0:T(8,128)(2,1)S(1)}, bf16[2,112,384]{2,1,0:T(8,128)(2,1)S(1)}, u32[]{:S(2)}, u32[]{:S(2)}) collective-permute-start(bf16[2,112,384]{2,1,0:T(8,128)(2,1)S(1)} %pad_maximum_fusion.17), channel_id=1, source_target_pairs={{0,32},{32,0},{64,96},{96,64},{1,33},{33,1},{65,97},{97,65},{2,34}... | collective-permute-start | bytes 516104 | tf_op jit(solution)/shard_map/ppermute | solution.py:25
  35.4 5.7 %collective-permute-done.17 = bf16[2,112,384]{2,1,0:T(8,128)(2,1)S(1)} collective-permute-done((bf16[2,112,384]{2,1,0:T(8,128)(2,1)S(1)}, bf16[2,112,384]{2,1,0:T(8,128)(2,1)S(1)}, u32[]{:S(2)}, u32[]{:S(2)}) %collective-permute-start.17) | collective-permute-done | bytes 172064 | tf_op jit(solution)/shard_map/ppermute | solution.py:25
  41.1 1.7 collective-permute-start.19
  42.8 3.7 %copy-done = bf16[8,1,192,3072]{3,2,1,0:T(8,128)(2,1)S(1)} copy-done((bf16[8,1,192,3072]{3,2,1,0:T(8,128)(2,1)S(1)}, bf16[8,1,192,3072]{3,2,1,0:T(8,128)(2,1)}, u32[]{:S(2)}) %copy-start) | copy-done | bytes 9437208
  47.8 5.0 %shard_map.79 = (bf16[3,192,512]{2,1,0:T(8,128)(2,1)S(1)}, bf16[3,192,512]{2,1,0:T(8,128)(2,1)S(1)}, bf16[192,16,512]{2,1,0:T(8,128)(2,1)S(1)}) custom-call(s32[4]{0:T(128)S(1)} %pad_add_fusion.pos_ref.refs_0_, bf16[4,384,3072]{2,1,0:T(8,128)(2,1)S(1)} %shard_map.77.refs_1_.tile_ref, bf16[8,3,16,512]{3,2,1,0:T(8,128)(2,1)S(1)} %pad_maximum_fusion.refs_2_, ...), custom_call_target="tpu_custom_call" | custom-call | flops 3221225472 | bytes 1048576 | tf_op jit(solution)/shard_map/pallas_call | solution.py:30
  53.4 1.7 collective-permute-start.24
  55.1 2.0 %shard_map.80 = (bf16[1,192,512]{2,1,0:T(8,128)(2,1)S(1)}, bf16[1,192,512]{2,1,0:T(8,128)(2,1)S(1)}) custom-call(s32[4]{0:T(128)S(1)} %pad_add_fusion.pos_ref.refs_0_, bf16[4,384,3072]{2,1,0:T(8,128)(2,1)S(1)} %shard_map.77.refs_1_.tile_ref, bf16[192,16,512]{2,1,0:T(8,128)(2,1)S(1)} %get-tuple-element.98.filled), custom_call_target="tpu_custom_call" | custom-call | flops 1073741824 | bytes 1048576 | tf_op jit(solution)/shard_map/pallas_call | solution.py:30
  57.4 3.1 %collective-permute-start.23 = (bf16[192,512]{1,0:T(8,128)(2,1)S(1)}, bf16[192,512]{1,0:T(8,128)(2,1)S(1)}, u32[]{:S(2)}, u32[]{:S(2)}) collective-permute-start(bf16[192,512]{1,0:T(8,128)(2,1)S(1)} %get-tuple-element.135), channel_id=1, source_target_pairs={{0,6},{2,4},{4,2},{6,0},{1,7},{3,5},{5,3},{7,1},{8,14},{10,12},{12... | collective-permute-start | bytes 589832 | tf_op jit(solution)/shard_map/ppermute | solution.py:25
  61.6 1.9 %collective-permute-done.25.refs_7_ = bf16[4,112,384]{2,1,0:T(8,128)(2,1)S(1)} collective-permute-done((bf16[4,112,384]{2,1,0:T(8,128)(2,1)S(1)}, bf16[4,112,384]{2,1,0:T(8,128)(2,1)S(1)}, u32[]{:S(2)}, u32[]{:S(2)}) %collective-permute-start.25) | collective-permute-done | bytes 344096 | tf_op jit(solution)/shard_map/ppermute | solution.py:25
  63.5 1.4 collective-permute-done.24.refs_5_
  64.9 5.3 %collective-permute-done.23.refs_2_ = bf16[192,512]{1,0:T(8,128)(2,1)S(1)} collective-permute-done((bf16[192,512]{1,0:T(8,128)(2,1)S(1)}, bf16[192,512]{1,0:T(8,128)(2,1)S(1)}, u32[]{:S(2)}, u32[]{:S(2)}) %collective-permute-start.23) | collective-permute-done | bytes 196640 | tf_op jit(solution)/shard_map/ppermute | solution.py:25
  70.2 0.7 collective-permute-done.21.refs_0_
  70.9 1.1 shard_map.81
  72.0 4.8 %all-to-all-start = ((bf16[16,192,128]{2,1,0:T(8,128)(2,1)}), bf16[16,192,128]{2,1,0:T(8,128)(2,1)S(1)}, u32[]{:S(2)}, u32[]{:S(2)}) async-start(bf16[16,192,128]{2,1,0:T(8,128)(2,1)} %get-tuple-element.105), calls=%async_computation | async-start | bytes 1572864 | tf_op jit(solution)/shard_map/all_to_all | solution.py:160
  76.9 13.9 %all-to-all-done = bf16[16,192,128]{2,1,0:T(8,128)(2,1)S(1)} async-done(((bf16[16,192,128]{2,1,0:T(8,128)(2,1)}), bf16[16,192,128]{2,1,0:T(8,128)(2,1)S(1)}, u32[]{:S(2)}, u32[]{:S(2)}) %all-to-all-start) | async-done | bytes 786464 | tf_op jit(solution)/shard_map/all_to_all | solution.py:160
  90.8 1.2 shard_map.82
  92.0 0.8 collective-permute-start.30
  93.7 1.6 collective-permute-start.36
  95.4 2.1 %collective-permute-done.30 = bf16[1,12,16,128]{3,2,1,0:T(8,128)(2,1)S(1)} collective-permute-done((bf16[1,12,16,128]{3,2,1,0:T(8,128)(2,1)S(1)}, bf16[1,12,16,128]{3,2,1,0:T(8,128)(2,1)S(1)}, u32[]{:S(2)}, u32[]{:S(2)}) %collective-permute-start.30) | collective-permute-done | bytes 49184 | tf_op jit(solution)/shard_map/ppermute | solution.py:25
  97.6 2.2 %collective-permute-start.28 = (bf16[2,12,16,128]{3,2,1,0:T(8,128)(2,1)S(1)}, bf16[2,12,16,128]{3,2,1,0:T(8,128)(2,1)S(1)}, u32[]{:S(2)}, u32[]{:S(2)}) collective-permute-start(bf16[2,12,16,128]{3,2,1,0:T(8,128)(2,1)S(1)} %pad_maximum_fusion.23), channel_id=1, source_target_pairs={{0,24},{8,16},{16,8},{24,0},{1,25},{9,17},{17,9},{25,1},{2,26},{10... | collective-permute-start | bytes 294920 | tf_op jit(solution)/shard_map/ppermute | solution.py:25
  99.8 1.1 collective-permute-start.34
  100.9 0.9 collective-permute-start.37
  102.2 1.2 collective-permute-start.32
  103.5 1.4 collective-permute-start.29
  104.9 0.9 collective-permute-done.34
  105.9 2.5 %collective-permute-start.38 = (bf16[4,12,16,128]{3,2,1,0:T(8,128)(2,1)S(1)}, bf16[4,12,16,128]{3,2,1,0:T(8,128)(2,1)S(1)}, u32[]{:S(2)}, u32[]{:S(2)}) collective-permute-start(bf16[4,12,16,128]{3,2,1,0:T(8,128)(2,1)S(1)} %pad_maximum_fusion.15), channel_id=1, source_target_pairs={{0,24},{8,16},{16,8},{24,0},{1,25},{9,17},{17,9},{25,1},{2,26},{10... | collective-permute-start | bytes 589832 | tf_op jit(solution)/shard_map/ppermute | solution.py:25
  108.4 0.7 collective-permute-done.32
  109.3 2.2 %collective-permute-done.35 = bf16[4,12,16,128]{3,2,1,0:T(8,128)(2,1)S(1)} collective-permute-done((bf16[4,12,16,128]{3,2,1,0:T(8,128)(2,1)S(1)}, bf16[4,12,16,128]{3,2,1,0:T(8,128)(2,1)S(1)}, u32[]{:S(2)}, u32[]{:S(2)}) %collective-permute-start.35) | collective-permute-done | bytes 196640 | tf_op jit(solution)/shard_map/ppermute | solution.py:25
  111.5 1.5 collective-permute-done.38
  113.1 2.4 %collective-permute-start.39 = (bf16[8,12,16,128]{3,2,1,0:T(8,128)(2,1)S(1)}, bf16[8,12,16,128]{3,2,1,0:T(8,128)(2,1)S(1)}, u32[]{:S(2)}, u32[]{:S(2)}) collective-permute-start(bf16[8,12,16,128]{3,2,1,0:T(8,128)(2,1)S(1)} %pad_maximum_fusion.4.refs_2_), channel_id=1, source_target_pairs={{0,96},{32,64},{64,32},{96,0},{1,97},{33,65},{65,33},{97,1},{2,98}... | collective-permute-start | bytes 1179656 | tf_op jit(solution)/shard_map/ppermute | solution.py:25
  115.5 1.0 collective-permute-start.41
  117.1 3.7 %copy-done.1 = bf16[8,1,192,3072]{3,2,1,0:T(8,128)(2,1)S(1)} copy-done((bf16[8,1,192,3072]{3,2,1,0:T(8,128)(2,1)S(1)}, bf16[8,1,192,3072]{3,2,1,0:T(8,128)(2,1)}, u32[]{:S(2)}) %copy-start.1) | copy-done | bytes 9437208
  120.8 0.6 shard_map.83.refs_1_.tile_ref
  121.4 0.8 collective-permute-done.39.refs_3_
  122.2 1.1 collective-permute-done.40.refs_5_
  123.2 1.2 collective-permute-done.41.refs_7_
  124.5 5.4 %shard_map.84 = (bf16[3,192,512]{2,1,0:T(8,128)(2,1)S(1)}, bf16[3,192,512]{2,1,0:T(8,128)(2,1)S(1)}, bf16[192,16,512]{2,1,0:T(8,128)(2,1)S(1)}) custom-call(s32[4]{0:T(128)S(1)} %pad_add_fusion.pos_ref.refs_0_, bf16[4,384,3072]{2,1,0:T(8,128)(2,1)S(1)} %shard_map.83.refs_1_.tile_ref, bf16[8,12,16,128]{3,2,1,0:T(8,128)(2,1)S(1)} %pad_maximum_fusion.4.refs_2_, ...), custom_call_target="tpu_custom_call" | custom-call | flops 3221225472 | bytes 1048576 | tf_op jit(solution)/shard_map/pallas_call | solution.py:30
  129.9 2.0 %shard_map.85 = (bf16[1,192,512]{2,1,0:T(8,128)(2,1)S(1)}, bf16[1,192,512]{2,1,0:T(8,128)(2,1)S(1)}) custom-call(s32[4]{0:T(128)S(1)} %pad_add_fusion.pos_ref.refs_0_, bf16[4,384,3072]{2,1,0:T(8,128)(2,1)S(1)} %shard_map.83.refs_1_.tile_ref, bf16[192,16,512]{2,1,0:T(8,128)(2,1)S(1)} %get-tuple-element.124.filled), custom_call_target="tpu_custom_call" | custom-call | flops 1073741824 | bytes 1048576 | tf_op jit(solution)/shard_map/pallas_call | solution.py:30
  132.6 2.6 %collective-permute-start.47 = (bf16[192,512]{1,0:T(8,128)(2,1)S(1)}, bf16[192,512]{1,0:T(8,128)(2,1)S(1)}, u32[]{:S(2)}, u32[]{:S(2)}) collective-permute-start(bf16[192,512]{1,0:T(8,128)(2,1)S(1)} %get-tuple-element.132), channel_id=1, source_target_pairs={{0,6},{2,4},{4,2},{6,0},{1,7},{3,5},{5,3},{7,1},{8,14},{10,12},{12... | collective-permute-start | bytes 589832 | tf_op jit(solution)/shard_map/ppermute | solution.py:25
  135.9 0.9 collective-permute-start.45
  136.9 8.1 %collective-permute-done.47.refs_2_ = bf16[192,512]{1,0:T(8,128)(2,1)S(1)} collective-permute-done((bf16[192,512]{1,0:T(8,128)(2,1)S(1)}, bf16[192,512]{1,0:T(8,128)(2,1)S(1)}, u32[]{:S(2)}, u32[]{:S(2)}) %collective-permute-start.47) | collective-permute-done | bytes 196640 | tf_op jit(solution)/shard_map/ppermute | solution.py:25
  145.6 0.9 shard_map.86
  146.5 19.7 %all_to_all.15 = bf16[16,192,128]{2,1,0:T(8,128)(2,1)S(1)} all-to-all(bf16[16,192,128]{2,1,0:T(8,128)(2,1)S(1)} %get-tuple-element.129), channel_id=1, replica_groups=mesh['x'=4,'z'=4,'y'=4,'core'=2] {'x','z'}, dimensions={0} | all-to-all | bytes 1572864 | tf_op jit(solution)/shard_map/all_to_all | solution.py:160
  166.2 1.2 shard_map.87
  167.5 11.5 %all_to_all.16.pieces_ref = bf16[16,48,128]{2,1,0:T(8,128)(2,1)S(1)} all-to-all(bf16[16,48,128]{2,1,0:T(8,128)(2,1)S(1)} %shard_map.87), channel_id=1, replica_groups=mesh['x'=4,'z'=4,'y'=4,'core'=2] {'x','z'}, dimensions={0} | all-to-all | bytes 393216 | tf_op jit(solution)/shard_map/all_to_all | solution.py:273
  179.0 0.8 shard_map.88
  (108 shorter events, 9.8 us)
Async XLA Ops:
  1.7 10.2 %collective-permute-start.8 = (bf16[1,3,16,512]{3,2,1,0:T(8,128)(2,1)S(1)}, bf16[1,3,16,512]{3,2,1,0:T(8,128)(2,1)S(1)}, u32[]{:S(2)}, u32[]{:S(2)}) collective-permute-start(bf16[1,3,16,512]{3,2,1,0:T(8,128)(2,1)S(1)} %bitcast.76), channel_id=1, source_target_pairs={{0,32},{32,0},{64,96},{96,64},{1,33},{33,1},{65,97},{97,65},{2,34}... | collective-permute-start | bytes 147464 | tf_op jit(solution)/shard_map/ppermute | solution.py:25
  3.3 9.8 %collective-permute-start.12 = (bf16[1,3,16,512]{3,2,1,0:T(8,128)(2,1)S(1)}, bf16[1,3,16,512]{3,2,1,0:T(8,128)(2,1)S(1)}, u32[]{:S(2)}, u32[]{:S(2)}) collective-permute-start(bf16[1,3,16,512]{3,2,1,0:T(8,128)(2,1)S(1)} %bitcast.80), channel_id=1, source_target_pairs={{0,96},{32,64},{64,32},{96,0},{1,97},{33,65},{65,33},{97,1},{2,98}... | collective-permute-start | bytes 147464 | tf_op jit(solution)/shard_map/ppermute | solution.py:25
  5.4 7.8 %collective-permute-start.4 = (bf16[1,3,16,512]{3,2,1,0:T(8,128)(2,1)S(1)}, bf16[1,3,16,512]{3,2,1,0:T(8,128)(2,1)S(1)}, u32[]{:S(2)}, u32[]{:S(2)}) collective-permute-start(bf16[1,3,16,512]{3,2,1,0:T(8,128)(2,1)S(1)} %bitcast.84), channel_id=1, source_target_pairs={{0,24},{8,16},{16,8},{24,0},{1,25},{9,17},{17,9},{25,1},{2,26},{10... | collective-permute-start | bytes 147464 | tf_op jit(solution)/shard_map/ppermute | solution.py:25
  9.5 5.9 %collective-permute-start = (bf16[1,3,16,512]{3,2,1,0:T(8,128)(2,1)S(1)}, bf16[1,3,16,512]{3,2,1,0:T(8,128)(2,1)S(1)}, u32[]{:S(2)}, u32[]{:S(2)}) collective-permute-start(bf16[1,3,16,512]{3,2,1,0:T(8,128)(2,1)S(1)} %bitcast.88), channel_id=1, source_target_pairs={{0,8},{8,0},{16,24},{24,16},{1,9},{9,1},{17,25},{25,17},{2,10},{10... | collective-permute-start | bytes 147464 | tf_op jit(solution)/shard_map/ppermute | solution.py:25
  9.5 1.1 copy-start.3
  10.6 0.7 copy-start.6
  11.9 5.9 %collective-permute-start.9 = (bf16[2,3,16,512]{3,2,1,0:T(8,128)(2,1)S(1)}, bf16[2,3,16,512]{3,2,1,0:T(8,128)(2,1)S(1)}, u32[]{:S(2)}, u32[]{:S(2)}) collective-permute-start(bf16[2,3,16,512]{3,2,1,0:T(8,128)(2,1)S(1)} %pad_maximum_fusion.21), channel_id=1, source_target_pairs={{0,96},{32,64},{64,32},{96,0},{1,97},{33,65},{65,33},{97,1},{2,98}... | collective-permute-start | bytes 294920 | tf_op jit(solution)/shard_map/ppermute | solution.py:25
  13.1 6.8 %collective-permute-start.13 = (bf16[2,3,16,512]{3,2,1,0:T(8,128)(2,1)S(1)}, bf16[2,3,16,512]{3,2,1,0:T(8,128)(2,1)S(1)}, u32[]{:S(2)}, u32[]{:S(2)}) collective-permute-start(bf16[2,3,16,512]{3,2,1,0:T(8,128)(2,1)S(1)} %pad_maximum_fusion.22), channel_id=1, source_target_pairs={{0,32},{32,0},{64,96},{96,64},{1,33},{33,1},{65,97},{97,65},{2,34}... | collective-permute-start | bytes 294920 | tf_op jit(solution)/shard_map/ppermute | solution.py:25
  13.3 7.8 %collective-permute-start.5 = (bf16[2,3,16,512]{3,2,1,0:T(8,128)(2,1)S(1)}, bf16[2,3,16,512]{3,2,1,0:T(8,128)(2,1)S(1)}, u32[]{:S(2)}, u32[]{:S(2)}) collective-permute-start(bf16[2,3,16,512]{3,2,1,0:T(8,128)(2,1)S(1)} %pad_maximum_fusion.20), channel_id=1, source_target_pairs={{0,8},{8,0},{16,24},{24,16},{1,9},{9,1},{17,25},{25,17},{2,10},{10... | collective-permute-start | bytes 294920 | tf_op jit(solution)/shard_map/ppermute | solution.py:25
  15.4 7.9 %collective-permute-start.1 = (bf16[2,3,16,512]{3,2,1,0:T(8,128)(2,1)S(1)}, bf16[2,3,16,512]{3,2,1,0:T(8,128)(2,1)S(1)}, u32[]{:S(2)}, u32[]{:S(2)}) collective-permute-start(bf16[2,3,16,512]{3,2,1,0:T(8,128)(2,1)S(1)} %pad_maximum_fusion.19), channel_id=1, source_target_pairs={{0,24},{8,16},{16,8},{24,0},{1,25},{9,17},{17,9},{25,1},{2,26},{10... | collective-permute-start | bytes 294920 | tf_op jit(solution)/shard_map/ppermute | solution.py:25
  15.5 9.3 %collective-permute-start.16 = (bf16[2,112,384]{2,1,0:T(8,128)(2,1)S(1)}, bf16[2,112,384]{2,1,0:T(8,128)(2,1)S(1)}, u32[]{:S(2)}, u32[]{:S(2)}) collective-permute-start(bf16[2,112,384]{2,1,0:T(8,128)(2,1)S(1)} %pad_maximum_fusion.16), channel_id=1, source_target_pairs={{0,8},{8,0},{16,24},{24,16},{1,9},{9,1},{17,25},{25,17},{2,10},{10... | collective-permute-start | bytes 516104 | tf_op jit(solution)/shard_map/ppermute | solution.py:25
  17.8 14.8 %collective-permute-start.10 = (bf16[4,3,16,512]{3,2,1,0:T(8,128)(2,1)S(1)}, bf16[4,3,16,512]{3,2,1,0:T(8,128)(2,1)S(1)}, u32[]{:S(2)}, u32[]{:S(2)}) collective-permute-start(bf16[4,3,16,512]{3,2,1,0:T(8,128)(2,1)S(1)} %pad_maximum_fusion.10), channel_id=1, source_target_pairs={{0,8},{8,0},{16,24},{24,16},{1,9},{9,1},{17,25},{25,17},{2,10},{10... | collective-permute-start | bytes 589832 | tf_op jit(solution)/shard_map/ppermute | solution.py:25
  20.0 12.4 %collective-permute-start.14 = (bf16[4,3,16,512]{3,2,1,0:T(8,128)(2,1)S(1)}, bf16[4,3,16,512]{3,2,1,0:T(8,128)(2,1)S(1)}, u32[]{:S(2)}, u32[]{:S(2)}) collective-permute-start(bf16[4,3,16,512]{3,2,1,0:T(8,128)(2,1)S(1)} %pad_maximum_fusion.11), channel_id=1, source_target_pairs={{0,24},{8,16},{16,8},{24,0},{1,25},{9,17},{17,9},{25,1},{2,26},{10... | collective-permute-start | bytes 589832 | tf_op jit(solution)/shard_map/ppermute | solution.py:25
  21.1 9.3 %collective-permute-start.6 = (bf16[4,3,16,512]{3,2,1,0:T(8,128)(2,1)S(1)}, bf16[4,3,16,512]{3,2,1,0:T(8,128)(2,1)S(1)}, u32[]{:S(2)}, u32[]{:S(2)}) collective-permute-start(bf16[4,3,16,512]{3,2,1,0:T(8,128)(2,1)S(1)} %pad_maximum_fusion.9), channel_id=1, source_target_pairs={{0,96},{32,64},{64,32},{96,0},{1,97},{33,65},{65,33},{97,1},{2,98}... | collective-permute-start | bytes 589832 | tf_op jit(solution)/shard_map/ppermute | solution.py:25
  23.3 6.1 %collective-permute-start.2 = (bf16[4,3,16,512]{3,2,1,0:T(8,128)(2,1)S(1)}, bf16[4,3,16,512]{3,2,1,0:T(8,128)(2,1)S(1)}, u32[]{:S(2)}, u32[]{:S(2)}) collective-permute-start(bf16[4,3,16,512]{3,2,1,0:T(8,128)(2,1)S(1)} %pad_maximum_fusion.8), channel_id=1, source_target_pairs={{0,32},{32,0},{64,96},{96,64},{1,33},{33,1},{65,97},{97,65},{2,34}... | collective-permute-start | bytes 589832 | tf_op jit(solution)/shard_map/ppermute | solution.py:25
  24.8 8.5 %collective-permute-start.18 = (bf16[2,112,384]{2,1,0:T(8,128)(2,1)S(1)}, bf16[2,112,384]{2,1,0:T(8,128)(2,1)S(1)}, u32[]{:S(2)}, u32[]{:S(2)}) collective-permute-start(bf16[2,112,384]{2,1,0:T(8,128)(2,1)S(1)} %pad_maximum_fusion.18), channel_id=1, source_target_pairs={{0,24},{8,16},{16,8},{24,0},{1,25},{9,17},{17,9},{25,1},{2,26},{10... | collective-permute-start | bytes 516104 | tf_op jit(solution)/shard_map/ppermute | solution.py:25
  29.4 18.4 %collective-permute-start.3 = (bf16[8,3,16,512]{3,2,1,0:T(8,128)(2,1)S(1)}, bf16[8,3,16,512]{3,2,1,0:T(8,128)(2,1)S(1)}, u32[]{:S(2)}, u32[]{:S(2)}) collective-permute-start(bf16[8,3,16,512]{3,2,1,0:T(8,128)(2,1)S(1)} %pad_maximum_fusion.refs_2_), channel_id=1, source_target_pairs={{0,96},{32,64},{64,32},{96,0},{1,97},{33,65},{65,33},{97,1},{2,98}... | collective-permute-start | bytes 1179656 | tf_op jit(solution)/shard_map/ppermute | solution.py:25
  30.4 17.4 %collective-permute-start.7 = (bf16[8,3,16,512]{3,2,1,0:T(8,128)(2,1)S(1)}, bf16[8,3,16,512]{3,2,1,0:T(8,128)(2,1)S(1)}, u32[]{:S(2)}, u32[]{:S(2)}) collective-permute-start(bf16[8,3,16,512]{3,2,1,0:T(8,128)(2,1)S(1)} %pad_maximum_fusion.1.refs_4_), channel_id=1, source_target_pairs={{0,32},{32,0},{64,96},{96,64},{1,33},{33,1},{65,97},{97,65},{2,34}... | collective-permute-start | bytes 1179656 | tf_op jit(solution)/shard_map/ppermute | solution.py:25
  32.4 15.4 %collective-permute-start.15 = (bf16[8,3,16,512]{3,2,1,0:T(8,128)(2,1)S(1)}, bf16[8,3,16,512]{3,2,1,0:T(8,128)(2,1)S(1)}, u32[]{:S(2)}, u32[]{:S(2)}) collective-permute-start(bf16[8,3,16,512]{3,2,1,0:T(8,128)(2,1)S(1)} %pad_maximum_fusion.3.refs_8_), channel_id=1, source_target_pairs={{0,8},{8,0},{16,24},{24,16},{1,9},{9,1},{17,25},{25,17},{2,10},{10... | collective-permute-start | bytes 1179656 | tf_op jit(solution)/shard_map/ppermute | solution.py:25
  32.6 15.2 %collective-permute-start.11 = (bf16[8,3,16,512]{3,2,1,0:T(8,128)(2,1)S(1)}, bf16[8,3,16,512]{3,2,1,0:T(8,128)(2,1)S(1)}, u32[]{:S(2)}, u32[]{:S(2)}) collective-permute-start(bf16[8,3,16,512]{3,2,1,0:T(8,128)(2,1)S(1)} %pad_maximum_fusion.2.refs_6_), channel_id=1, source_target_pairs={{0,24},{8,16},{16,8},{24,0},{1,25},{9,17},{17,9},{25,1},{2,26},{10... | collective-permute-start | bytes 1179656 | tf_op jit(solution)/shard_map/ppermute | solution.py:25
  33.3 7.8 %collective-permute-start.17 = (bf16[2,112,384]{2,1,0:T(8,128)(2,1)S(1)}, bf16[2,112,384]{2,1,0:T(8,128)(2,1)S(1)}, u32[]{:S(2)}, u32[]{:S(2)}) collective-permute-start(bf16[2,112,384]{2,1,0:T(8,128)(2,1)S(1)} %pad_maximum_fusion.17), channel_id=1, source_target_pairs={{0,32},{32,0},{64,96},{96,64},{1,33},{33,1},{65,97},{97,65},{2,34}... | collective-permute-start | bytes 516104 | tf_op jit(solution)/shard_map/ppermute | solution.py:25
  41.1 6.6 %collective-permute-start.19 = (bf16[2,112,384]{2,1,0:T(8,128)(2,1)S(1)}, bf16[2,112,384]{2,1,0:T(8,128)(2,1)S(1)}, u32[]{:S(2)}, u32[]{:S(2)}) collective-permute-start(bf16[2,112,384]{2,1,0:T(8,128)(2,1)S(1)} %collective-permute-done.18), channel_id=1, source_target_pairs={{0,96},{32,64},{64,32},{96,0},{1,97},{33,65},{65,33},{97,1},{2,98}... | collective-permute-start | bytes 516104 | tf_op jit(solution)/shard_map/ppermute | solution.py:25
  42.8 3.7 %copy-start = (bf16[8,1,192,3072]{3,2,1,0:T(8,128)(2,1)S(1)}, bf16[8,1,192,3072]{3,2,1,0:T(8,128)(2,1)}, u32[]{:S(2)}) copy-start(bf16[8,1,192,3072]{3,2,1,0:T(8,128)(2,1)} %param.6) | copy-start | bytes 28311556
  52.8 18.1 %copy-start.4 = (f32[1,192,512]{2,1,0:T(8,128)S(1)}, f32[1,192,512]{2,1,0:T(8,128)}, u32[]{:S(2)}) copy-start(f32[1,192,512]{2,1,0:T(8,128)} %param.7) | copy-start | bytes 1179652
  52.8 4.4 %collective-permute-start.20 = (bf16[3,192,512]{2,1,0:T(8,128)(2,1)S(1)}, bf16[3,192,512]{2,1,0:T(8,128)(2,1)S(1)}, u32[]{:S(2)}, u32[]{:S(2)}) collective-permute-start(bf16[3,192,512]{2,1,0:T(8,128)(2,1)S(1)} %get-tuple-element.89), channel_id=1, source_target_pairs={{0,1},{1,0},{2,3},{3,2},{4,5},{5,4},{6,7},{7,6},{8,9},{9,8},{10,11... | collective-permute-start | bytes 1769480 | tf_op jit(solution)/shard_map/ppermute | solution.py:25
  53.0 37.8 %copy-start.5 = (s32[192]{0:T(256)S(1)}, s32[192]{0:T(256)}, u32[]{:S(2)}) copy-start(s32[192]{0:T(256)} %refs_2_.3) | copy-start | bytes 2308
  53.0 10.5 %collective-permute-start.25 = (bf16[4,112,384]{2,1,0:T(8,128)(2,1)S(1)}, bf16[4,112,384]{2,1,0:T(8,128)(2,1)S(1)}, u32[]{:S(2)}, u32[]{:S(2)}) collective-permute-start(bf16[4,112,384]{2,1,0:T(8,128)(2,1)S(1)} %constant_dynamic-update-slice_fusion.2.refs_6_), channel_id=1, source_target_pairs={{0,32},{32,0},{64,96},{96,64},{1,33},{33,1},{65,97},{97,65},{2,34}... | collective-permute-start | bytes 1032200 | tf_op jit(solution)/shard_map/ppermute | solution.py:25
  53.4 11.5 %collective-permute-start.24 = (bf16[4,112,384]{2,1,0:T(8,128)(2,1)S(1)}, bf16[4,112,384]{2,1,0:T(8,128)(2,1)S(1)}, u32[]{:S(2)}, u32[]{:S(2)}) collective-permute-start(bf16[4,112,384]{2,1,0:T(8,128)(2,1)S(1)} %constant_dynamic-update-slice_fusion.refs_4_), channel_id=1, source_target_pairs={{0,96},{32,64},{64,32},{96,0},{1,97},{33,65},{65,33},{97,1},{2,98}... | collective-permute-start | bytes 1032200 | tf_op jit(solution)/shard_map/ppermute | solution.py:25
  57.1 4.0 %collective-permute-start.26 = (bf16[1,192,512]{2,1,0:T(8,128)(2,1)S(1)}, bf16[1,192,512]{2,1,0:T(8,128)(2,1)S(1)}, u32[]{:S(2)}, u32[]{:S(2)}) collective-permute-start(bf16[1,192,512]{2,1,0:T(8,128)(2,1)S(1)} %get-tuple-element.100), channel_id=1, source_target_pairs={{0,1},{1,0},{2,3},{3,2},{4,5},{5,4},{6,7},{7,6},{8,9},{9,8},{10,11... | collective-permute-start | bytes 589832 | tf_op jit(solution)/shard_map/ppermute | solution.py:25
  57.4 12.8 %collective-permute-start.23 = (bf16[192,512]{1,0:T(8,128)(2,1)S(1)}, bf16[192,512]{1,0:T(8,128)(2,1)S(1)}, u32[]{:S(2)}, u32[]{:S(2)}) collective-permute-start(bf16[192,512]{1,0:T(8,128)(2,1)S(1)} %get-tuple-element.135), channel_id=1, source_target_pairs={{0,6},{2,4},{4,2},{6,0},{1,7},{3,5},{5,3},{7,1},{8,14},{10,12},{12... | collective-permute-start | bytes 589832 | tf_op jit(solution)/shard_map/ppermute | solution.py:25
  60.5 9.7 %collective-permute-start.22 = (bf16[192,512]{1,0:T(8,128)(2,1)S(1)}, bf16[192,512]{1,0:T(8,128)(2,1)S(1)}, u32[]{:S(2)}, u32[]{:S(2)}) collective-permute-start(bf16[192,512]{1,0:T(8,128)(2,1)S(1)} %get-tuple-element.136), channel_id=1, source_target_pairs={{0,4},{2,6},{4,0},{6,2},{1,5},{3,7},{5,1},{7,3},{8,12},{10,14},{12... | collective-permute-start | bytes 589832 | tf_op jit(solution)/shard_map/ppermute | solution.py:25
  61.1 9.8 %collective-permute-start.21 = (bf16[192,512]{1,0:T(8,128)(2,1)S(1)}, bf16[192,512]{1,0:T(8,128)(2,1)S(1)}, u32[]{:S(2)}, u32[]{:S(2)}) collective-permute-start(bf16[192,512]{1,0:T(8,128)(2,1)S(1)} %get-tuple-element.137), channel_id=1, source_target_pairs={{0,2},{2,0},{4,6},{6,4},{1,3},{3,1},{5,7},{7,5},{8,10},{10,8},{12,... | collective-permute-start | bytes 589832 | tf_op jit(solution)/shard_map/ppermute | solution.py:25
  72.0 18.9 %all-to-all-start = ((bf16[16,192,128]{2,1,0:T(8,128)(2,1)}), bf16[16,192,128]{2,1,0:T(8,128)(2,1)S(1)}, u32[]{:S(2)}, u32[]{:S(2)}) async-start(bf16[16,192,128]{2,1,0:T(8,128)(2,1)} %get-tuple-element.105), calls=%async_computation | async-start | bytes 1572864 | tf_op jit(solution)/shard_map/all_to_all | solution.py:160
  92.0 5.4 %collective-permute-start.30 = (bf16[1,12,16,128]{3,2,1,0:T(8,128)(2,1)S(1)}, bf16[1,12,16,128]{3,2,1,0:T(8,128)(2,1)S(1)}, u32[]{:S(2)}, u32[]{:S(2)}) collective-permute-start(bf16[1,12,16,128]{3,2,1,0:T(8,128)(2,1)S(1)} %bitcast.67), channel_id=1, source_target_pairs={{0,24},{8,16},{16,8},{24,0},{1,25},{9,17},{17,9},{25,1},{2,26},{10... | collective-permute-start | bytes 147464 | tf_op jit(solution)/shard_map/ppermute | solution.py:25
  92.9 4.7 %collective-permute-start.27 = (bf16[1,12,16,128]{3,2,1,0:T(8,128)(2,1)S(1)}, bf16[1,12,16,128]{3,2,1,0:T(8,128)(2,1)S(1)}, u32[]{:S(2)}, u32[]{:S(2)}) collective-permute-start(bf16[1,12,16,128]{3,2,1,0:T(8,128)(2,1)S(1)} %bitcast.63), channel_id=1, source_target_pairs={{0,8},{8,0},{16,24},{24,16},{1,9},{9,1},{17,25},{25,17},{2,10},{10... | collective-permute-start | bytes 147464 | tf_op jit(solution)/shard_map/ppermute | solution.py:25
  93.2 6.6 %collective-permute-start.33 = (bf16[1,12,16,128]{3,2,1,0:T(8,128)(2,1)S(1)}, bf16[1,12,16,128]{3,2,1,0:T(8,128)(2,1)S(1)}, u32[]{:S(2)}, u32[]{:S(2)}) collective-permute-start(bf16[1,12,16,128]{3,2,1,0:T(8,128)(2,1)S(1)} %bitcast.59), channel_id=1, source_target_pairs={{0,32},{32,0},{64,96},{96,64},{1,33},{33,1},{65,97},{97,65},{2,34}... | collective-permute-start | bytes 147464 | tf_op jit(solution)/shard_map/ppermute | solution.py:25
  93.7 7.2 %collective-permute-start.36 = (bf16[1,12,16,128]{3,2,1,0:T(8,128)(2,1)S(1)}, bf16[1,12,16,128]{3,2,1,0:T(8,128)(2,1)S(1)}, u32[]{:S(2)}, u32[]{:S(2)}) collective-permute-start(bf16[1,12,16,128]{3,2,1,0:T(8,128)(2,1)S(1)} %bitcast.55), channel_id=1, source_target_pairs={{0,96},{32,64},{64,32},{96,0},{1,97},{33,65},{65,33},{97,1},{2,98}... | collective-permute-start | bytes 147464 | tf_op jit(solution)/shard_map/ppermute | solution.py:25
  97.4 4.7 %collective-permute-start.31 = (bf16[2,12,16,128]{3,2,1,0:T(8,128)(2,1)S(1)}, bf16[2,12,16,128]{3,2,1,0:T(8,128)(2,1)S(1)}, u32[]{:S(2)}, u32[]{:S(2)}) collective-permute-start(bf16[2,12,16,128]{3,2,1,0:T(8,128)(2,1)S(1)} %pad_maximum_fusion.24), channel_id=1, source_target_pairs={{0,8},{8,0},{16,24},{24,16},{1,9},{9,1},{17,25},{25,17},{2,10},{10... | collective-permute-start | bytes 294920 | tf_op jit(solution)/shard_map/ppermute | solution.py:25
  97.6 5.9 %collective-permute-start.28 = (bf16[2,12,16,128]{3,2,1,0:T(8,128)(2,1)S(1)}, bf16[2,12,16,128]{3,2,1,0:T(8,128)(2,1)S(1)}, u32[]{:S(2)}, u32[]{:S(2)}) collective-permute-start(bf16[2,12,16,128]{3,2,1,0:T(8,128)(2,1)S(1)} %pad_maximum_fusion.23), channel_id=1, source_target_pairs={{0,24},{8,16},{16,8},{24,0},{1,25},{9,17},{17,9},{25,1},{2,26},{10... | collective-permute-start | bytes 294920 | tf_op jit(solution)/shard_map/ppermute | solution.py:25
  99.8 5.9 %collective-permute-start.34 = (bf16[2,12,16,128]{3,2,1,0:T(8,128)(2,1)S(1)}, bf16[2,12,16,128]{3,2,1,0:T(8,128)(2,1)S(1)}, u32[]{:S(2)}, u32[]{:S(2)}) collective-permute-start(bf16[2,12,16,128]{3,2,1,0:T(8,128)(2,1)S(1)} %pad_maximum_fusion.25), channel_id=1, source_target_pairs={{0,96},{32,64},{64,32},{96,0},{1,97},{33,65},{65,33},{97,1},{2,98}... | collective-permute-start | bytes 294920 | tf_op jit(solution)/shard_map/ppermute | solution.py:25
  100.9 4.9 %collective-permute-start.37 = (bf16[2,12,16,128]{3,2,1,0:T(8,128)(2,1)S(1)}, bf16[2,12,16,128]{3,2,1,0:T(8,128)(2,1)S(1)}, u32[]{:S(2)}, u32[]{:S(2)}) collective-permute-start(bf16[2,12,16,128]{3,2,1,0:T(8,128)(2,1)S(1)} %pad_maximum_fusion.26), channel_id=1, source_target_pairs={{0,32},{32,0},{64,96},{96,64},{1,33},{33,1},{65,97},{97,65},{2,34}... | collective-permute-start | bytes 294920 | tf_op jit(solution)/shard_map/ppermute | solution.py:25
  102.2 7.0 %collective-permute-start.32 = (bf16[4,12,16,128]{3,2,1,0:T(8,128)(2,1)S(1)}, bf16[4,12,16,128]{3,2,1,0:T(8,128)(2,1)S(1)}, u32[]{:S(2)}, u32[]{:S(2)}) collective-permute-start(bf16[4,12,16,128]{3,2,1,0:T(8,128)(2,1)S(1)} %pad_maximum_fusion.13), channel_id=1, source_target_pairs={{0,96},{32,64},{64,32},{96,0},{1,97},{33,65},{65,33},{97,1},{2,98}... | collective-permute-start | bytes 589832 | tf_op jit(solution)/shard_map/ppermute | solution.py:25
  103.5 5.7 %collective-permute-start.29 = (bf16[4,12,16,128]{3,2,1,0:T(8,128)(2,1)S(1)}, bf16[4,12,16,128]{3,2,1,0:T(8,128)(2,1)S(1)}, u32[]{:S(2)}, u32[]{:S(2)}) collective-permute-start(bf16[4,12,16,128]{3,2,1,0:T(8,128)(2,1)S(1)} %pad_maximum_fusion.12), channel_id=1, source_target_pairs={{0,32},{32,0},{64,96},{96,64},{1,33},{33,1},{65,97},{97,65},{2,34}... | collective-permute-start | bytes 589832 | tf_op jit(solution)/shard_map/ppermute | solution.py:25
  105.7 5.8 %collective-permute-start.35 = (bf16[4,12,16,128]{3,2,1,0:T(8,128)(2,1)S(1)}, bf16[4,12,16,128]{3,2,1,0:T(8,128)(2,1)S(1)}, u32[]{:S(2)}, u32[]{:S(2)}) collective-permute-start(bf16[4,12,16,128]{3,2,1,0:T(8,128)(2,1)S(1)} %pad_maximum_fusion.14), channel_id=1, source_target_pairs={{0,8},{8,0},{16,24},{24,16},{1,9},{9,1},{17,25},{25,17},{2,10},{10... | collective-permute-start | bytes 589832 | tf_op jit(solution)/shard_map/ppermute | solution.py:25
  105.9 7.2 %collective-permute-start.38 = (bf16[4,12,16,128]{3,2,1,0:T(8,128)(2,1)S(1)}, bf16[4,12,16,128]{3,2,1,0:T(8,128)(2,1)S(1)}, u32[]{:S(2)}, u32[]{:S(2)}) collective-permute-start(bf16[4,12,16,128]{3,2,1,0:T(8,128)(2,1)S(1)} %pad_maximum_fusion.15), channel_id=1, source_target_pairs={{0,24},{8,16},{16,8},{24,0},{1,25},{9,17},{17,9},{25,1},{2,26},{10... | collective-permute-start | bytes 589832 | tf_op jit(solution)/shard_map/ppermute | solution.py:25
  113.1 9.1 %collective-permute-start.39 = (bf16[8,12,16,128]{3,2,1,0:T(8,128)(2,1)S(1)}, bf16[8,12,16,128]{3,2,1,0:T(8,128)(2,1)S(1)}, u32[]{:S(2)}, u32[]{:S(2)}) collective-permute-start(bf16[8,12,16,128]{3,2,1,0:T(8,128)(2,1)S(1)} %pad_maximum_fusion.4.refs_2_), channel_id=1, source_target_pairs={{0,96},{32,64},{64,32},{96,0},{1,97},{33,65},{65,33},{97,1},{2,98}... | collective-permute-start | bytes 1179656 | tf_op jit(solution)/shard_map/ppermute | solution.py:25
  115.5 7.8 %collective-permute-start.40 = (bf16[8,12,16,128]{3,2,1,0:T(8,128)(2,1)S(1)}, bf16[8,12,16,128]{3,2,1,0:T(8,128)(2,1)S(1)}, u32[]{:S(2)}, u32[]{:S(2)}) collective-permute-start(bf16[8,12,16,128]{3,2,1,0:T(8,128)(2,1)S(1)} %pad_maximum_fusion.5.refs_4_), channel_id=1, source_target_pairs={{0,32},{32,0},{64,96},{96,64},{1,33},{33,1},{65,97},{97,65},{2,34}... | collective-permute-start | bytes 1179656 | tf_op jit(solution)/shard_map/ppermute | solution.py:25
  115.5 9.0 %collective-permute-start.41 = (bf16[8,12,16,128]{3,2,1,0:T(8,128)(2,1)S(1)}, bf16[8,12,16,128]{3,2,1,0:T(8,128)(2,1)S(1)}, u32[]{:S(2)}, u32[]{:S(2)}) collective-permute-start(bf16[8,12,16,128]{3,2,1,0:T(8,128)(2,1)S(1)} %pad_maximum_fusion.6.refs_6_), channel_id=1, source_target_pairs={{0,24},{8,16},{16,8},{24,0},{1,25},{9,17},{17,9},{25,1},{2,26},{10... | collective-permute-start | bytes 1179656 | tf_op jit(solution)/shard_map/ppermute | solution.py:25
  116.5 8.0 %collective-permute-start.42 = (bf16[8,12,16,128]{3,2,1,0:T(8,128)(2,1)S(1)}, bf16[8,12,16,128]{3,2,1,0:T(8,128)(2,1)S(1)}, u32[]{:S(2)}, u32[]{:S(2)}) collective-permute-start(bf16[8,12,16,128]{3,2,1,0:T(8,128)(2,1)S(1)} %pad_maximum_fusion.7.refs_8_), channel_id=1, source_target_pairs={{0,8},{8,0},{16,24},{24,16},{1,9},{9,1},{17,25},{25,17},{2,10},{10... | collective-permute-start | bytes 1179656 | tf_op jit(solution)/shard_map/ppermute | solution.py:25
  117.1 3.7 %copy-start.1 = (bf16[8,1,192,3072]{3,2,1,0:T(8,128)(2,1)S(1)}, bf16[8,1,192,3072]{3,2,1,0:T(8,128)(2,1)}, u32[]{:S(2)}) copy-start(bf16[8,1,192,3072]{3,2,1,0:T(8,128)(2,1)} %param.6) | copy-start | bytes 28311556
  129.8 2.6 %collective-permute-start.44 = (bf16[3,192,512]{2,1,0:T(8,128)(2,1)S(1)}, bf16[3,192,512]{2,1,0:T(8,128)(2,1)S(1)}, u32[]{:S(2)}, u32[]{:S(2)}) collective-permute-start(bf16[3,192,512]{2,1,0:T(8,128)(2,1)S(1)} %get-tuple-element.128), channel_id=1, source_target_pairs={{0,1},{1,0},{2,3},{3,2},{4,5},{5,4},{6,7},{7,6},{8,9},{9,8},{10,11... | collective-permute-start | bytes 1769480 | tf_op jit(solution)/shard_map/ppermute | solution.py:25
  129.9 49.0 %copy-start.2 = (f32[1,192,512]{2,1,0:T(8,128)S(1)}, f32[1,192,512]{2,1,0:T(8,128)}, u32[]{:S(2)}) copy-start(f32[1,192,512]{2,1,0:T(8,128)} %param.8) | copy-start | bytes 1179652
  131.9 4.9 %collective-permute-start.43 = (bf16[1,192,512]{2,1,0:T(8,128)(2,1)S(1)}, bf16[1,192,512]{2,1,0:T(8,128)(2,1)S(1)}, u32[]{:S(2)}, u32[]{:S(2)}) collective-permute-start(bf16[1,192,512]{2,1,0:T(8,128)(2,1)S(1)} %get-tuple-element.126), channel_id=1, source_target_pairs={{0,1},{1,0},{2,3},{3,2},{4,5},{5,4},{6,7},{7,6},{8,9},{9,8},{10,11... | collective-permute-start | bytes 589832 | tf_op jit(solution)/shard_map/ppermute | solution.py:25
  132.6 12.3 %collective-permute-start.47 = (bf16[192,512]{1,0:T(8,128)(2,1)S(1)}, bf16[192,512]{1,0:T(8,128)(2,1)S(1)}, u32[]{:S(2)}, u32[]{:S(2)}) collective-permute-start(bf16[192,512]{1,0:T(8,128)(2,1)S(1)} %get-tuple-element.132), channel_id=1, source_target_pairs={{0,6},{2,4},{4,2},{6,0},{1,7},{3,5},{5,3},{7,1},{8,14},{10,12},{12... | collective-permute-start | bytes 589832 | tf_op jit(solution)/shard_map/ppermute | solution.py:25
  135.2 9.7 %collective-permute-start.46 = (bf16[192,512]{1,0:T(8,128)(2,1)S(1)}, bf16[192,512]{1,0:T(8,128)(2,1)S(1)}, u32[]{:S(2)}, u32[]{:S(2)}) collective-permute-start(bf16[192,512]{1,0:T(8,128)(2,1)S(1)} %get-tuple-element.133), channel_id=1, source_target_pairs={{0,4},{2,6},{4,0},{6,2},{1,5},{3,7},{5,1},{7,3},{8,12},{10,14},{12... | collective-permute-start | bytes 589832 | tf_op jit(solution)/shard_map/ppermute | solution.py:25
  135.9 9.7 %collective-permute-start.45 = (bf16[192,512]{1,0:T(8,128)(2,1)S(1)}, bf16[192,512]{1,0:T(8,128)(2,1)S(1)}, u32[]{:S(2)}, u32[]{:S(2)}) collective-permute-start(bf16[192,512]{1,0:T(8,128)(2,1)S(1)} %get-tuple-element.134), channel_id=1, source_target_pairs={{0,2},{2,0},{4,6},{6,4},{1,3},{3,1},{5,7},{7,5},{8,10},{10,8},{12,... | collective-permute-start | bytes 589832 | tf_op jit(solution)/shard_map/ppermute | solution.py:25

commit v4 on v3

--- a/solution.py
+++ b/solution.py
@@ -99,41 +99,47 @@
 
 
 def multiply(masks, pos_ref, tile_ref, filled, other_ref, mine_ref):
-    def one(turn, carry):
-        rows = tile_ref[pos_ref[2] ^ (masks[0] + turn)]
-        vectors = filled[...].reshape(rows.shape[1], -1)
+    vectors = filled[...].reshape(tile_ref.shape[2], -1)
+    for turn, mask in enumerate(masks):
+        rows = tile_ref[pos_ref[2] ^ mask]
         result = jnp.dot(rows, vectors, preferred_element_type=F32).astype(BF16)
         for core in range(2):
             @pl.when(pos_ref[3] == core)
             def _():
                 mine_ref[turn] = result[core * 192:(core + 1) * 192]
                 other_ref[turn] = result[(1 - core) * 192:(2 - core) * 192]
-        return carry
-
-    lax.fori_loop(0, len(masks), one, 0)
-
-
-def far_product_kernel(by_columns, pos_ref, tile_ref, *rest):
+
+
+def first_product_kernel(by_columns, masks, pos_ref, tile_ref, *rest):
     bundles, (other_ref, mine_ref, filled) = rest[:8], rest[8:]
     fill_kernel(by_columns, pos_ref, bundles, filled)
-    multiply((1, 2, 3), pos_ref, tile_ref, filled, other_ref, mine_ref)
-
-
-def near_product_kernel(pos_ref, tile_ref, filled, other_ref, mine_ref):
-    multiply((0,), pos_ref, tile_ref, filled, other_ref, mine_ref)
-
-
-def product(tile, bundles, pos, by_columns):
-    far = jax.ShapeDtypeStruct((3, 192, 512), BF16)
-    near = jax.ShapeDtypeStruct((1, 192, 512), BF16)
+    multiply(masks, pos_ref, tile_ref, filled, other_ref, mine_ref)
+
+
+def sums_over_col(tile, bundles, pos, by_columns):
+    def out(masks):
+        return (jax.ShapeDtypeStruct((len(masks), 192, 512), BF16),) * 2
+
+    def later(masks, filled):
+        return whole_call(
+            lambda *refs: multiply(masks, *refs), out(masks), scalars=1, flops=len(masks) << 30
+        )(pos, tile, filled)
+
+    def send(both, masks):
+        other, mine = both
+        got = swap(other, "core", 1)
+        both = [mine[turn].astype(F32) + got[turn].astype(F32) for turn in range(len(masks))]
+        return both if masks == (0,) else [value.astype(BF16) for value in both]
+
     filled = jax.ShapeDtypeStruct((192, 16, 512), BF16)
-    other, mine, filled = whole_call(
-        lambda *refs: far_product_kernel(by_columns, *refs), (far, far, filled), scalars=1, flops=3 << 30
+    *across, filled = whole_call(
+        lambda *refs: first_product_kernel(by_columns, (2,), *refs), (*out((2,)), filled), scalars=1, flops=1 << 30
     )(pos, tile, *bundles)
-    other_near, mine_near = whole_call(near_product_kernel, (near, near), scalars=1, flops=1 << 30)(pos, tile, filled)
-    got = swap(other, "core", 1)
-    sent = [(mine[at].astype(F32) + got[at].astype(F32)).astype(BF16) for at in range(3)]
-    return sent, mine_near[0].astype(F32) + swap(other_near, "core", 1)[0].astype(F32)
+    beside = later((1, 3), filled)
+    across = send(across, (2,))
+    near = later((0,), after(across, filled))
+    beside, near = send(beside, (1, 3)), send(near, (0,))
+    return [swap(beside[0], "y", 1), swap(across[0], "y", 2), swap(beside[1], "y", 3)], near[0]
 
 
 def residual_kernel(before_ref, own_ref, *refs):
@@ -145,10 +151,6 @@
     for x in range(4):
         for z in range(4):
             sent_ref[x * 4 + z] = half[:, x * 128:(x + 1) * 128]
-
-
-def sums_over_y(sent):
-    return [swap(sent[mask - 1], "y", mask) for mask in (1, 2, 3)]
 
 
 def residual_of(before, near, sums):
@@ -239,19 +241,20 @@
             near["low"] = jnp.stack([start[0], first[0]])
             near["low_far"] = swap(near["low"], "x", 1)
         else:
-            near["high"] = after(held, near["second"])
+            near["tile"] = hold(rows)
+            near["high"] = after((held, near["tile"]), near["second"])
             near["high_far"] = swap(near["high"], "x", 3)
         return held
 
     half = start.astype(BF16).reshape(4, 3, 16, 512)
     bundles = gather_swaps([half[at] for at in range(4)], between)
     tile, bundles, low, high = lax.optimization_barrier(
-        (hold(rows), bundles, [near["low"], near["low_far"]], [near["high"], near["high_far"]])
+        (near["tile"], bundles, [near["low"], near["low_far"]], [near["high"], near["high_far"]])
     )
-    far, near = product(tile, bundles, pos, False)
     low, high = jnp.concatenate(low), jnp.concatenate(high)
     inverses = low, swap(low, "x", 3), high, swap(high, "x", 1)
-    sums, inverses = lax.optimization_barrier((sums_over_y(far), inverses))
+    sums, near = sums_over_col(tile, bundles, pos, False)
+    sums, inverses = lax.optimization_barrier((sums, inverses))
     lists = jnp.concatenate([bundle[:, 96, :3] for bundle in inverses]).astype(jnp.int32)
 
     residual, sent = residual_of(target, near, sums)
@@ -267,8 +270,8 @@
 
     bundles = gather_swaps(quarters, between)
     tile, bundles = lax.optimization_barrier((hold(held[0]), bundles))
-    far, near = product(tile, bundles, pos, True)
-    residual, sent = residual_of(residual, near, sums_over_y(far))
+    sums, near = sums_over_col(tile, bundles, pos, True)
+    residual, sent = residual_of(residual, near, sums)
     sent = solve(exchange(sent), inverses, lists, counts, pos, fix)
     pieces = lax.all_to_all(sent, ("x", "z"), 0, 0, tiled=True)
     result = whole_call(join_kernel, jax.ShapeDtypeStruct((192, 512), F32))(start, pieces)

time: 180 us -> 179 us (level)
  waiting for transfers between devices: 54.5 us -> 51 us
    ppermute x48 -> x50, waiting for transfers between devices: 40.6 us -> 36.9 us  [swap(): return lax.ppermute(value, axis, [(i, i ^ mask) for i in range(size)])]
    pallas_call x10 -> x12, Pallas kernels: 20.1 us -> 21.2 us  [call(): pl.pallas_call(body, in_specs=[SMEM] * scalars + [VMEM] * (len(args) - sc...]
    ppermute x48 -> x50, starting transfers between devices: 55.3 us -> 55.9 us  [swap(): return lax.ppermute(value, axis, [(i, i ^ mask) for i in range(size)])]
  transfers between devices with their start and end apart: 49 -> 51, of which waited for: 22 -> 20; matrix products, arithmetic and copies ran while one was open for 1% -> 1% of each run, Pallas kernels for 3% -> 8%
where the time goes in v4:
time: 179 us
  starting transfers between devices  60.7 us (34%)
  waiting for transfers between devices  51 us (28%)
  blocking collectives  32 us (18%)
  Pallas kernels  22.5 us (13%)
  local copies, waits for them, and re-layouts  9.26 us (5%)
  other arithmetic  2.19 us (1%)
    ppermute x50, starting transfers between devices, swap(): return lax.ppermute(value, axis, [(i, i ^ mask) for i in range(size)])  55.9 us
    ppermute x50, waiting for transfers between devices, swap(): return lax.ppermute(value, axis, [(i, i ^ mask) for i in range(size)])  36.9 us
    pallas_call x12, Pallas kernels, call(): pl.pallas_call(body, in_specs=[SMEM] * scalars + [VMEM] * (len(args) - sc...  21.2 us
    all_to_all x1, blocking collectives, exchange(): return lax.all_to_all(sent, ('x', 'z'), 0, 0, tiled=True).reshape(3072, 128)  20.5 us
    all_to_all x1, waiting for transfers between devices, exchange(): return lax.all_to_all(sent, ('x', 'z'), 0, 0, tiled=True).reshape(3072, 128)  14.1 us
    all_to_all x1, blocking collectives, body(): pieces = lax.all_to_all(sent, ('x', 'z'), 0, 0, tiled=True)  11.6 us
    unnamed x18, local copies, waits for them, and re-layouts  9.14 us
    all_to_all x1, starting transfers between devices, exchange(): return lax.all_to_all(sent, ('x', 'z'), 0, 0, tiled=True).reshape(3072, 128)  4.84 us
  transfers between devices with their start and end apart: 51, of which 20 were waited for; matrix products, arithmetic and copies ran while one was open for 1% of the time, Pallas kernels for 8%

profile of v4, /device:TPU:0, one launch (start us, length us, event | category | flops | bytes accessed | tf_op | source)
XLA Modules:
  0.0 178.8 jit_solution(2658091724383994085)
XLA Ops:
  0.6 1.0 bitcast_convert_fusion
  1.7 1.7 collective-permute-start.8
  3.3 2.1 %collective-permute-start.12 = (bf16[1,3,16,512]{3,2,1,0:T(8,128)(2,1)S(1)}, bf16[1,3,16,512]{3,2,1,0:T(8,128)(2,1)S(1)}, u32[]{:S(2)}, u32[]{:S(2)}) collective-permute-start(bf16[1,3,16,512]{3,2,1,0:T(8,128)(2,1)S(1)} %bitcast.80), channel_id=1, source_target_pairs={{0,96},{32,64},{64,32},{96,0},{1,97},{33,65},{65,33},{97,1},{2,98}... | collective-permute-start | bytes 147464 | tf_op jit(solution)/shard_map/ppermute | solution.py:25
  5.4 4.0 %collective-permute-start.4 = (bf16[1,3,16,512]{3,2,1,0:T(8,128)(2,1)S(1)}, bf16[1,3,16,512]{3,2,1,0:T(8,128)(2,1)S(1)}, u32[]{:S(2)}, u32[]{:S(2)}) collective-permute-start(bf16[1,3,16,512]{3,2,1,0:T(8,128)(2,1)S(1)} %bitcast.84), channel_id=1, source_target_pairs={{0,24},{8,16},{16,8},{24,0},{1,25},{9,17},{17,9},{25,1},{2,26},{10... | collective-permute-start | bytes 147464 | tf_op jit(solution)/shard_map/ppermute | solution.py:25
  9.5 1.1 copy-done.3
  11.9 1.2 collective-permute-start.9
  13.3 2.1 %collective-permute-start.5 = (bf16[2,3,16,512]{3,2,1,0:T(8,128)(2,1)S(1)}, bf16[2,3,16,512]{3,2,1,0:T(8,128)(2,1)S(1)}, u32[]{:S(2)}, u32[]{:S(2)}) collective-permute-start(bf16[2,3,16,512]{3,2,1,0:T(8,128)(2,1)S(1)} %pad_maximum_fusion.20), channel_id=1, source_target_pairs={{0,8},{8,0},{16,24},{24,16},{1,9},{9,1},{17,25},{25,17},{2,10},{10... | collective-permute-start | bytes 294920 | tf_op jit(solution)/shard_map/ppermute | solution.py:25
  15.5 1.0 collective-permute-start.16
  16.5 1.3 collective-permute-done.9
  17.8 2.1 %collective-permute-start.10 = (bf16[4,3,16,512]{3,2,1,0:T(8,128)(2,1)S(1)}, bf16[4,3,16,512]{3,2,1,0:T(8,128)(2,1)S(1)}, u32[]{:S(2)}, u32[]{:S(2)}) collective-permute-start(bf16[4,3,16,512]{3,2,1,0:T(8,128)(2,1)S(1)} %pad_maximum_fusion.10), channel_id=1, source_target_pairs={{0,8},{8,0},{16,24},{24,16},{1,9},{9,1},{17,25},{25,17},{2,10},{10... | collective-permute-start | bytes 589832 | tf_op jit(solution)/shard_map/ppermute | solution.py:25
  20.0 1.1 collective-permute-start.14
  21.1 2.2 %collective-permute-start.6 = (bf16[4,3,16,512]{3,2,1,0:T(8,128)(2,1)S(1)}, bf16[4,3,16,512]{3,2,1,0:T(8,128)(2,1)S(1)}, u32[]{:S(2)}, u32[]{:S(2)}) collective-permute-start(bf16[4,3,16,512]{3,2,1,0:T(8,128)(2,1)S(1)} %pad_maximum_fusion.9), channel_id=1, source_target_pairs={{0,96},{32,64},{64,32},{96,0},{1,97},{33,65},{65,33},{97,1},{2,98}... | collective-permute-start | bytes 589832 | tf_op jit(solution)/shard_map/ppermute | solution.py:25
  23.3 1.5 collective-permute-start.2
  25.4 3.9 %collective-permute-done.2 = bf16[4,3,16,512]{3,2,1,0:T(8,128)(2,1)S(1)} collective-permute-done((bf16[4,3,16,512]{3,2,1,0:T(8,128)(2,1)S(1)}, bf16[4,3,16,512]{3,2,1,0:T(8,128)(2,1)S(1)}, u32[]{:S(2)}, u32[]{:S(2)}) %collective-permute-start.2) | collective-permute-done | bytes 196640 | tf_op jit(solution)/shard_map/ppermute | solution.py:25
  29.4 0.9 collective-permute-start.3
  30.4 1.9 %collective-permute-start.7 = (bf16[8,3,16,512]{3,2,1,0:T(8,128)(2,1)S(1)}, bf16[8,3,16,512]{3,2,1,0:T(8,128)(2,1)S(1)}, u32[]{:S(2)}, u32[]{:S(2)}) collective-permute-start(bf16[8,3,16,512]{3,2,1,0:T(8,128)(2,1)S(1)} %pad_maximum_fusion.1.refs_4_), channel_id=1, source_target_pairs={{0,32},{32,0},{64,96},{96,64},{1,33},{33,1},{65,97},{97,65},{2,34}... | collective-permute-start | bytes 1179656 | tf_op jit(solution)/shard_map/ppermute | solution.py:25
  33.3 2.1 %collective-permute-start.17 = (bf16[2,112,384]{2,1,0:T(8,128)(2,1)S(1)}, bf16[2,112,384]{2,1,0:T(8,128)(2,1)S(1)}, u32[]{:S(2)}, u32[]{:S(2)}) collective-permute-start(bf16[2,112,384]{2,1,0:T(8,128)(2,1)S(1)} %pad_maximum_fusion.17), channel_id=1, source_target_pairs={{0,32},{32,0},{64,96},{96,64},{1,33},{33,1},{65,97},{97,65},{2,34}... | collective-permute-start | bytes 516104 | tf_op jit(solution)/shard_map/ppermute | solution.py:25
  35.4 3.7 %copy-done = bf16[8,1,192,3072]{3,2,1,0:T(8,128)(2,1)S(1)} copy-done((bf16[8,1,192,3072]{3,2,1,0:T(8,128)(2,1)S(1)}, bf16[8,1,192,3072]{3,2,1,0:T(8,128)(2,1)}, u32[]{:S(2)}) %copy-start) | copy-done | bytes 9437208
  39.8 1.4 collective-permute-done.17
  41.1 1.7 collective-permute-start.19
  42.8 4.9 %collective-permute-done.19 = bf16[2,112,384]{2,1,0:T(8,128)(2,1)S(1)} collective-permute-done((bf16[2,112,384]{2,1,0:T(8,128)(2,1)S(1)}, bf16[2,112,384]{2,1,0:T(8,128)(2,1)S(1)}, u32[]{:S(2)}, u32[]{:S(2)}) %collective-permute-start.19) | collective-permute-done | bytes 172064 | tf_op jit(solution)/shard_map/ppermute | solution.py:25
  48.1 2.2 %shard_map.79 = (bf16[1,192,512]{2,1,0:T(8,128)(2,1)S(1)}, bf16[1,192,512]{2,1,0:T(8,128)(2,1)S(1)}, bf16[192,16,512]{2,1,0:T(8,128)(2,1)S(1)}) custom-call(s32[4]{0:T(128)S(1)} %pad_add_fusion.pos_ref.refs_0_, bf16[4,384,3072]{2,1,0:T(8,128)(2,1)S(1)} %shard_map.77.refs_1_, bf16[8,3,16,512]{3,2,1,0:T(8,128)(2,1)S(1)} %pad_maximum_fusion.refs_2_, ...), custom_call_target="tpu_custom_call" | custom-call | flops 1073741824 | bytes 1048576 | tf_op jit(solution)/shard_map/pallas_call | solution.py:30
  50.4 3.4 %shard_map.80 = (bf16[2,192,512]{2,1,0:T(8,128)(2,1)S(1)}, bf16[2,192,512]{2,1,0:T(8,128)(2,1)S(1)}) custom-call(s32[4]{0:T(128)S(1)} %pad_add_fusion.pos_ref.refs_0_, bf16[4,384,3072]{2,1,0:T(8,128)(2,1)S(1)} %shard_map.77.refs_1_, bf16[192,16,512]{2,1,0:T(8,128)(2,1)S(1)} %get-tuple-element.107.refs_2_), custom_call_target="tpu_custom_call" | custom-call | flops 2147483648 | bytes 1048576 | tf_op jit(solution)/shard_map/pallas_call | solution.py:30
  54.4 1.8 collective-permute-start.25
  56.2 3.3 %collective-permute-start.23 = (bf16[192,512]{1,0:T(8,128)(2,1)S(1)}, bf16[192,512]{1,0:T(8,128)(2,1)S(1)}, u32[]{:S(2)}, u32[]{:S(2)}) collective-permute-start(bf16[192,512]{1,0:T(8,128)(2,1)S(1)} %fusion.1), channel_id=1, source_target_pairs={{0,4},{2,6},{4,0},{6,2},{1,5},{3,7},{5,1},{7,3},{8,12},{10,14},{12... | collective-permute-start | bytes 589832 | tf_op jit(solution)/shard_map/ppermute | solution.py:25
  59.5 2.0 %shard_map.81 = (bf16[1,192,512]{2,1,0:T(8,128)(2,1)S(1)}, bf16[1,192,512]{2,1,0:T(8,128)(2,1)S(1)}) custom-call(s32[4]{0:T(128)S(1)} %pad_add_fusion.pos_ref.refs_0_, bf16[4,384,3072]{2,1,0:T(8,128)(2,1)S(1)} %shard_map.77.refs_1_, bf16[192,16,512]{2,1,0:T(8,128)(2,1)S(1)} %get-tuple-element.107.refs_2_), custom_call_target="tpu_custom_call" | custom-call | flops 1073741824 | bytes 1048576 | tf_op jit(solution)/shard_map/pallas_call | solution.py:30
  61.7 1.1 collective-permute-start.24
  63.7 2.0 %collective-permute-done.25.refs_5_ = bf16[4,112,384]{2,1,0:T(8,128)(2,1)S(1)} collective-permute-done((bf16[4,112,384]{2,1,0:T(8,128)(2,1)S(1)}, bf16[4,112,384]{2,1,0:T(8,128)(2,1)S(1)}, u32[]{:S(2)}, u32[]{:S(2)}) %collective-permute-start.25) | collective-permute-done | bytes 344096 | tf_op jit(solution)/shard_map/ppermute | solution.py:25
  65.7 4.6 %collective-permute-done.24.refs_2_ = bf16[192,512]{1,0:T(8,128)(2,1)S(1)} collective-permute-done((bf16[192,512]{1,0:T(8,128)(2,1)S(1)}, bf16[192,512]{1,0:T(8,128)(2,1)S(1)}, u32[]{:S(2)}, u32[]{:S(2)}) %collective-permute-start.24) | collective-permute-done | bytes 196640 | tf_op jit(solution)/shard_map/ppermute | solution.py:25
  70.3 1.1 shard_map.82
  71.4 4.8 %all-to-all-start = ((bf16[16,192,128]{2,1,0:T(8,128)(2,1)}), bf16[16,192,128]{2,1,0:T(8,128)(2,1)S(1)}, u32[]{:S(2)}, u32[]{:S(2)}) async-start(bf16[16,192,128]{2,1,0:T(8,128)(2,1)} %get-tuple-element.114), calls=%async_computation | async-start | bytes 1572864 | tf_op jit(solution)/shard_map/all_to_all | solution.py:162
  76.3 14.1 %all-to-all-done = bf16[16,192,128]{2,1,0:T(8,128)(2,1)S(1)} async-done(((bf16[16,192,128]{2,1,0:T(8,128)(2,1)}), bf16[16,192,128]{2,1,0:T(8,128)(2,1)S(1)}, u32[]{:S(2)}, u32[]{:S(2)}) %all-to-all-start) | async-done | bytes 786464 | tf_op jit(solution)/shard_map/all_to_all | solution.py:162
  90.4 1.2 shard_map.83
  91.6 0.8 collective-permute-start.31
  92.7 0.7 collective-permute-start.34
  93.4 1.6 collective-permute-start.37
  95.0 2.1 %collective-permute-done.31 = bf16[1,12,16,128]{3,2,1,0:T(8,128)(2,1)S(1)} collective-permute-done((bf16[1,12,16,128]{3,2,1,0:T(8,128)(2,1)S(1)}, bf16[1,12,16,128]{3,2,1,0:T(8,128)(2,1)S(1)}, u32[]{:S(2)}, u32[]{:S(2)}) %collective-permute-start.31) | collective-permute-done | bytes 49184 | tf_op jit(solution)/shard_map/ppermute | solution.py:25
  97.2 2.5 %collective-permute-start.29 = (bf16[2,12,16,128]{3,2,1,0:T(8,128)(2,1)S(1)}, bf16[2,12,16,128]{3,2,1,0:T(8,128)(2,1)S(1)}, u32[]{:S(2)}, u32[]{:S(2)}) collective-permute-start(bf16[2,12,16,128]{3,2,1,0:T(8,128)(2,1)S(1)} %pad_maximum_fusion.23), channel_id=1, source_target_pairs={{0,24},{8,16},{16,8},{24,0},{1,25},{9,17},{17,9},{25,1},{2,26},{10... | collective-permute-start | bytes 294920 | tf_op jit(solution)/shard_map/ppermute | solution.py:25
  99.7 0.8 collective-permute-start.35
  100.5 0.9 collective-permute-start.38
  101.8 1.5 collective-permute-start.33
  103.3 1.5 collective-permute-start.30
  104.7 0.9 collective-permute-done.35
  105.8 2.3 %collective-permute-start.39 = (bf16[4,12,16,128]{3,2,1,0:T(8,128)(2,1)S(1)}, bf16[4,12,16,128]{3,2,1,0:T(8,128)(2,1)S(1)}, u32[]{:S(2)}, u32[]{:S(2)}) collective-permute-start(bf16[4,12,16,128]{3,2,1,0:T(8,128)(2,1)S(1)} %pad_maximum_fusion.15), channel_id=1, source_target_pairs={{0,24},{8,16},{16,8},{24,0},{1,25},{9,17},{17,9},{25,1},{2,26},{10... | collective-permute-start | bytes 589832 | tf_op jit(solution)/shard_map/ppermute | solution.py:25
  109.1 2.3 %collective-permute-done.36 = bf16[4,12,16,128]{3,2,1,0:T(8,128)(2,1)S(1)} collective-permute-done((bf16[4,12,16,128]{3,2,1,0:T(8,128)(2,1)S(1)}, bf16[4,12,16,128]{3,2,1,0:T(8,128)(2,1)S(1)}, u32[]{:S(2)}, u32[]{:S(2)}) %collective-permute-start.36) | collective-permute-done | bytes 196640 | tf_op jit(solution)/shard_map/ppermute | solution.py:25
  111.4 1.7 collective-permute-done.39
  113.2 2.1 %collective-permute-start.40 = (bf16[8,12,16,128]{3,2,1,0:T(8,128)(2,1)S(1)}, bf16[8,12,16,128]{3,2,1,0:T(8,128)(2,1)S(1)}, u32[]{:S(2)}, u32[]{:S(2)}) collective-permute-start(bf16[8,12,16,128]{3,2,1,0:T(8,128)(2,1)S(1)} %pad_maximum_fusion.4.refs_2_), channel_id=1, source_target_pairs={{0,96},{32,64},{64,32},{96,0},{1,97},{33,65},{65,33},{97,1},{2,98}... | collective-permute-start | bytes 1179656 | tf_op jit(solution)/shard_map/ppermute | solution.py:25
  115.2 0.9 collective-permute-start.42
  116.6 3.7 %copy-done.1 = bf16[8,1,192,3072]{3,2,1,0:T(8,128)(2,1)S(1)} copy-done((bf16[8,1,192,3072]{3,2,1,0:T(8,128)(2,1)S(1)}, bf16[8,1,192,3072]{3,2,1,0:T(8,128)(2,1)}, u32[]{:S(2)}) %copy-start.1) | copy-done | bytes 9437208
  120.9 1.3 collective-permute-done.40.refs_3_
  122.2 0.8 collective-permute-done.41.refs_5_
  123.0 1.2 collective-permute-done.42.refs_7_
  124.2 2.5 %shard_map.85 = (bf16[1,192,512]{2,1,0:T(8,128)(2,1)S(1)}, bf16[1,192,512]{2,1,0:T(8,128)(2,1)S(1)}, bf16[192,16,512]{2,1,0:T(8,128)(2,1)S(1)}) custom-call(s32[4]{0:T(128)S(1)} %pad_add_fusion.pos_ref.refs_0_, bf16[4,384,3072]{2,1,0:T(8,128)(2,1)S(1)} %shard_map.84.refs_1_, bf16[8,12,16,128]{3,2,1,0:T(8,128)(2,1)S(1)} %pad_maximum_fusion.4.refs_2_, ...), custom_call_target="tpu_custom_call" | custom-call | flops 1073741824 | bytes 1048576 | tf_op jit(solution)/shard_map/pallas_call | solution.py:30
  126.8 3.4 %shard_map.87 = (bf16[2,192,512]{2,1,0:T(8,128)(2,1)S(1)}, bf16[2,192,512]{2,1,0:T(8,128)(2,1)S(1)}) custom-call(s32[4]{0:T(128)S(1)} %pad_add_fusion.pos_ref.refs_0_, bf16[4,384,3072]{2,1,0:T(8,128)(2,1)S(1)} %shard_map.84.refs_1_, bf16[192,16,512]{2,1,0:T(8,128)(2,1)S(1)} %get-tuple-element.136.refs_2_), custom_call_target="tpu_custom_call" | custom-call | flops 2147483648 | bytes 1048576 | tf_op jit(solution)/shard_map/pallas_call | solution.py:30
  130.9 2.3 %collective-permute-start.48 = (bf16[192,512]{1,0:T(8,128)(2,1)S(1)}, bf16[192,512]{1,0:T(8,128)(2,1)S(1)}, u32[]{:S(2)}, u32[]{:S(2)}) collective-permute-start(bf16[192,512]{1,0:T(8,128)(2,1)S(1)} %fusion.3), channel_id=1, source_target_pairs={{0,4},{2,6},{4,0},{6,2},{1,5},{3,7},{5,1},{7,3},{8,12},{10,14},{12... | collective-permute-start | bytes 589832 | tf_op jit(solution)/shard_map/ppermute | solution.py:25
  133.1 2.0 %shard_map.86 = (bf16[1,192,512]{2,1,0:T(8,128)(2,1)S(1)}, bf16[1,192,512]{2,1,0:T(8,128)(2,1)S(1)}) custom-call(s32[4]{0:T(128)S(1)} %pad_add_fusion.pos_ref.refs_0_, bf16[4,384,3072]{2,1,0:T(8,128)(2,1)S(1)} %shard_map.84.refs_1_, bf16[192,16,512]{2,1,0:T(8,128)(2,1)S(1)} %get-tuple-element.136.refs_2_), custom_call_target="tpu_custom_call" | custom-call | flops 1073741824 | bytes 1048576 | tf_op jit(solution)/shard_map/pallas_call | solution.py:30
  135.3 1.0 collective-permute-start.49
  136.8 2.5 %collective-permute-done.48.refs_1_ = bf16[192,512]{1,0:T(8,128)(2,1)S(1)} collective-permute-done((bf16[192,512]{1,0:T(8,128)(2,1)S(1)}, bf16[192,512]{1,0:T(8,128)(2,1)S(1)}, u32[]{:S(2)}, u32[]{:S(2)}) %collective-permute-start.48) | collective-permute-done | bytes 196640 | tf_op jit(solution)/shard_map/ppermute | solution.py:25
  139.3 4.6 %collective-permute-done.49.refs_2_ = bf16[192,512]{1,0:T(8,128)(2,1)S(1)} collective-permute-done((bf16[192,512]{1,0:T(8,128)(2,1)S(1)}, bf16[192,512]{1,0:T(8,128)(2,1)S(1)}, u32[]{:S(2)}, u32[]{:S(2)}) %collective-permute-start.49) | collective-permute-done | bytes 196640 | tf_op jit(solution)/shard_map/ppermute | solution.py:25
  143.9 0.9 shard_map.88
  144.8 20.5 %all_to_all.15 = bf16[16,192,128]{2,1,0:T(8,128)(2,1)S(1)} all-to-all(bf16[16,192,128]{2,1,0:T(8,128)(2,1)S(1)} %get-tuple-element.141), channel_id=1, replica_groups=mesh['x'=4,'z'=4,'y'=4,'core'=2] {'x','z'}, dimensions={0} | all-to-all | bytes 1572864 | tf_op jit(solution)/shard_map/all_to_all | solution.py:162
  165.2 1.2 shard_map.89
  166.5 11.6 %all_to_all.16.pieces_ref = bf16[16,48,128]{2,1,0:T(8,128)(2,1)S(1)} all-to-all(bf16[16,48,128]{2,1,0:T(8,128)(2,1)S(1)} %shard_map.89), channel_id=1, replica_groups=mesh['x'=4,'z'=4,'y'=4,'core'=2] {'x','z'}, dimensions={0} | all-to-all | bytes 393216 | tf_op jit(solution)/shard_map/all_to_all | solution.py:276
  178.0 0.8 shard_map.90
  (116 shorter events, 10.7 us)
Async XLA Ops:
  1.7 10.2 %collective-permute-start.8 = (bf16[1,3,16,512]{3,2,1,0:T(8,128)(2,1)S(1)}, bf16[1,3,16,512]{3,2,1,0:T(8,128)(2,1)S(1)}, u32[]{:S(2)}, u32[]{:S(2)}) collective-permute-start(bf16[1,3,16,512]{3,2,1,0:T(8,128)(2,1)S(1)} %bitcast.76), channel_id=1, source_target_pairs={{0,32},{32,0},{64,96},{96,64},{1,33},{33,1},{65,97},{97,65},{2,34}... | collective-permute-start | bytes 147464 | tf_op jit(solution)/shard_map/ppermute | solution.py:25
  3.3 9.8 %collective-permute-start.12 = (bf16[1,3,16,512]{3,2,1,0:T(8,128)(2,1)S(1)}, bf16[1,3,16,512]{3,2,1,0:T(8,128)(2,1)S(1)}, u32[]{:S(2)}, u32[]{:S(2)}) collective-permute-start(bf16[1,3,16,512]{3,2,1,0:T(8,128)(2,1)S(1)} %bitcast.80), channel_id=1, source_target_pairs={{0,96},{32,64},{64,32},{96,0},{1,97},{33,65},{65,33},{97,1},{2,98}... | collective-permute-start | bytes 147464 | tf_op jit(solution)/shard_map/ppermute | solution.py:25
  5.4 7.8 %collective-permute-start.4 = (bf16[1,3,16,512]{3,2,1,0:T(8,128)(2,1)S(1)}, bf16[1,3,16,512]{3,2,1,0:T(8,128)(2,1)S(1)}, u32[]{:S(2)}, u32[]{:S(2)}) collective-permute-start(bf16[1,3,16,512]{3,2,1,0:T(8,128)(2,1)S(1)} %bitcast.84), channel_id=1, source_target_pairs={{0,24},{8,16},{16,8},{24,0},{1,25},{9,17},{17,9},{25,1},{2,26},{10... | collective-permute-start | bytes 147464 | tf_op jit(solution)/shard_map/ppermute | solution.py:25
  9.5 5.9 %collective-permute-start = (bf16[1,3,16,512]{3,2,1,0:T(8,128)(2,1)S(1)}, bf16[1,3,16,512]{3,2,1,0:T(8,128)(2,1)S(1)}, u32[]{:S(2)}, u32[]{:S(2)}) collective-permute-start(bf16[1,3,16,512]{3,2,1,0:T(8,128)(2,1)S(1)} %bitcast.88), channel_id=1, source_target_pairs={{0,8},{8,0},{16,24},{24,16},{1,9},{9,1},{17,25},{25,17},{2,10},{10... | collective-permute-start | bytes 147464 | tf_op jit(solution)/shard_map/ppermute | solution.py:25
  9.5 1.1 copy-start.3
  10.6 0.7 copy-start.6
  11.9 5.9 %collective-permute-start.9 = (bf16[2,3,16,512]{3,2,1,0:T(8,128)(2,1)S(1)}, bf16[2,3,16,512]{3,2,1,0:T(8,128)(2,1)S(1)}, u32[]{:S(2)}, u32[]{:S(2)}) collective-permute-start(bf16[2,3,16,512]{3,2,1,0:T(8,128)(2,1)S(1)} %pad_maximum_fusion.21), channel_id=1, source_target_pairs={{0,96},{32,64},{64,32},{96,0},{1,97},{33,65},{65,33},{97,1},{2,98}... | collective-permute-start | bytes 294920 | tf_op jit(solution)/shard_map/ppermute | solution.py:25
  13.1 6.8 %collective-permute-start.13 = (bf16[2,3,16,512]{3,2,1,0:T(8,128)(2,1)S(1)}, bf16[2,3,16,512]{3,2,1,0:T(8,128)(2,1)S(1)}, u32[]{:S(2)}, u32[]{:S(2)}) collective-permute-start(bf16[2,3,16,512]{3,2,1,0:T(8,128)(2,1)S(1)} %pad_maximum_fusion.22), channel_id=1, source_target_pairs={{0,32},{32,0},{64,96},{96,64},{1,33},{33,1},{65,97},{97,65},{2,34}... | collective-permute-start | bytes 294920 | tf_op jit(solution)/shard_map/ppermute | solution.py:25
  13.3 7.8 %collective-permute-start.5 = (bf16[2,3,16,512]{3,2,1,0:T(8,128)(2,1)S(1)}, bf16[2,3,16,512]{3,2,1,0:T(8,128)(2,1)S(1)}, u32[]{:S(2)}, u32[]{:S(2)}) collective-permute-start(bf16[2,3,16,512]{3,2,1,0:T(8,128)(2,1)S(1)} %pad_maximum_fusion.20), channel_id=1, source_target_pairs={{0,8},{8,0},{16,24},{24,16},{1,9},{9,1},{17,25},{25,17},{2,10},{10... | collective-permute-start | bytes 294920 | tf_op jit(solution)/shard_map/ppermute | solution.py:25
  15.4 7.9 %collective-permute-start.1 = (bf16[2,3,16,512]{3,2,1,0:T(8,128)(2,1)S(1)}, bf16[2,3,16,512]{3,2,1,0:T(8,128)(2,1)S(1)}, u32[]{:S(2)}, u32[]{:S(2)}) collective-permute-start(bf16[2,3,16,512]{3,2,1,0:T(8,128)(2,1)S(1)} %pad_maximum_fusion.19), channel_id=1, source_target_pairs={{0,24},{8,16},{16,8},{24,0},{1,25},{9,17},{17,9},{25,1},{2,26},{10... | collective-permute-start | bytes 294920 | tf_op jit(solution)/shard_map/ppermute | solution.py:25
  15.5 9.3 %collective-permute-start.16 = (bf16[2,112,384]{2,1,0:T(8,128)(2,1)S(1)}, bf16[2,112,384]{2,1,0:T(8,128)(2,1)S(1)}, u32[]{:S(2)}, u32[]{:S(2)}) collective-permute-start(bf16[2,112,384]{2,1,0:T(8,128)(2,1)S(1)} %pad_maximum_fusion.16), channel_id=1, source_target_pairs={{0,8},{8,0},{16,24},{24,16},{1,9},{9,1},{17,25},{25,17},{2,10},{10... | collective-permute-start | bytes 516104 | tf_op jit(solution)/shard_map/ppermute | solution.py:25
  17.8 14.8 %collective-permute-start.10 = (bf16[4,3,16,512]{3,2,1,0:T(8,128)(2,1)S(1)}, bf16[4,3,16,512]{3,2,1,0:T(8,128)(2,1)S(1)}, u32[]{:S(2)}, u32[]{:S(2)}) collective-permute-start(bf16[4,3,16,512]{3,2,1,0:T(8,128)(2,1)S(1)} %pad_maximum_fusion.10), channel_id=1, source_target_pairs={{0,8},{8,0},{16,24},{24,16},{1,9},{9,1},{17,25},{25,17},{2,10},{10... | collective-permute-start | bytes 589832 | tf_op jit(solution)/shard_map/ppermute | solution.py:25
  20.0 12.4 %collective-permute-start.14 = (bf16[4,3,16,512]{3,2,1,0:T(8,128)(2,1)S(1)}, bf16[4,3,16,512]{3,2,1,0:T(8,128)(2,1)S(1)}, u32[]{:S(2)}, u32[]{:S(2)}) collective-permute-start(bf16[4,3,16,512]{3,2,1,0:T(8,128)(2,1)S(1)} %pad_maximum_fusion.11), channel_id=1, source_target_pairs={{0,24},{8,16},{16,8},{24,0},{1,25},{9,17},{17,9},{25,1},{2,26},{10... | collective-permute-start | bytes 589832 | tf_op jit(solution)/shard_map/ppermute | solution.py:25
  21.1 9.3 %collective-permute-start.6 = (bf16[4,3,16,512]{3,2,1,0:T(8,128)(2,1)S(1)}, bf16[4,3,16,512]{3,2,1,0:T(8,128)(2,1)S(1)}, u32[]{:S(2)}, u32[]{:S(2)}) collective-permute-start(bf16[4,3,16,512]{3,2,1,0:T(8,128)(2,1)S(1)} %pad_maximum_fusion.9), channel_id=1, source_target_pairs={{0,96},{32,64},{64,32},{96,0},{1,97},{33,65},{65,33},{97,1},{2,98}... | collective-permute-start | bytes 589832 | tf_op jit(solution)/shard_map/ppermute | solution.py:25
  23.3 6.1 %collective-permute-start.2 = (bf16[4,3,16,512]{3,2,1,0:T(8,128)(2,1)S(1)}, bf16[4,3,16,512]{3,2,1,0:T(8,128)(2,1)S(1)}, u32[]{:S(2)}, u32[]{:S(2)}) collective-permute-start(bf16[4,3,16,512]{3,2,1,0:T(8,128)(2,1)S(1)} %pad_maximum_fusion.8), channel_id=1, source_target_pairs={{0,32},{32,0},{64,96},{96,64},{1,33},{33,1},{65,97},{97,65},{2,34}... | collective-permute-start | bytes 589832 | tf_op jit(solution)/shard_map/ppermute | solution.py:25
  24.8 8.5 %collective-permute-start.18 = (bf16[2,112,384]{2,1,0:T(8,128)(2,1)S(1)}, bf16[2,112,384]{2,1,0:T(8,128)(2,1)S(1)}, u32[]{:S(2)}, u32[]{:S(2)}) collective-permute-start(bf16[2,112,384]{2,1,0:T(8,128)(2,1)S(1)} %pad_maximum_fusion.18), channel_id=1, source_target_pairs={{0,24},{8,16},{16,8},{24,0},{1,25},{9,17},{17,9},{25,1},{2,26},{10... | collective-permute-start | bytes 516104 | tf_op jit(solution)/shard_map/ppermute | solution.py:25
  29.4 18.4 %collective-permute-start.3 = (bf16[8,3,16,512]{3,2,1,0:T(8,128)(2,1)S(1)}, bf16[8,3,16,512]{3,2,1,0:T(8,128)(2,1)S(1)}, u32[]{:S(2)}, u32[]{:S(2)}) collective-permute-start(bf16[8,3,16,512]{3,2,1,0:T(8,128)(2,1)S(1)} %pad_maximum_fusion.refs_2_), channel_id=1, source_target_pairs={{0,96},{32,64},{64,32},{96,0},{1,97},{33,65},{65,33},{97,1},{2,98}... | collective-permute-start | bytes 1179656 | tf_op jit(solution)/shard_map/ppermute | solution.py:25
  30.4 17.4 %collective-permute-start.7 = (bf16[8,3,16,512]{3,2,1,0:T(8,128)(2,1)S(1)}, bf16[8,3,16,512]{3,2,1,0:T(8,128)(2,1)S(1)}, u32[]{:S(2)}, u32[]{:S(2)}) collective-permute-start(bf16[8,3,16,512]{3,2,1,0:T(8,128)(2,1)S(1)} %pad_maximum_fusion.1.refs_4_), channel_id=1, source_target_pairs={{0,32},{32,0},{64,96},{96,64},{1,33},{33,1},{65,97},{97,65},{2,34}... | collective-permute-start | bytes 1179656 | tf_op jit(solution)/shard_map/ppermute | solution.py:25
  32.4 15.4 %collective-permute-start.15 = (bf16[8,3,16,512]{3,2,1,0:T(8,128)(2,1)S(1)}, bf16[8,3,16,512]{3,2,1,0:T(8,128)(2,1)S(1)}, u32[]{:S(2)}, u32[]{:S(2)}) collective-permute-start(bf16[8,3,16,512]{3,2,1,0:T(8,128)(2,1)S(1)} %pad_maximum_fusion.3.refs_8_), channel_id=1, source_target_pairs={{0,8},{8,0},{16,24},{24,16},{1,9},{9,1},{17,25},{25,17},{2,10},{10... | collective-permute-start | bytes 1179656 | tf_op jit(solution)/shard_map/ppermute | solution.py:25
  32.6 15.2 %collective-permute-start.11 = (bf16[8,3,16,512]{3,2,1,0:T(8,128)(2,1)S(1)}, bf16[8,3,16,512]{3,2,1,0:T(8,128)(2,1)S(1)}, u32[]{:S(2)}, u32[]{:S(2)}) collective-permute-start(bf16[8,3,16,512]{3,2,1,0:T(8,128)(2,1)S(1)} %pad_maximum_fusion.2.refs_6_), channel_id=1, source_target_pairs={{0,24},{8,16},{16,8},{24,0},{1,25},{9,17},{17,9},{25,1},{2,26},{10... | collective-permute-start | bytes 1179656 | tf_op jit(solution)/shard_map/ppermute | solution.py:25
  33.3 7.8 %collective-permute-start.17 = (bf16[2,112,384]{2,1,0:T(8,128)(2,1)S(1)}, bf16[2,112,384]{2,1,0:T(8,128)(2,1)S(1)}, u32[]{:S(2)}, u32[]{:S(2)}) collective-permute-start(bf16[2,112,384]{2,1,0:T(8,128)(2,1)S(1)} %pad_maximum_fusion.17), channel_id=1, source_target_pairs={{0,32},{32,0},{64,96},{96,64},{1,33},{33,1},{65,97},{97,65},{2,34}... | collective-permute-start | bytes 516104 | tf_op jit(solution)/shard_map/ppermute | solution.py:25
  35.4 3.7 %copy-start = (bf16[8,1,192,3072]{3,2,1,0:T(8,128)(2,1)S(1)}, bf16[8,1,192,3072]{3,2,1,0:T(8,128)(2,1)}, u32[]{:S(2)}) copy-start(bf16[8,1,192,3072]{3,2,1,0:T(8,128)(2,1)} %param.6) | copy-start | bytes 28311556
  41.1 6.6 %collective-permute-start.19 = (bf16[2,112,384]{2,1,0:T(8,128)(2,1)S(1)}, bf16[2,112,384]{2,1,0:T(8,128)(2,1)S(1)}, u32[]{:S(2)}, u32[]{:S(2)}) collective-permute-start(bf16[2,112,384]{2,1,0:T(8,128)(2,1)S(1)} %collective-permute-done.18), channel_id=1, source_target_pairs={{0,96},{32,64},{64,32},{96,0},{1,97},{33,65},{65,33},{97,1},{2,98}... | collective-permute-start | bytes 516104 | tf_op jit(solution)/shard_map/ppermute | solution.py:25
  47.8 15.9 %collective-permute-start.26 = (bf16[4,112,384]{2,1,0:T(8,128)(2,1)S(1)}, bf16[4,112,384]{2,1,0:T(8,128)(2,1)S(1)}, u32[]{:S(2)}, u32[]{:S(2)}) collective-permute-start(bf16[4,112,384]{2,1,0:T(8,128)(2,1)S(1)} %constant_dynamic-update-slice_fusion.2.refs_6_), channel_id=1, source_target_pairs={{0,32},{32,0},{64,96},{96,64},{1,33},{33,1},{65,97},{97,65},{2,34}... | collective-permute-start | bytes 1032200 | tf_op jit(solution)/shard_map/ppermute | solution.py:25
  50.3 5.9 %collective-permute-start.22 = (bf16[1,192,512]{2,1,0:T(8,128)(2,1)S(1)}, bf16[1,192,512]{2,1,0:T(8,128)(2,1)S(1)}, u32[]{:S(2)}, u32[]{:S(2)}) collective-permute-start(bf16[1,192,512]{2,1,0:T(8,128)(2,1)S(1)} %get-tuple-element.98), channel_id=1, source_target_pairs={{0,1},{1,0},{2,3},{3,2},{4,5},{5,4},{6,7},{7,6},{8,9},{9,8},{10,11... | collective-permute-start | bytes 589832 | tf_op jit(solution)/shard_map/ppermute | solution.py:25
  53.8 16.5 %copy-start.4 = (f32[1,192,512]{2,1,0:T(8,128)S(1)}, f32[1,192,512]{2,1,0:T(8,128)}, u32[]{:S(2)}) copy-start(f32[1,192,512]{2,1,0:T(8,128)} %param.7) | copy-start | bytes 1179652
  53.8 36.6 %copy-start.5 = (s32[192]{0:T(256)S(1)}, s32[192]{0:T(256)}, u32[]{:S(2)}) copy-start(s32[192]{0:T(256)} %refs_2_.3) | copy-start | bytes 2308
  53.8 7.8 %collective-permute-start.20 = (bf16[2,192,512]{2,1,0:T(8,128)(2,1)S(1)}, bf16[2,192,512]{2,1,0:T(8,128)(2,1)S(1)}, u32[]{:S(2)}, u32[]{:S(2)}) collective-permute-start(bf16[2,192,512]{2,1,0:T(8,128)(2,1)S(1)} %get-tuple-element.96), channel_id=1, source_target_pairs={{0,1},{1,0},{2,3},{3,2},{4,5},{5,4},{6,7},{7,6},{8,9},{9,8},{10,11... | collective-permute-start | bytes 1179656 | tf_op jit(solution)/shard_map/ppermute | solution.py:25
  54.4 11.3 %collective-permute-start.25 = (bf16[4,112,384]{2,1,0:T(8,128)(2,1)S(1)}, bf16[4,112,384]{2,1,0:T(8,128)(2,1)S(1)}, u32[]{:S(2)}, u32[]{:S(2)}) collective-permute-start(bf16[4,112,384]{2,1,0:T(8,128)(2,1)S(1)} %constant_dynamic-update-slice_fusion.refs_4_), channel_id=1, source_target_pairs={{0,96},{32,64},{64,32},{96,0},{1,97},{33,65},{65,33},{97,1},{2,98}... | collective-permute-start | bytes 1032200 | tf_op jit(solution)/shard_map/ppermute | solution.py:25
  56.2 9.5 %collective-permute-start.23 = (bf16[192,512]{1,0:T(8,128)(2,1)S(1)}, bf16[192,512]{1,0:T(8,128)(2,1)S(1)}, u32[]{:S(2)}, u32[]{:S(2)}) collective-permute-start(bf16[192,512]{1,0:T(8,128)(2,1)S(1)} %fusion.1), channel_id=1, source_target_pairs={{0,4},{2,6},{4,0},{6,2},{1,5},{3,7},{5,1},{7,3},{8,12},{10,14},{12... | collective-permute-start | bytes 589832 | tf_op jit(solution)/shard_map/ppermute | solution.py:25
  61.5 1.5 collective-permute-start.27
  61.7 8.6 %collective-permute-start.24 = (bf16[192,512]{1,0:T(8,128)(2,1)S(1)}, bf16[192,512]{1,0:T(8,128)(2,1)S(1)}, u32[]{:S(2)}, u32[]{:S(2)}) collective-permute-start(bf16[192,512]{1,0:T(8,128)(2,1)S(1)} %get-tuple-element.146), channel_id=1, source_target_pairs={{0,6},{2,4},{4,2},{6,0},{1,7},{3,5},{5,3},{7,1},{8,14},{10,12},{12... | collective-permute-start | bytes 589832 | tf_op jit(solution)/shard_map/ppermute | solution.py:25
  63.0 7.3 %collective-permute-start.21 = (bf16[192,512]{1,0:T(8,128)(2,1)S(1)}, bf16[192,512]{1,0:T(8,128)(2,1)S(1)}, u32[]{:S(2)}, u32[]{:S(2)}) collective-permute-start(bf16[192,512]{1,0:T(8,128)(2,1)S(1)} %get-tuple-element.147), channel_id=1, source_target_pairs={{0,2},{2,0},{4,6},{6,4},{1,3},{3,1},{5,7},{7,5},{8,10},{10,8},{12,... | collective-permute-start | bytes 589832 | tf_op jit(solution)/shard_map/ppermute | solution.py:25
  71.4 19.0 %all-to-all-start = ((bf16[16,192,128]{2,1,0:T(8,128)(2,1)}), bf16[16,192,128]{2,1,0:T(8,128)(2,1)S(1)}, u32[]{:S(2)}, u32[]{:S(2)}) async-start(bf16[16,192,128]{2,1,0:T(8,128)(2,1)} %get-tuple-element.114), calls=%async_computation | async-start | bytes 1572864 | tf_op jit(solution)/shard_map/all_to_all | solution.py:162
  91.6 5.4 %collective-permute-start.31 = (bf16[1,12,16,128]{3,2,1,0:T(8,128)(2,1)S(1)}, bf16[1,12,16,128]{3,2,1,0:T(8,128)(2,1)S(1)}, u32[]{:S(2)}, u32[]{:S(2)}) collective-permute-start(bf16[1,12,16,128]{3,2,1,0:T(8,128)(2,1)S(1)} %bitcast.67), channel_id=1, source_target_pairs={{0,24},{8,16},{16,8},{24,0},{1,25},{9,17},{17,9},{25,1},{2,26},{10... | collective-permute-start | bytes 147464 | tf_op jit(solution)/shard_map/ppermute | solution.py:25
  92.5 4.6 %collective-permute-start.28 = (bf16[1,12,16,128]{3,2,1,0:T(8,128)(2,1)S(1)}, bf16[1,12,16,128]{3,2,1,0:T(8,128)(2,1)S(1)}, u32[]{:S(2)}, u32[]{:S(2)}) collective-permute-start(bf16[1,12,16,128]{3,2,1,0:T(8,128)(2,1)S(1)} %bitcast.63), channel_id=1, source_target_pairs={{0,8},{8,0},{16,24},{24,16},{1,9},{9,1},{17,25},{25,17},{2,10},{10... | collective-permute-start | bytes 147464 | tf_op jit(solution)/shard_map/ppermute | solution.py:25
  92.7 7.0 %collective-permute-start.34 = (bf16[1,12,16,128]{3,2,1,0:T(8,128)(2,1)S(1)}, bf16[1,12,16,128]{3,2,1,0:T(8,128)(2,1)S(1)}, u32[]{:S(2)}, u32[]{:S(2)}) collective-permute-start(bf16[1,12,16,128]{3,2,1,0:T(8,128)(2,1)S(1)} %bitcast.59), channel_id=1, source_target_pairs={{0,32},{32,0},{64,96},{96,64},{1,33},{33,1},{65,97},{97,65},{2,34}... | collective-permute-start | bytes 147464 | tf_op jit(solution)/shard_map/ppermute | solution.py:25
  93.4 7.1 %collective-permute-start.37 = (bf16[1,12,16,128]{3,2,1,0:T(8,128)(2,1)S(1)}, bf16[1,12,16,128]{3,2,1,0:T(8,128)(2,1)S(1)}, u32[]{:S(2)}, u32[]{:S(2)}) collective-permute-start(bf16[1,12,16,128]{3,2,1,0:T(8,128)(2,1)S(1)} %bitcast.55), channel_id=1, source_target_pairs={{0,96},{32,64},{64,32},{96,0},{1,97},{33,65},{65,33},{97,1},{2,98}... | collective-permute-start | bytes 147464 | tf_op jit(solution)/shard_map/ppermute | solution.py:25
  97.0 4.7 %collective-permute-start.32 = (bf16[2,12,16,128]{3,2,1,0:T(8,128)(2,1)S(1)}, bf16[2,12,16,128]{3,2,1,0:T(8,128)(2,1)S(1)}, u32[]{:S(2)}, u32[]{:S(2)}) collective-permute-start(bf16[2,12,16,128]{3,2,1,0:T(8,128)(2,1)S(1)} %pad_maximum_fusion.24), channel_id=1, source_target_pairs={{0,8},{8,0},{16,24},{24,16},{1,9},{9,1},{17,25},{25,17},{2,10},{10... | collective-permute-start | bytes 294920 | tf_op jit(solution)/shard_map/ppermute | solution.py:25
  97.2 6.1 %collective-permute-start.29 = (bf16[2,12,16,128]{3,2,1,0:T(8,128)(2,1)S(1)}, bf16[2,12,16,128]{3,2,1,0:T(8,128)(2,1)S(1)}, u32[]{:S(2)}, u32[]{:S(2)}) collective-permute-start(bf16[2,12,16,128]{3,2,1,0:T(8,128)(2,1)S(1)} %pad_maximum_fusion.23), channel_id=1, source_target_pairs={{0,24},{8,16},{16,8},{24,0},{1,25},{9,17},{17,9},{25,1},{2,26},{10... | collective-permute-start | bytes 294920 | tf_op jit(solution)/shard_map/ppermute | solution.py:25
  99.7 5.9 %collective-permute-start.35 = (bf16[2,12,16,128]{3,2,1,0:T(8,128)(2,1)S(1)}, bf16[2,12,16,128]{3,2,1,0:T(8,128)(2,1)S(1)}, u32[]{:S(2)}, u32[]{:S(2)}) collective-permute-start(bf16[2,12,16,128]{3,2,1,0:T(8,128)(2,1)S(1)} %pad_maximum_fusion.25), channel_id=1, source_target_pairs={{0,96},{32,64},{64,32},{96,0},{1,97},{33,65},{65,33},{97,1},{2,98}... | collective-permute-start | bytes 294920 | tf_op jit(solution)/shard_map/ppermute | solution.py:25
  100.5 5.2 %collective-permute-start.38 = (bf16[2,12,16,128]{3,2,1,0:T(8,128)(2,1)S(1)}, bf16[2,12,16,128]{3,2,1,0:T(8,128)(2,1)S(1)}, u32[]{:S(2)}, u32[]{:S(2)}) collective-permute-start(bf16[2,12,16,128]{3,2,1,0:T(8,128)(2,1)S(1)} %pad_maximum_fusion.26), channel_id=1, source_target_pairs={{0,32},{32,0},{64,96},{96,64},{1,33},{33,1},{65,97},{97,65},{2,34}... | collective-permute-start | bytes 294920 | tf_op jit(solution)/shard_map/ppermute | solution.py:25
  101.8 7.0 %collective-permute-start.33 = (bf16[4,12,16,128]{3,2,1,0:T(8,128)(2,1)S(1)}, bf16[4,12,16,128]{3,2,1,0:T(8,128)(2,1)S(1)}, u32[]{:S(2)}, u32[]{:S(2)}) collective-permute-start(bf16[4,12,16,128]{3,2,1,0:T(8,128)(2,1)S(1)} %pad_maximum_fusion.13), channel_id=1, source_target_pairs={{0,96},{32,64},{64,32},{96,0},{1,97},{33,65},{65,33},{97,1},{2,98}... | collective-permute-start | bytes 589832 | tf_op jit(solution)/shard_map/ppermute | solution.py:25
  103.3 5.7 %collective-permute-start.30 = (bf16[4,12,16,128]{3,2,1,0:T(8,128)(2,1)S(1)}, bf16[4,12,16,128]{3,2,1,0:T(8,128)(2,1)S(1)}, u32[]{:S(2)}, u32[]{:S(2)}) collective-permute-start(bf16[4,12,16,128]{3,2,1,0:T(8,128)(2,1)S(1)} %pad_maximum_fusion.12), channel_id=1, source_target_pairs={{0,32},{32,0},{64,96},{96,64},{1,33},{33,1},{65,97},{97,65},{2,34}... | collective-permute-start | bytes 589832 | tf_op jit(solution)/shard_map/ppermute | solution.py:25
  105.6 5.8 %collective-permute-start.36 = (bf16[4,12,16,128]{3,2,1,0:T(8,128)(2,1)S(1)}, bf16[4,12,16,128]{3,2,1,0:T(8,128)(2,1)S(1)}, u32[]{:S(2)}, u32[]{:S(2)}) collective-permute-start(bf16[4,12,16,128]{3,2,1,0:T(8,128)(2,1)S(1)} %pad_maximum_fusion.14), channel_id=1, source_target_pairs={{0,8},{8,0},{16,24},{24,16},{1,9},{9,1},{17,25},{25,17},{2,10},{10... | collective-permute-start | bytes 589832 | tf_op jit(solution)/shard_map/ppermute | solution.py:25
  105.8 7.4 %collective-permute-start.39 = (bf16[4,12,16,128]{3,2,1,0:T(8,128)(2,1)S(1)}, bf16[4,12,16,128]{3,2,1,0:T(8,128)(2,1)S(1)}, u32[]{:S(2)}, u32[]{:S(2)}) collective-permute-start(bf16[4,12,16,128]{3,2,1,0:T(8,128)(2,1)S(1)} %pad_maximum_fusion.15), channel_id=1, source_target_pairs={{0,24},{8,16},{16,8},{24,0},{1,25},{9,17},{17,9},{25,1},{2,26},{10... | collective-permute-start | bytes 589832 | tf_op jit(solution)/shard_map/ppermute | solution.py:25
  113.2 9.1 %collective-permute-start.40 = (bf16[8,12,16,128]{3,2,1,0:T(8,128)(2,1)S(1)}, bf16[8,12,16,128]{3,2,1,0:T(8,128)(2,1)S(1)}, u32[]{:S(2)}, u32[]{:S(2)}) collective-permute-start(bf16[8,12,16,128]{3,2,1,0:T(8,128)(2,1)S(1)} %pad_maximum_fusion.4.refs_2_), channel_id=1, source_target_pairs={{0,96},{32,64},{64,32},{96,0},{1,97},{33,65},{65,33},{97,1},{2,98}... | collective-permute-start | bytes 1179656 | tf_op jit(solution)/shard_map/ppermute | solution.py:25
  115.2 7.8 %collective-permute-start.41 = (bf16[8,12,16,128]{3,2,1,0:T(8,128)(2,1)S(1)}, bf16[8,12,16,128]{3,2,1,0:T(8,128)(2,1)S(1)}, u32[]{:S(2)}, u32[]{:S(2)}) collective-permute-start(bf16[8,12,16,128]{3,2,1,0:T(8,128)(2,1)S(1)} %pad_maximum_fusion.5.refs_4_), channel_id=1, source_target_pairs={{0,32},{32,0},{64,96},{96,64},{1,33},{33,1},{65,97},{97,65},{2,34}... | collective-permute-start | bytes 1179656 | tf_op jit(solution)/shard_map/ppermute | solution.py:25
  115.2 9.0 %collective-permute-start.42 = (bf16[8,12,16,128]{3,2,1,0:T(8,128)(2,1)S(1)}, bf16[8,12,16,128]{3,2,1,0:T(8,128)(2,1)S(1)}, u32[]{:S(2)}, u32[]{:S(2)}) collective-permute-start(bf16[8,12,16,128]{3,2,1,0:T(8,128)(2,1)S(1)} %pad_maximum_fusion.6.refs_6_), channel_id=1, source_target_pairs={{0,24},{8,16},{16,8},{24,0},{1,25},{9,17},{17,9},{25,1},{2,26},{10... | collective-permute-start | bytes 1179656 | tf_op jit(solution)/shard_map/ppermute | solution.py:25
  116.1 8.1 %collective-permute-start.43 = (bf16[8,12,16,128]{3,2,1,0:T(8,128)(2,1)S(1)}, bf16[8,12,16,128]{3,2,1,0:T(8,128)(2,1)S(1)}, u32[]{:S(2)}, u32[]{:S(2)}) collective-permute-start(bf16[8,12,16,128]{3,2,1,0:T(8,128)(2,1)S(1)} %pad_maximum_fusion.7.refs_8_), channel_id=1, source_target_pairs={{0,8},{8,0},{16,24},{24,16},{1,9},{9,1},{17,25},{25,17},{2,10},{10... | collective-permute-start | bytes 1179656 | tf_op jit(solution)/shard_map/ppermute | solution.py:25
  116.6 3.7 %copy-start.1 = (bf16[8,1,192,3072]{3,2,1,0:T(8,128)(2,1)S(1)}, bf16[8,1,192,3072]{3,2,1,0:T(8,128)(2,1)}, u32[]{:S(2)}) copy-start(bf16[8,1,192,3072]{3,2,1,0:T(8,128)(2,1)} %param.6) | copy-start | bytes 28311556
  126.7 4.1 %collective-permute-start.44 = (bf16[1,192,512]{2,1,0:T(8,128)(2,1)S(1)}, bf16[1,192,512]{2,1,0:T(8,128)(2,1)S(1)}, u32[]{:S(2)}, u32[]{:S(2)}) collective-permute-start(bf16[1,192,512]{2,1,0:T(8,128)(2,1)S(1)} %get-tuple-element.134), channel_id=1, source_target_pairs={{0,1},{1,0},{2,3},{3,2},{4,5},{5,4},{6,7},{7,6},{8,9},{9,8},{10,11... | collective-permute-start | bytes 589832 | tf_op jit(solution)/shard_map/ppermute | solution.py:25
  130.2 4.9 %collective-permute-start.46 = (bf16[2,192,512]{2,1,0:T(8,128)(2,1)S(1)}, bf16[2,192,512]{2,1,0:T(8,128)(2,1)S(1)}, u32[]{:S(2)}, u32[]{:S(2)}) collective-permute-start(bf16[2,192,512]{2,1,0:T(8,128)(2,1)S(1)} %get-tuple-element.140), channel_id=1, source_target_pairs={{0,1},{1,0},{2,3},{3,2},{4,5},{5,4},{6,7},{7,6},{8,9},{9,8},{10,11... | collective-permute-start | bytes 1179656 | tf_op jit(solution)/shard_map/ppermute | solution.py:25
  130.9 47.2 %copy-start.2 = (f32[1,192,512]{2,1,0:T(8,128)S(1)}, f32[1,192,512]{2,1,0:T(8,128)}, u32[]{:S(2)}) copy-start(f32[1,192,512]{2,1,0:T(8,128)} %param.8) | copy-start | bytes 1179652
  130.9 8.4 %collective-permute-start.48 = (bf16[192,512]{1,0:T(8,128)(2,1)S(1)}, bf16[192,512]{1,0:T(8,128)(2,1)S(1)}, u32[]{:S(2)}, u32[]{:S(2)}) collective-permute-start(bf16[192,512]{1,0:T(8,128)(2,1)S(1)} %fusion.3), channel_id=1, source_target_pairs={{0,4},{2,6},{4,0},{6,2},{1,5},{3,7},{5,1},{7,3},{8,12},{10,14},{12... | collective-permute-start | bytes 589832 | tf_op jit(solution)/shard_map/ppermute | solution.py:25
  135.1 1.6 collective-permute-start.45
  135.3 8.6 %collective-permute-start.49 = (bf16[192,512]{1,0:T(8,128)(2,1)S(1)}, bf16[192,512]{1,0:T(8,128)(2,1)S(1)}, u32[]{:S(2)}, u32[]{:S(2)}) collective-permute-start(bf16[192,512]{1,0:T(8,128)(2,1)S(1)} %get-tuple-element.144), channel_id=1, source_target_pairs={{0,6},{2,4},{4,2},{6,0},{1,7},{3,5},{5,3},{7,1},{8,14},{10,12},{12... | collective-permute-start | bytes 589832 | tf_op jit(solution)/shard_map/ppermute | solution.py:25
  136.3 7.6 %collective-permute-start.47 = (bf16[192,512]{1,0:T(8,128)(2,1)S(1)}, bf16[192,512]{1,0:T(8,128)(2,1)S(1)}, u32[]{:S(2)}, u32[]{:S(2)}) collective-permute-start(bf16[192,512]{1,0:T(8,128)(2,1)S(1)} %get-tuple-element.145), channel_id=1, source_target_pairs={{0,2},{2,0},{4,6},{6,4},{1,3},{3,1},{5,7},{7,5},{8,10},{10,8},{12,... | collective-permute-start | bytes 589832 | tf_op jit(solution)/shard_map/ppermute | solution.py:25

commit v5 on v4

--- a/solution.py
+++ b/solution.py
@@ -14,9 +14,9 @@
 VMEM_LIMIT = 24 * 1024 * 1024
 QUARTER_STEPS = (
     (("z", 1), ("z", 3), ("x", 1), ("x", 3)),
-    (("z", 3), ("z", 1), ("x", 3), ("x", 1)),
+    (("z", 1), ("z", 3), ("x", 3), ("x", 1)),
     (("x", 1), ("x", 3), ("z", 1), ("z", 3)),
-    (("x", 3), ("x", 1), ("z", 3), ("z", 1)),
+    (("x", 1), ("x", 3), ("z", 3), ("z", 1)),
 )
 
 
@@ -49,9 +49,12 @@
 
 
 def gather_swaps(parts, between=lambda turn, held: held):
-    held = [part[None] for part in parts]
-    for turn in range(3):
-        held = between(turn, joined(held, swap_turn(held, turn)))
+    held = [jnp.stack(parts[at:at + 2])[None] for at in (0, 2)]
+    for turn in range(2):
+        got = [swap(pair, *QUARTER_STEPS[2 * p][turn]) for p, pair in enumerate(held)]
+        held = between(turn, joined(held, got))
+    held = [pair[:, at] for pair in held for at in range(2)]
+    held = between(2, joined(held, swap_turn(held, 2)))
     return [bundle for pair in zip(held, swap_turn(held, 3)) for bundle in pair]
 
 

time: 179 us -> 180 us (level)
  waiting for transfers between devices: 51 us -> 63.5 us
  starting transfers between devices: 60.7 us -> 48.8 us
    ppermute x50 -> x42, starting transfers between devices: 55.9 us -> 42.9 us  [swap(): return lax.ppermute(value, axis, [(i, i ^ mask) for i in range(size)])]
    ppermute x50 -> x42, waiting for transfers between devices: 36.9 us -> 49.4 us  [swap(): return lax.ppermute(value, axis, [(i, i ^ mask) for i in range(size)])]
  transfers between devices with their start and end apart: 51 -> 43, of which waited for: 20 -> 23; matrix products, arithmetic and copies ran while one was open for 1% -> 1% of each run, Pallas kernels for 8% -> 8%
where the time goes in v5:
time: 180 us; the launch traced here: 179 us
  waiting for transfers between devices  63.5 us (35%)
  starting transfers between devices  48.8 us (27%)
  blocking collectives  31.6 us (18%)
  Pallas kernels  22.4 us (12%)
  local copies, waits for them, and re-layouts  9.37 us (5%)
  other arithmetic  2.17 us (1%)
    ppermute x42, waiting for transfers between devices, swap(): return lax.ppermute(value, axis, [(i, i ^ mask) for i in range(size)])  49.4 us
    ppermute x42, starting transfers between devices, swap(): return lax.ppermute(value, axis, [(i, i ^ mask) for i in range(size)])  42.9 us
    pallas_call x12, Pallas kernels, call(): pl.pallas_call(body, in_specs=[SMEM] * scalars + [VMEM] * (len(args) - sc...  21.2 us
    all_to_all x1, blocking collectives, exchange(): return lax.all_to_all(sent, ('x', 'z'), 0, 0, tiled=True).reshape(3072, 128)  20.1 us
    all_to_all x1, waiting for transfers between devices, exchange(): return lax.all_to_all(sent, ('x', 'z'), 0, 0, tiled=True).reshape(3072, 128)  14.1 us
    all_to_all x1, blocking collectives, body(): pieces = lax.all_to_all(sent, ('x', 'z'), 0, 0, tiled=True)  11.6 us
    unnamed x18, local copies, waits for them, and re-layouts  9.14 us
    all_to_all x1, starting transfers between devices, exchange(): return lax.all_to_all(sent, ('x', 'z'), 0, 0, tiled=True).reshape(3072, 128)  5.92 us
  transfers between devices with their start and end apart: 43, of which 23 were waited for; matrix products, arithmetic and copies ran while one was open for 1% of the time, Pallas kernels for 8%

profile of v5, /device:TPU:0, one launch (start us, length us, event | category | flops | bytes accessed | tf_op | source)
XLA Modules:
  0.0 179.1 jit_solution(514502864055891474)
XLA Ops:
  0.6 1.0 bitcast_convert_fusion
  1.7 2.1 %collective-permute-start = (bf16[1,2,3,16,512]{4,3,2,0,1:T(8,128)(2,1)S(1)}, bf16[1,2,3,16,512]{4,3,2,0,1:T(8,128)(2,1)S(1)}, u32[]{:S(2)}, u32[]{:S(2)}) collective-permute-start(bf16[1,2,3,16,512]{4,3,2,0,1:T(8,128)(2,1)S(1)} %maximum_bitcast_fusion), channel_id=1, source_target_pairs={{0,8},{8,0},{16,24},{24,16},{1,9},{9,1},{17,25},{25,17},{2,10},{10... | collective-permute-start | bytes 294920 | tf_op jit(solution)/shard_map/ppermute | solution.py:25
  3.8 1.6 collective-permute-start.6
  5.4 1.1 copy-done.3
  7.8 0.7 collective-permute-done.6
  8.5 2.8 %collective-permute-start.7 = (bf16[2,2,3,16,512]{4,3,2,0,1:T(8,128)(2,1)S(1)}, bf16[2,2,3,16,512]{4,3,2,0,1:T(8,128)(2,1)S(1)}, u32[]{:S(2)}, u32[]{:S(2)}) collective-permute-start(bf16[2,2,3,16,512]{4,3,2,0,1:T(8,128)(2,1)S(1)} %pad_maximum_fusion.13), channel_id=1, source_target_pairs={{0,96},{32,64},{64,32},{96,0},{1,97},{33,65},{65,33},{97,1},{2,98}... | collective-permute-start | bytes 589832 | tf_op jit(solution)/shard_map/ppermute | solution.py:25
  11.4 2.6 %collective-permute-start.1 = (bf16[2,2,3,16,512]{4,3,2,0,1:T(8,128)(2,1)S(1)}, bf16[2,2,3,16,512]{4,3,2,0,1:T(8,128)(2,1)S(1)}, u32[]{:S(2)}, u32[]{:S(2)}) collective-permute-start(bf16[2,2,3,16,512]{4,3,2,0,1:T(8,128)(2,1)S(1)} %pad_maximum_fusion.12), channel_id=1, source_target_pairs={{0,24},{8,16},{16,8},{24,0},{1,25},{9,17},{17,9},{25,1},{2,26},{10... | collective-permute-start | bytes 589832 | tf_op jit(solution)/shard_map/ppermute | solution.py:25
  14.0 1.1 collective-permute-start.12
  15.6 2.8 %collective-permute-done.1 = bf16[2,2,3,16,512]{4,3,2,0,1:T(8,128)(2,1)S(1)} collective-permute-done((bf16[2,2,3,16,512]{4,3,2,0,1:T(8,128)(2,1)S(1)}, bf16[2,2,3,16,512]{4,3,2,0,1:T(8,128)(2,1)S(1)}, u32[]{:S(2)}, u32[]{:S(2)}) %collective-permute-start.1) | collective-permute-done | bytes 196640 | tf_op jit(solution)/shard_map/ppermute | solution.py:25
  18.4 1.1 collective-permute-done.12
  19.7 1.2 collective-permute-start.4
  21.0 1.6 collective-permute-start.14
  22.6 1.7 collective-permute-start.10
  24.3 0.9 collective-permute-done.2
  25.2 1.3 collective-permute-start.3
  26.5 1.7 collective-permute-done.4
  28.3 1.2 collective-permute-start.5
  29.5 1.0 collective-permute-done.8
  30.6 1.4 collective-permute-start.9
  32.7 3.7 %copy-done = bf16[8,1,192,3072]{3,2,1,0:T(8,128)(2,1)S(1)} copy-done((bf16[8,1,192,3072]{3,2,1,0:T(8,128)(2,1)S(1)}, bf16[8,1,192,3072]{3,2,1,0:T(8,128)(2,1)}, u32[]{:S(2)}) %copy-start) | copy-done | bytes 9437208
  37.0 1.0 collective-permute-done.13
  38.0 2.0 %collective-permute-start.15 = (bf16[2,112,384]{2,1,0:T(8,128)(2,1)S(1)}, bf16[2,112,384]{2,1,0:T(8,128)(2,1)S(1)}, u32[]{:S(2)}, u32[]{:S(2)}) collective-permute-start(bf16[2,112,384]{2,1,0:T(8,128)(2,1)S(1)} %collective-permute-done.14), channel_id=1, source_target_pairs={{0,96},{32,64},{64,32},{96,0},{1,97},{33,65},{65,33},{97,1},{2,98}... | collective-permute-start | bytes 516104 | tf_op jit(solution)/shard_map/ppermute | solution.py:25
  40.0 4.6 %collective-permute-done.15 = bf16[2,112,384]{2,1,0:T(8,128)(2,1)S(1)} collective-permute-done((bf16[2,112,384]{2,1,0:T(8,128)(2,1)S(1)}, bf16[2,112,384]{2,1,0:T(8,128)(2,1)S(1)}, u32[]{:S(2)}, u32[]{:S(2)}) %collective-permute-start.15) | collective-permute-done | bytes 172064 | tf_op jit(solution)/shard_map/ppermute | solution.py:25
  44.8 2.2 %shard_map.79 = (bf16[1,192,512]{2,1,0:T(8,128)(2,1)S(1)}, bf16[1,192,512]{2,1,0:T(8,128)(2,1)S(1)}, bf16[192,16,512]{2,1,0:T(8,128)(2,1)S(1)}) custom-call(s32[4]{0:T(128)S(1)} %pad_add_fusion.pos_ref.refs_0_, bf16[4,384,3072]{2,1,0:T(8,128)(2,1)S(1)} %shard_map.77.refs_1_, bf16[8,3,16,512]{3,2,1,0:T(8,128)(2,1)S(1)} %pad_maximum_fusion.1.refs_2_, ...), custom_call_target="tpu_custom_call" | custom-call | flops 1073741824 | bytes 1048576 | tf_op jit(solution)/shard_map/pallas_call | solution.py:30
  47.0 3.4 %shard_map.80 = (bf16[2,192,512]{2,1,0:T(8,128)(2,1)S(1)}, bf16[2,192,512]{2,1,0:T(8,128)(2,1)S(1)}) custom-call(s32[4]{0:T(128)S(1)} %pad_add_fusion.pos_ref.refs_0_, bf16[4,384,3072]{2,1,0:T(8,128)(2,1)S(1)} %shard_map.77.refs_1_, bf16[192,16,512]{2,1,0:T(8,128)(2,1)S(1)} %get-tuple-element.107.refs_2_), custom_call_target="tpu_custom_call" | custom-call | flops 2147483648 | bytes 1048576 | tf_op jit(solution)/shard_map/pallas_call | solution.py:30
  51.1 2.1 %collective-permute-start.21 = (bf16[4,112,384]{2,1,0:T(8,128)(2,1)S(1)}, bf16[4,112,384]{2,1,0:T(8,128)(2,1)S(1)}, u32[]{:S(2)}, u32[]{:S(2)}) collective-permute-start(bf16[4,112,384]{2,1,0:T(8,128)(2,1)S(1)} %constant_dynamic-update-slice_fusion.refs_4_), channel_id=1, source_target_pairs={{0,96},{32,64},{64,32},{96,0},{1,97},{33,65},{65,33},{97,1},{2,98}... | collective-permute-start | bytes 1032200 | tf_op jit(solution)/shard_map/ppermute | solution.py:25
  53.2 3.3 %collective-permute-start.19 = (bf16[192,512]{1,0:T(8,128)(2,1)S(1)}, bf16[192,512]{1,0:T(8,128)(2,1)S(1)}, u32[]{:S(2)}, u32[]{:S(2)}) collective-permute-start(bf16[192,512]{1,0:T(8,128)(2,1)S(1)} %fusion.1), channel_id=1, source_target_pairs={{0,4},{2,6},{4,0},{6,2},{1,5},{3,7},{5,1},{7,3},{8,12},{10,14},{12... | collective-permute-start | bytes 589832 | tf_op jit(solution)/shard_map/ppermute | solution.py:25
  56.5 2.0 %shard_map.81 = (bf16[1,192,512]{2,1,0:T(8,128)(2,1)S(1)}, bf16[1,192,512]{2,1,0:T(8,128)(2,1)S(1)}) custom-call(s32[4]{0:T(128)S(1)} %pad_add_fusion.pos_ref.refs_0_, bf16[4,384,3072]{2,1,0:T(8,128)(2,1)S(1)} %shard_map.77.refs_1_, bf16[192,16,512]{2,1,0:T(8,128)(2,1)S(1)} %get-tuple-element.107.refs_2_), custom_call_target="tpu_custom_call" | custom-call | flops 1073741824 | bytes 1048576 | tf_op jit(solution)/shard_map/pallas_call | solution.py:30
  58.7 1.1 collective-permute-start.20
  60.0 0.7 collective-permute-start.17
  60.7 1.7 collective-permute-done.21.refs_5_
  62.4 4.9 %collective-permute-done.20.refs_2_ = bf16[192,512]{1,0:T(8,128)(2,1)S(1)} collective-permute-done((bf16[192,512]{1,0:T(8,128)(2,1)S(1)}, bf16[192,512]{1,0:T(8,128)(2,1)S(1)}, u32[]{:S(2)}, u32[]{:S(2)}) %collective-permute-start.20) | collective-permute-done | bytes 196640 | tf_op jit(solution)/shard_map/ppermute | solution.py:25
  67.3 1.1 shard_map.82
  68.3 5.9 %all-to-all-start = ((bf16[16,192,128]{2,1,0:T(8,128)(2,1)}), bf16[16,192,128]{2,1,0:T(8,128)(2,1)S(1)}, u32[]{:S(2)}, u32[]{:S(2)}) async-start(bf16[16,192,128]{2,1,0:T(8,128)(2,1)} %get-tuple-element.114), calls=%async_computation | async-start | bytes 1572864 | tf_op jit(solution)/shard_map/all_to_all | solution.py:165
  74.3 14.1 %all-to-all-done = bf16[16,192,128]{2,1,0:T(8,128)(2,1)S(1)} async-done(((bf16[16,192,128]{2,1,0:T(8,128)(2,1)}), bf16[16,192,128]{2,1,0:T(8,128)(2,1)S(1)}, u32[]{:S(2)}, u32[]{:S(2)}) %all-to-all-start) | async-done | bytes 786464 | tf_op jit(solution)/shard_map/all_to_all | solution.py:165
  88.4 1.2 shard_map.83
  90.4 3.9 %collective-permute-done.28 = bf16[1,2,12,16,128]{4,3,2,0,1:T(8,128)(2,1)S(1)} collective-permute-done((bf16[1,2,12,16,128]{4,3,2,0,1:T(8,128)(2,1)S(1)}, bf16[1,2,12,16,128]{4,3,2,0,1:T(8,128)(2,1)S(1)}, u32[]{:S(2)}, u32[]{:S(2)}) %collective-permute-start.28) | collective-permute-done | bytes 98336 | tf_op jit(solution)/shard_map/ppermute | solution.py:25
  94.4 1.2 collective-permute-start.29
  95.6 0.7 collective-permute-start.25
  96.3 5.0 %collective-permute-done.29 = bf16[2,2,12,16,128]{4,3,2,0,1:T(8,128)(2,1)S(1)} collective-permute-done((bf16[2,2,12,16,128]{4,3,2,0,1:T(8,128)(2,1)S(1)}, bf16[2,2,12,16,128]{4,3,2,0,1:T(8,128)(2,1)S(1)}, u32[]{:S(2)}, u32[]{:S(2)}) %collective-permute-start.29) | collective-permute-done | bytes 196640 | tf_op jit(solution)/shard_map/ppermute | solution.py:25
  101.4 0.8 collective-permute-start.31
  102.4 1.7 collective-permute-done.25
  104.2 2.7 %collective-permute-start.27 = (bf16[4,12,16,128]{3,2,1,0:T(8,128)(2,1)S(1)}, bf16[4,12,16,128]{3,2,1,0:T(8,128)(2,1)S(1)}, u32[]{:S(2)}, u32[]{:S(2)}) collective-permute-start(bf16[4,12,16,128]{3,2,1,0:T(8,128)(2,1)S(1)} %get-tuple-element.150), channel_id=1, source_target_pairs={{0,96},{32,64},{64,32},{96,0},{1,97},{33,65},{65,33},{97,1},{2,98}... | collective-permute-start | bytes 589832 | tf_op jit(solution)/shard_map/ppermute | solution.py:25
  106.9 1.5 collective-permute-done.31
  108.5 4.7 %collective-permute-done.27 = bf16[4,12,16,128]{3,2,1,0:T(8,128)(2,1)S(1)} collective-permute-done((bf16[4,12,16,128]{3,2,1,0:T(8,128)(2,1)S(1)}, bf16[4,12,16,128]{3,2,1,0:T(8,128)(2,1)S(1)}, u32[]{:S(2)}, u32[]{:S(2)}) %collective-permute-start.27) | collective-permute-done | bytes 196640 | tf_op jit(solution)/shard_map/ppermute | solution.py:25
  113.2 1.4 collective-permute-done.26
  114.7 1.3 collective-permute-start.32
  116.4 1.1 collective-permute-start.35
  117.4 3.7 %copy-done.1 = bf16[8,1,192,3072]{3,2,1,0:T(8,128)(2,1)S(1)} copy-done((bf16[8,1,192,3072]{3,2,1,0:T(8,128)(2,1)S(1)}, bf16[8,1,192,3072]{3,2,1,0:T(8,128)(2,1)}, u32[]{:S(2)}) %copy-start.1) | copy-done | bytes 9437208
  121.8 2.0 %collective-permute-done.32.refs_3_ = bf16[8,12,16,128]{3,2,1,0:T(8,128)(2,1)S(1)} collective-permute-done((bf16[8,12,16,128]{3,2,1,0:T(8,128)(2,1)S(1)}, bf16[8,12,16,128]{3,2,1,0:T(8,128)(2,1)S(1)}, u32[]{:S(2)}, u32[]{:S(2)}) %collective-permute-start.32) | collective-permute-done | bytes 393248 | tf_op jit(solution)/shard_map/ppermute | solution.py:25
  123.8 1.2 collective-permute-done.34.refs_7_
  125.0 2.5 %shard_map.85 = (bf16[1,192,512]{2,1,0:T(8,128)(2,1)S(1)}, bf16[1,192,512]{2,1,0:T(8,128)(2,1)S(1)}, bf16[192,16,512]{2,1,0:T(8,128)(2,1)S(1)}) custom-call(s32[4]{0:T(128)S(1)} %pad_add_fusion.pos_ref.refs_0_, bf16[4,384,3072]{2,1,0:T(8,128)(2,1)S(1)} %shard_map.84.refs_1_, bf16[8,12,16,128]{3,2,1,0:T(8,128)(2,1)S(1)} %pad_maximum_fusion.7.refs_2_, ...), custom_call_target="tpu_custom_call" | custom-call | flops 1073741824 | bytes 1048576 | tf_op jit(solution)/shard_map/pallas_call | solution.py:30
  127.6 3.4 %shard_map.87 = (bf16[2,192,512]{2,1,0:T(8,128)(2,1)S(1)}, bf16[2,192,512]{2,1,0:T(8,128)(2,1)S(1)}) custom-call(s32[4]{0:T(128)S(1)} %pad_add_fusion.pos_ref.refs_0_, bf16[4,384,3072]{2,1,0:T(8,128)(2,1)S(1)} %shard_map.84.refs_1_, bf16[192,16,512]{2,1,0:T(8,128)(2,1)S(1)} %get-tuple-element.136.refs_2_), custom_call_target="tpu_custom_call" | custom-call | flops 2147483648 | bytes 1048576 | tf_op jit(solution)/shard_map/pallas_call | solution.py:30
  131.6 2.1 %collective-permute-start.40 = (bf16[192,512]{1,0:T(8,128)(2,1)S(1)}, bf16[192,512]{1,0:T(8,128)(2,1)S(1)}, u32[]{:S(2)}, u32[]{:S(2)}) collective-permute-start(bf16[192,512]{1,0:T(8,128)(2,1)S(1)} %fusion.3), channel_id=1, source_target_pairs={{0,4},{2,6},{4,0},{6,2},{1,5},{3,7},{5,1},{7,3},{8,12},{10,14},{12... | collective-permute-start | bytes 589832 | tf_op jit(solution)/shard_map/ppermute | solution.py:25
  133.7 2.0 %shard_map.86 = (bf16[1,192,512]{2,1,0:T(8,128)(2,1)S(1)}, bf16[1,192,512]{2,1,0:T(8,128)(2,1)S(1)}) custom-call(s32[4]{0:T(128)S(1)} %pad_add_fusion.pos_ref.refs_0_, bf16[4,384,3072]{2,1,0:T(8,128)(2,1)S(1)} %shard_map.84.refs_1_, bf16[192,16,512]{2,1,0:T(8,128)(2,1)S(1)} %get-tuple-element.136.refs_2_), custom_call_target="tpu_custom_call" | custom-call | flops 1073741824 | bytes 1048576 | tf_op jit(solution)/shard_map/pallas_call | solution.py:30
  135.9 0.9 collective-permute-start.41
  136.8 0.7 collective-permute-start.39
  137.5 2.5 %collective-permute-done.40.refs_1_ = bf16[192,512]{1,0:T(8,128)(2,1)S(1)} collective-permute-done((bf16[192,512]{1,0:T(8,128)(2,1)S(1)}, bf16[192,512]{1,0:T(8,128)(2,1)S(1)}, u32[]{:S(2)}, u32[]{:S(2)}) %collective-permute-start.40) | collective-permute-done | bytes 196640 | tf_op jit(solution)/shard_map/ppermute | solution.py:25
  140.0 4.4 %collective-permute-done.41.refs_2_ = bf16[192,512]{1,0:T(8,128)(2,1)S(1)} collective-permute-done((bf16[192,512]{1,0:T(8,128)(2,1)S(1)}, bf16[192,512]{1,0:T(8,128)(2,1)S(1)}, u32[]{:S(2)}, u32[]{:S(2)}) %collective-permute-start.41) | collective-permute-done | bytes 196640 | tf_op jit(solution)/shard_map/ppermute | solution.py:25
  144.5 0.9 shard_map.88
  145.4 20.1 %all_to_all.15 = bf16[16,192,128]{2,1,0:T(8,128)(2,1)S(1)} all-to-all(bf16[16,192,128]{2,1,0:T(8,128)(2,1)S(1)} %get-tuple-element.141), channel_id=1, replica_groups=mesh['x'=4,'z'=4,'y'=4,'core'=2] {'x','z'}, dimensions={0} | all-to-all | bytes 1572864 | tf_op jit(solution)/shard_map/all_to_all | solution.py:165
  165.5 1.2 shard_map.89
  166.7 11.6 %all_to_all.16.pieces_ref = bf16[16,48,128]{2,1,0:T(8,128)(2,1)S(1)} all-to-all(bf16[16,48,128]{2,1,0:T(8,128)(2,1)S(1)} %shard_map.89), channel_id=1, replica_groups=mesh['x'=4,'z'=4,'y'=4,'core'=2] {'x','z'}, dimensions={0} | all-to-all | bytes 393216 | tf_op jit(solution)/shard_map/all_to_all | solution.py:279
  178.3 0.8 shard_map.90
  (100 shorter events, 8.2 us)
Async XLA Ops:
  1.7 9.7 %collective-permute-start = (bf16[1,2,3,16,512]{4,3,2,0,1:T(8,128)(2,1)S(1)}, bf16[1,2,3,16,512]{4,3,2,0,1:T(8,128)(2,1)S(1)}, u32[]{:S(2)}, u32[]{:S(2)}) collective-permute-start(bf16[1,2,3,16,512]{4,3,2,0,1:T(8,128)(2,1)S(1)} %maximum_bitcast_fusion), channel_id=1, source_target_pairs={{0,8},{8,0},{16,24},{24,16},{1,9},{9,1},{17,25},{25,17},{2,10},{10... | collective-permute-start | bytes 294920 | tf_op jit(solution)/shard_map/ppermute | solution.py:25
  3.8 4.7 %collective-permute-start.6 = (bf16[1,2,3,16,512]{4,3,2,0,1:T(8,128)(2,1)S(1)}, bf16[1,2,3,16,512]{4,3,2,0,1:T(8,128)(2,1)S(1)}, u32[]{:S(2)}, u32[]{:S(2)}) collective-permute-start(bf16[1,2,3,16,512]{4,3,2,0,1:T(8,128)(2,1)S(1)} %maximum_bitcast_fusion.1), channel_id=1, source_target_pairs={{0,32},{32,0},{64,96},{96,64},{1,33},{33,1},{65,97},{97,65},{2,34}... | collective-permute-start | bytes 294920 | tf_op jit(solution)/shard_map/ppermute | solution.py:25
  5.4 1.1 copy-start.3
  6.5 0.7 copy-start.6
  8.5 7.0 %collective-permute-start.7 = (bf16[2,2,3,16,512]{4,3,2,0,1:T(8,128)(2,1)S(1)}, bf16[2,2,3,16,512]{4,3,2,0,1:T(8,128)(2,1)S(1)}, u32[]{:S(2)}, u32[]{:S(2)}) collective-permute-start(bf16[2,2,3,16,512]{4,3,2,0,1:T(8,128)(2,1)S(1)} %pad_maximum_fusion.13), channel_id=1, source_target_pairs={{0,96},{32,64},{64,32},{96,0},{1,97},{33,65},{65,33},{97,1},{2,98}... | collective-permute-start | bytes 589832 | tf_op jit(solution)/shard_map/ppermute | solution.py:25
  11.4 7.0 %collective-permute-start.1 = (bf16[2,2,3,16,512]{4,3,2,0,1:T(8,128)(2,1)S(1)}, bf16[2,2,3,16,512]{4,3,2,0,1:T(8,128)(2,1)S(1)}, u32[]{:S(2)}, u32[]{:S(2)}) collective-permute-start(bf16[2,2,3,16,512]{4,3,2,0,1:T(8,128)(2,1)S(1)} %pad_maximum_fusion.12), channel_id=1, source_target_pairs={{0,24},{8,16},{16,8},{24,0},{1,25},{9,17},{17,9},{25,1},{2,26},{10... | collective-permute-start | bytes 589832 | tf_op jit(solution)/shard_map/ppermute | solution.py:25
  14.0 5.5 %collective-permute-start.12 = (bf16[2,112,384]{2,1,0:T(8,128)(2,1)S(1)}, bf16[2,112,384]{2,1,0:T(8,128)(2,1)S(1)}, u32[]{:S(2)}, u32[]{:S(2)}) collective-permute-start(bf16[2,112,384]{2,1,0:T(8,128)(2,1)S(1)} %pad_maximum_fusion.16), channel_id=1, source_target_pairs={{0,8},{8,0},{16,24},{24,16},{1,9},{9,1},{17,25},{25,17},{2,10},{10... | collective-permute-start | bytes 516104 | tf_op jit(solution)/shard_map/ppermute | solution.py:25
  19.5 5.7 %collective-permute-start.2 = (bf16[4,3,16,512]{3,2,1,0:T(8,128)(2,1)S(1)}, bf16[4,3,16,512]{3,2,1,0:T(8,128)(2,1)S(1)}, u32[]{:S(2)}, u32[]{:S(2)}) collective-permute-start(bf16[4,3,16,512]{3,2,1,0:T(8,128)(2,1)S(1)} %get-tuple-element.155), channel_id=1, source_target_pairs={{0,32},{32,0},{64,96},{96,64},{1,33},{33,1},{65,97},{97,65},{2,34}... | collective-permute-start | bytes 589832 | tf_op jit(solution)/shard_map/ppermute | solution.py:25
  19.7 8.5 %collective-permute-start.4 = (bf16[4,3,16,512]{3,2,1,0:T(8,128)(2,1)S(1)}, bf16[4,3,16,512]{3,2,1,0:T(8,128)(2,1)S(1)}, u32[]{:S(2)}, u32[]{:S(2)}) collective-permute-start(bf16[4,3,16,512]{3,2,1,0:T(8,128)(2,1)S(1)} %get-tuple-element.154), channel_id=1, source_target_pairs={{0,96},{32,64},{64,32},{96,0},{1,97},{33,65},{65,33},{97,1},{2,98}... | collective-permute-start | bytes 589832 | tf_op jit(solution)/shard_map/ppermute | solution.py:25
  21.0 11.2 %collective-permute-start.14 = (bf16[2,112,384]{2,1,0:T(8,128)(2,1)S(1)}, bf16[2,112,384]{2,1,0:T(8,128)(2,1)S(1)}, u32[]{:S(2)}, u32[]{:S(2)}) collective-permute-start(bf16[2,112,384]{2,1,0:T(8,128)(2,1)S(1)} %pad_maximum_fusion.18), channel_id=1, source_target_pairs={{0,24},{8,16},{16,8},{24,0},{1,25},{9,17},{17,9},{25,1},{2,26},{10... | collective-permute-start | bytes 516104 | tf_op jit(solution)/shard_map/ppermute | solution.py:25
  22.6 9.4 %collective-permute-start.10 = (bf16[4,3,16,512]{3,2,1,0:T(8,128)(2,1)S(1)}, bf16[4,3,16,512]{3,2,1,0:T(8,128)(2,1)S(1)}, u32[]{:S(2)}, u32[]{:S(2)}) collective-permute-start(bf16[4,3,16,512]{3,2,1,0:T(8,128)(2,1)S(1)} %get-tuple-element.152), channel_id=1, source_target_pairs={{0,24},{8,16},{16,8},{24,0},{1,25},{9,17},{17,9},{25,1},{2,26},{10... | collective-permute-start | bytes 589832 | tf_op jit(solution)/shard_map/ppermute | solution.py:25
  24.3 6.2 %collective-permute-start.8 = (bf16[4,3,16,512]{3,2,1,0:T(8,128)(2,1)S(1)}, bf16[4,3,16,512]{3,2,1,0:T(8,128)(2,1)S(1)}, u32[]{:S(2)}, u32[]{:S(2)}) collective-permute-start(bf16[4,3,16,512]{3,2,1,0:T(8,128)(2,1)S(1)} %get-tuple-element.153), channel_id=1, source_target_pairs={{0,8},{8,0},{16,24},{24,16},{1,9},{9,1},{17,25},{25,17},{2,10},{10... | collective-permute-start | bytes 589832 | tf_op jit(solution)/shard_map/ppermute | solution.py:25
  25.2 19.4 %collective-permute-start.3 = (bf16[8,3,16,512]{3,2,1,0:T(8,128)(2,1)S(1)}, bf16[8,3,16,512]{3,2,1,0:T(8,128)(2,1)S(1)}, u32[]{:S(2)}, u32[]{:S(2)}) collective-permute-start(bf16[8,3,16,512]{3,2,1,0:T(8,128)(2,1)S(1)} %pad_maximum_fusion.1.refs_2_), channel_id=1, source_target_pairs={{0,96},{32,64},{64,32},{96,0},{1,97},{33,65},{65,33},{97,1},{2,98}... | collective-permute-start | bytes 1179656 | tf_op jit(solution)/shard_map/ppermute | solution.py:25
  28.3 16.3 %collective-permute-start.5 = (bf16[8,3,16,512]{3,2,1,0:T(8,128)(2,1)S(1)}, bf16[8,3,16,512]{3,2,1,0:T(8,128)(2,1)S(1)}, u32[]{:S(2)}, u32[]{:S(2)}) collective-permute-start(bf16[8,3,16,512]{3,2,1,0:T(8,128)(2,1)S(1)} %pad_maximum_fusion.2.refs_4_), channel_id=1, source_target_pairs={{0,32},{32,0},{64,96},{96,64},{1,33},{33,1},{65,97},{97,65},{2,34}... | collective-permute-start | bytes 1179656 | tf_op jit(solution)/shard_map/ppermute | solution.py:25
  30.6 14.0 %collective-permute-start.9 = (bf16[8,3,16,512]{3,2,1,0:T(8,128)(2,1)S(1)}, bf16[8,3,16,512]{3,2,1,0:T(8,128)(2,1)S(1)}, u32[]{:S(2)}, u32[]{:S(2)}) collective-permute-start(bf16[8,3,16,512]{3,2,1,0:T(8,128)(2,1)S(1)} %pad_maximum_fusion.4.refs_6_), channel_id=1, source_target_pairs={{0,24},{8,16},{16,8},{24,0},{1,25},{9,17},{17,9},{25,1},{2,26},{10... | collective-permute-start | bytes 1179656 | tf_op jit(solution)/shard_map/ppermute | solution.py:25
  32.0 12.6 %collective-permute-start.11 = (bf16[8,3,16,512]{3,2,1,0:T(8,128)(2,1)S(1)}, bf16[8,3,16,512]{3,2,1,0:T(8,128)(2,1)S(1)}, u32[]{:S(2)}, u32[]{:S(2)}) collective-permute-start(bf16[8,3,16,512]{3,2,1,0:T(8,128)(2,1)S(1)} %pad_maximum_fusion.5.refs_8_), channel_id=1, source_target_pairs={{0,8},{8,0},{16,24},{24,16},{1,9},{9,1},{17,25},{25,17},{2,10},{10... | collective-permute-start | bytes 1179656 | tf_op jit(solution)/shard_map/ppermute | solution.py:25
  32.2 5.8 %collective-permute-start.13 = (bf16[2,112,384]{2,1,0:T(8,128)(2,1)S(1)}, bf16[2,112,384]{2,1,0:T(8,128)(2,1)S(1)}, u32[]{:S(2)}, u32[]{:S(2)}) collective-permute-start(bf16[2,112,384]{2,1,0:T(8,128)(2,1)S(1)} %pad_maximum_fusion.17), channel_id=1, source_target_pairs={{0,32},{32,0},{64,96},{96,64},{1,33},{33,1},{65,97},{97,65},{2,34}... | collective-permute-start | bytes 516104 | tf_op jit(solution)/shard_map/ppermute | solution.py:25
  32.7 3.7 %copy-start = (bf16[8,1,192,3072]{3,2,1,0:T(8,128)(2,1)S(1)}, bf16[8,1,192,3072]{3,2,1,0:T(8,128)(2,1)}, u32[]{:S(2)}) copy-start(bf16[8,1,192,3072]{3,2,1,0:T(8,128)(2,1)} %param.6) | copy-start | bytes 28311556
  38.0 6.6 %collective-permute-start.15 = (bf16[2,112,384]{2,1,0:T(8,128)(2,1)S(1)}, bf16[2,112,384]{2,1,0:T(8,128)(2,1)S(1)}, u32[]{:S(2)}, u32[]{:S(2)}) collective-permute-start(bf16[2,112,384]{2,1,0:T(8,128)(2,1)S(1)} %collective-permute-done.14), channel_id=1, source_target_pairs={{0,96},{32,64},{64,32},{96,0},{1,97},{33,65},{65,33},{97,1},{2,98}... | collective-permute-start | bytes 516104 | tf_op jit(solution)/shard_map/ppermute | solution.py:25
  44.7 16.0 %collective-permute-start.22 = (bf16[4,112,384]{2,1,0:T(8,128)(2,1)S(1)}, bf16[4,112,384]{2,1,0:T(8,128)(2,1)S(1)}, u32[]{:S(2)}, u32[]{:S(2)}) collective-permute-start(bf16[4,112,384]{2,1,0:T(8,128)(2,1)S(1)} %constant_dynamic-update-slice_fusion.2.refs_6_), channel_id=1, source_target_pairs={{0,32},{32,0},{64,96},{96,64},{1,33},{33,1},{65,97},{97,65},{2,34}... | collective-permute-start | bytes 1032200 | tf_op jit(solution)/shard_map/ppermute | solution.py:25
  46.9 6.2 %collective-permute-start.18 = (bf16[1,192,512]{2,1,0:T(8,128)(2,1)S(1)}, bf16[1,192,512]{2,1,0:T(8,128)(2,1)S(1)}, u32[]{:S(2)}, u32[]{:S(2)}) collective-permute-start(bf16[1,192,512]{2,1,0:T(8,128)(2,1)S(1)} %get-tuple-element.98), channel_id=1, source_target_pairs={{0,1},{1,0},{2,3},{3,2},{4,5},{5,4},{6,7},{7,6},{8,9},{9,8},{10,11... | collective-permute-start | bytes 589832 | tf_op jit(solution)/shard_map/ppermute | solution.py:25
  50.4 16.8 %copy-start.4 = (f32[1,192,512]{2,1,0:T(8,128)S(1)}, f32[1,192,512]{2,1,0:T(8,128)}, u32[]{:S(2)}) copy-start(f32[1,192,512]{2,1,0:T(8,128)} %param.7) | copy-start | bytes 1179652
  50.4 38.0 %copy-start.5 = (s32[192]{0:T(256)S(1)}, s32[192]{0:T(256)}, u32[]{:S(2)}) copy-start(s32[192]{0:T(256)} %refs_2_.3) | copy-start | bytes 2308
  50.5 8.1 %collective-permute-start.16 = (bf16[2,192,512]{2,1,0:T(8,128)(2,1)S(1)}, bf16[2,192,512]{2,1,0:T(8,128)(2,1)S(1)}, u32[]{:S(2)}, u32[]{:S(2)}) collective-permute-start(bf16[2,192,512]{2,1,0:T(8,128)(2,1)S(1)} %get-tuple-element.96), channel_id=1, source_target_pairs={{0,1},{1,0},{2,3},{3,2},{4,5},{5,4},{6,7},{7,6},{8,9},{9,8},{10,11... | collective-permute-start | bytes 1179656 | tf_op jit(solution)/shard_map/ppermute | solution.py:25
  51.1 11.3 %collective-permute-start.21 = (bf16[4,112,384]{2,1,0:T(8,128)(2,1)S(1)}, bf16[4,112,384]{2,1,0:T(8,128)(2,1)S(1)}, u32[]{:S(2)}, u32[]{:S(2)}) collective-permute-start(bf16[4,112,384]{2,1,0:T(8,128)(2,1)S(1)} %constant_dynamic-update-slice_fusion.refs_4_), channel_id=1, source_target_pairs={{0,96},{32,64},{64,32},{96,0},{1,97},{33,65},{65,33},{97,1},{2,98}... | collective-permute-start | bytes 1032200 | tf_op jit(solution)/shard_map/ppermute | solution.py:25
  53.2 9.2 %collective-permute-start.19 = (bf16[192,512]{1,0:T(8,128)(2,1)S(1)}, bf16[192,512]{1,0:T(8,128)(2,1)S(1)}, u32[]{:S(2)}, u32[]{:S(2)}) collective-permute-start(bf16[192,512]{1,0:T(8,128)(2,1)S(1)} %fusion.1), channel_id=1, source_target_pairs={{0,4},{2,6},{4,0},{6,2},{1,5},{3,7},{5,1},{7,3},{8,12},{10,14},{12... | collective-permute-start | bytes 589832 | tf_op jit(solution)/shard_map/ppermute | solution.py:25
  58.4 1.5 collective-permute-start.23
  58.7 8.6 %collective-permute-start.20 = (bf16[192,512]{1,0:T(8,128)(2,1)S(1)}, bf16[192,512]{1,0:T(8,128)(2,1)S(1)}, u32[]{:S(2)}, u32[]{:S(2)}) collective-permute-start(bf16[192,512]{1,0:T(8,128)(2,1)S(1)} %get-tuple-element.146), channel_id=1, source_target_pairs={{0,6},{2,4},{4,2},{6,0},{1,7},{3,5},{5,3},{7,1},{8,14},{10,12},{12... | collective-permute-start | bytes 589832 | tf_op jit(solution)/shard_map/ppermute | solution.py:25
  60.0 7.3 %collective-permute-start.17 = (bf16[192,512]{1,0:T(8,128)(2,1)S(1)}, bf16[192,512]{1,0:T(8,128)(2,1)S(1)}, u32[]{:S(2)}, u32[]{:S(2)}) collective-permute-start(bf16[192,512]{1,0:T(8,128)(2,1)S(1)} %get-tuple-element.147), channel_id=1, source_target_pairs={{0,2},{2,0},{4,6},{6,4},{1,3},{3,1},{5,7},{7,5},{8,10},{10,8},{12,... | collective-permute-start | bytes 589832 | tf_op jit(solution)/shard_map/ppermute | solution.py:25
  68.3 20.1 %all-to-all-start = ((bf16[16,192,128]{2,1,0:T(8,128)(2,1)}), bf16[16,192,128]{2,1,0:T(8,128)(2,1)S(1)}, u32[]{:S(2)}, u32[]{:S(2)}) async-start(bf16[16,192,128]{2,1,0:T(8,128)(2,1)} %get-tuple-element.114), calls=%async_computation | async-start | bytes 1572864 | tf_op jit(solution)/shard_map/all_to_all | solution.py:165
  89.7 4.7 %collective-permute-start.28 = (bf16[1,2,12,16,128]{4,3,2,0,1:T(8,128)(2,1)S(1)}, bf16[1,2,12,16,128]{4,3,2,0,1:T(8,128)(2,1)S(1)}, u32[]{:S(2)}, u32[]{:S(2)}) collective-permute-start(bf16[1,2,12,16,128]{4,3,2,0,1:T(8,128)(2,1)S(1)} %maximum_bitcast_fusion.3), channel_id=1, source_target_pairs={{0,32},{32,0},{64,96},{96,64},{1,33},{33,1},{65,97},{97,65},{2,34}... | collective-permute-start | bytes 294920 | tf_op jit(solution)/shard_map/ppermute | solution.py:25
  89.8 5.8 %collective-permute-start.24 = (bf16[1,2,12,16,128]{4,3,2,0,1:T(8,128)(2,1)S(1)}, bf16[1,2,12,16,128]{4,3,2,0,1:T(8,128)(2,1)S(1)}, u32[]{:S(2)}, u32[]{:S(2)}) collective-permute-start(bf16[1,2,12,16,128]{4,3,2,0,1:T(8,128)(2,1)S(1)} %maximum_bitcast_fusion.2), channel_id=1, source_target_pairs={{0,8},{8,0},{16,24},{24,16},{1,9},{9,1},{17,25},{25,17},{2,10},{10... | collective-permute-start | bytes 294920 | tf_op jit(solution)/shard_map/ppermute | solution.py:25
  94.4 7.0 %collective-permute-start.29 = (bf16[2,2,12,16,128]{4,3,2,0,1:T(8,128)(2,1)S(1)}, bf16[2,2,12,16,128]{4,3,2,0,1:T(8,128)(2,1)S(1)}, u32[]{:S(2)}, u32[]{:S(2)}) collective-permute-start(bf16[2,2,12,16,128]{4,3,2,0,1:T(8,128)(2,1)S(1)} %pad_maximum_fusion.15), channel_id=1, source_target_pairs={{0,96},{32,64},{64,32},{96,0},{1,97},{33,65},{65,33},{97,1},{2,98}... | collective-permute-start | bytes 589832 | tf_op jit(solution)/shard_map/ppermute | solution.py:25
  95.6 8.5 %collective-permute-start.25 = (bf16[2,2,12,16,128]{4,3,2,0,1:T(8,128)(2,1)S(1)}, bf16[2,2,12,16,128]{4,3,2,0,1:T(8,128)(2,1)S(1)}, u32[]{:S(2)}, u32[]{:S(2)}) collective-permute-start(bf16[2,2,12,16,128]{4,3,2,0,1:T(8,128)(2,1)S(1)} %pad_maximum_fusion.14), channel_id=1, source_target_pairs={{0,24},{8,16},{16,8},{24,0},{1,25},{9,17},{17,9},{25,1},{2,26},{10... | collective-permute-start | bytes 589832 | tf_op jit(solution)/shard_map/ppermute | solution.py:25
  101.4 7.0 %collective-permute-start.31 = (bf16[4,12,16,128]{3,2,1,0:T(8,128)(2,1)S(1)}, bf16[4,12,16,128]{3,2,1,0:T(8,128)(2,1)S(1)}, u32[]{:S(2)}, u32[]{:S(2)}) collective-permute-start(bf16[4,12,16,128]{3,2,1,0:T(8,128)(2,1)S(1)} %get-tuple-element.148), channel_id=1, source_target_pairs={{0,24},{8,16},{16,8},{24,0},{1,25},{9,17},{17,9},{25,1},{2,26},{10... | collective-permute-start | bytes 589832 | tf_op jit(solution)/shard_map/ppermute | solution.py:25
  102.3 6.2 %collective-permute-start.30 = (bf16[4,12,16,128]{3,2,1,0:T(8,128)(2,1)S(1)}, bf16[4,12,16,128]{3,2,1,0:T(8,128)(2,1)S(1)}, u32[]{:S(2)}, u32[]{:S(2)}) collective-permute-start(bf16[4,12,16,128]{3,2,1,0:T(8,128)(2,1)S(1)} %get-tuple-element.149), channel_id=1, source_target_pairs={{0,8},{8,0},{16,24},{24,16},{1,9},{9,1},{17,25},{25,17},{2,10},{10... | collective-permute-start | bytes 589832 | tf_op jit(solution)/shard_map/ppermute | solution.py:25
  104.2 9.0 %collective-permute-start.27 = (bf16[4,12,16,128]{3,2,1,0:T(8,128)(2,1)S(1)}, bf16[4,12,16,128]{3,2,1,0:T(8,128)(2,1)S(1)}, u32[]{:S(2)}, u32[]{:S(2)}) collective-permute-start(bf16[4,12,16,128]{3,2,1,0:T(8,128)(2,1)S(1)} %get-tuple-element.150), channel_id=1, source_target_pairs={{0,96},{32,64},{64,32},{96,0},{1,97},{33,65},{65,33},{97,1},{2,98}... | collective-permute-start | bytes 589832 | tf_op jit(solution)/shard_map/ppermute | solution.py:25
  106.9 7.8 %collective-permute-start.26 = (bf16[4,12,16,128]{3,2,1,0:T(8,128)(2,1)S(1)}, bf16[4,12,16,128]{3,2,1,0:T(8,128)(2,1)S(1)}, u32[]{:S(2)}, u32[]{:S(2)}) collective-permute-start(bf16[4,12,16,128]{3,2,1,0:T(8,128)(2,1)S(1)} %get-tuple-element.151), channel_id=1, source_target_pairs={{0,32},{32,0},{64,96},{96,64},{1,33},{33,1},{65,97},{97,65},{2,34}... | collective-permute-start | bytes 589832 | tf_op jit(solution)/shard_map/ppermute | solution.py:25
  114.7 9.1 %collective-permute-start.32 = (bf16[8,12,16,128]{3,2,1,0:T(8,128)(2,1)S(1)}, bf16[8,12,16,128]{3,2,1,0:T(8,128)(2,1)S(1)}, u32[]{:S(2)}, u32[]{:S(2)}) collective-permute-start(bf16[8,12,16,128]{3,2,1,0:T(8,128)(2,1)S(1)} %pad_maximum_fusion.7.refs_2_), channel_id=1, source_target_pairs={{0,96},{32,64},{64,32},{96,0},{1,97},{33,65},{65,33},{97,1},{2,98}... | collective-permute-start | bytes 1179656 | tf_op jit(solution)/shard_map/ppermute | solution.py:25
  116.0 7.8 %collective-permute-start.33 = (bf16[8,12,16,128]{3,2,1,0:T(8,128)(2,1)S(1)}, bf16[8,12,16,128]{3,2,1,0:T(8,128)(2,1)S(1)}, u32[]{:S(2)}, u32[]{:S(2)}) collective-permute-start(bf16[8,12,16,128]{3,2,1,0:T(8,128)(2,1)S(1)} %pad_maximum_fusion.8.refs_4_), channel_id=1, source_target_pairs={{0,32},{32,0},{64,96},{96,64},{1,33},{33,1},{65,97},{97,65},{2,34}... | collective-permute-start | bytes 1179656 | tf_op jit(solution)/shard_map/ppermute | solution.py:25
  116.0 9.0 %collective-permute-start.34 = (bf16[8,12,16,128]{3,2,1,0:T(8,128)(2,1)S(1)}, bf16[8,12,16,128]{3,2,1,0:T(8,128)(2,1)S(1)}, u32[]{:S(2)}, u32[]{:S(2)}) collective-permute-start(bf16[8,12,16,128]{3,2,1,0:T(8,128)(2,1)S(1)} %pad_maximum_fusion.10.refs_6_), channel_id=1, source_target_pairs={{0,24},{8,16},{16,8},{24,0},{1,25},{9,17},{17,9},{25,1},{2,26},{10... | collective-permute-start | bytes 1179656 | tf_op jit(solution)/shard_map/ppermute | solution.py:25
  116.4 8.6 %collective-permute-start.35 = (bf16[8,12,16,128]{3,2,1,0:T(8,128)(2,1)S(1)}, bf16[8,12,16,128]{3,2,1,0:T(8,128)(2,1)S(1)}, u32[]{:S(2)}, u32[]{:S(2)}) collective-permute-start(bf16[8,12,16,128]{3,2,1,0:T(8,128)(2,1)S(1)} %pad_maximum_fusion.11.refs_8_), channel_id=1, source_target_pairs={{0,8},{8,0},{16,24},{24,16},{1,9},{9,1},{17,25},{25,17},{2,10},{10... | collective-permute-start | bytes 1179656 | tf_op jit(solution)/shard_map/ppermute | solution.py:25
  117.4 3.7 %copy-start.1 = (bf16[8,1,192,3072]{3,2,1,0:T(8,128)(2,1)S(1)}, bf16[8,1,192,3072]{3,2,1,0:T(8,128)(2,1)}, u32[]{:S(2)}) copy-start(bf16[8,1,192,3072]{3,2,1,0:T(8,128)(2,1)} %param.6) | copy-start | bytes 28311556
  127.5 4.1 %collective-permute-start.36 = (bf16[1,192,512]{2,1,0:T(8,128)(2,1)S(1)}, bf16[1,192,512]{2,1,0:T(8,128)(2,1)S(1)}, u32[]{:S(2)}, u32[]{:S(2)}) collective-permute-start(bf16[1,192,512]{2,1,0:T(8,128)(2,1)S(1)} %get-tuple-element.134), channel_id=1, source_target_pairs={{0,1},{1,0},{2,3},{3,2},{4,5},{5,4},{6,7},{7,6},{8,9},{9,8},{10,11... | collective-permute-start | bytes 589832 | tf_op jit(solution)/shard_map/ppermute | solution.py:25
  131.0 4.8 %collective-permute-start.38 = (bf16[2,192,512]{2,1,0:T(8,128)(2,1)S(1)}, bf16[2,192,512]{2,1,0:T(8,128)(2,1)S(1)}, u32[]{:S(2)}, u32[]{:S(2)}) collective-permute-start(bf16[2,192,512]{2,1,0:T(8,128)(2,1)S(1)} %get-tuple-element.140), channel_id=1, source_target_pairs={{0,1},{1,0},{2,3},{3,2},{4,5},{5,4},{6,7},{7,6},{8,9},{9,8},{10,11... | collective-permute-start | bytes 1179656 | tf_op jit(solution)/shard_map/ppermute | solution.py:25
  131.6 46.7 %copy-start.2 = (f32[1,192,512]{2,1,0:T(8,128)S(1)}, f32[1,192,512]{2,1,0:T(8,128)}, u32[]{:S(2)}) copy-start(f32[1,192,512]{2,1,0:T(8,128)} %param.8) | copy-start | bytes 1179652
  131.6 8.4 %collective-permute-start.40 = (bf16[192,512]{1,0:T(8,128)(2,1)S(1)}, bf16[192,512]{1,0:T(8,128)(2,1)S(1)}, u32[]{:S(2)}, u32[]{:S(2)}) collective-permute-start(bf16[192,512]{1,0:T(8,128)(2,1)S(1)} %fusion.3), channel_id=1, source_target_pairs={{0,4},{2,6},{4,0},{6,2},{1,5},{3,7},{5,1},{7,3},{8,12},{10,14},{12... | collective-permute-start | bytes 589832 | tf_op jit(solution)/shard_map/ppermute | solution.py:25
  135.7 1.8 collective-permute-start.37
  135.9 8.6 %collective-permute-start.41 = (bf16[192,512]{1,0:T(8,128)(2,1)S(1)}, bf16[192,512]{1,0:T(8,128)(2,1)S(1)}, u32[]{:S(2)}, u32[]{:S(2)}) collective-permute-start(bf16[192,512]{1,0:T(8,128)(2,1)S(1)} %get-tuple-element.144), channel_id=1, source_target_pairs={{0,6},{2,4},{4,2},{6,0},{1,7},{3,5},{5,3},{7,1},{8,14},{10,12},{12... | collective-permute-start | bytes 589832 | tf_op jit(solution)/shard_map/ppermute | solution.py:25
  136.8 7.7 %collective-permute-start.39 = (bf16[192,512]{1,0:T(8,128)(2,1)S(1)}, bf16[192,512]{1,0:T(8,128)(2,1)S(1)}, u32[]{:S(2)}, u32[]{:S(2)}) collective-permute-start(bf16[192,512]{1,0:T(8,128)(2,1)S(1)} %get-tuple-element.145), channel_id=1, source_target_pairs={{0,2},{2,0},{4,6},{6,4},{1,3},{3,1},{5,7},{7,5},{8,10},{10,8},{12,... | collective-permute-start | bytes 589832 | tf_op jit(solution)/shard_map/ppermute | solution.py:25
